TPU v7x, 128 devices: a whole 4x4x4 slice. The times are simulated.
128 devices in a mesh: dp: 32 (over x_hi, y, z), gen: 4 (over x_lo, core).
Axes of the slice: x: 4 (x_hi: 2, x_lo: 2; x = x_hi * 2 + x_lo), y: 4, z: 4, core: 2. Of those that a mesh axis runs over, the one named last changes fastest.
Arguments:
- src_ids: int32 [256, 256], P('dp'), may hold values from 0 to 32127
- tgt_ids: int32 [256, 128], P('dp'), may hold values from 0 to 32127
- task_ids: int32 [256], P('dp'), may hold values from 0 to 7
- task_len: int32 [8], replicated, may hold values from 64 to 256, as said below
- tgt_count: int32 [256], P('dp'), may hold values from 32 to 128, as said below
- table: bfloat16 [32128, 512], P('gen')
- attn_w: bfloat16 [3, 512, 2048], replicated, may hold values from -0.25 to 0.25
- ffn_in: bfloat16 [2, 512, 2048], replicated, may hold values from -0.25 to 0.25
- ffn_out: bfloat16 [2, 2048, 512], replicated, may hold values from -0.125 to 0.125
- gains: float32 [7, 512], replicated, may hold values from 0.5 to 1.5
- embeds: float32 [10, 64], replicated, may hold values from -4 to 4
- embeds_m: float32 [10, 64], replicated, may hold values from -4.7683716e-07 to 4.7683716e-07
- embeds_v: float32 [10, 64], replicated, may hold values from 6.289751e-16 to 2.5159005e-15
- proj_one: float32 [64, 128], replicated, may hold values from -4 to 4
- proj_one_m: float32 [64, 128], replicated, may hold values from -4.7683716e-07 to 4.7683716e-07
- proj_one_v: float32 [64, 128], replicated, may hold values from 6.289751e-16 to 2.5159005e-15
- proj_two: float32 [128, 64], replicated, may hold values from -4 to 4
- proj_two_m: float32 [128, 64], replicated, may hold values from -4.7683716e-07 to 4.7683716e-07
- proj_two_v: float32 [128, 64], replicated, may hold values from 6.289751e-16 to 2.5159005e-15
- hyper: float32 [64, 24576], P(None, 'gen'), may hold values from -1 to 1
- hyper_m: float32 [64, 24576], P(None, 'gen'), may hold values from -4.7683716e-07 to 4.7683716e-07
- hyper_v: float32 [64, 24576], P(None, 'gen'), may hold values from 6.289751e-16 to 2.5159005e-15
Outputs:
- loss_sum: float32 [], replicated
- token_count: float32 [], replicated
- grad_norm: float32 [], replicated
- new_embeds: float32 [10, 64], replicated
- new_embeds_m: float32 [10, 64], replicated
- new_embeds_v: float32 [10, 64], replicated
- new_proj_one: float32 [64, 128], replicated
- new_proj_one_m: float32 [64, 128], replicated
- new_proj_one_v: float32 [64, 128], replicated
- new_proj_two: float32 [128, 64], replicated
- new_proj_two_m: float32 [128, 64], replicated
- new_proj_two_v: float32 [128, 64], replicated
- new_hyper: float32 [64, 24576], P(None, 'gen')
- new_hyper_m: float32 [64, 24576], P(None, 'gen')
- new_hyper_v: float32 [64, 24576], P(None, 'gen')
Inputs may be any that keep to these rules, and one draw needn't show every extreme that they name: `task_len`: one task has exactly 256 input positions and another a quarter of 256. `tgt_count`: the counted positions of a sequence are its first ones; the first sequence counts a quarter of 128, the last all 128.
All inputs are finite; a program needn't handle non-finite values.
Results may differ from a plain program's by a relative error of at most 0.00215.
Values may be sent and summed in bfloat16 or wider, within the bound.
A program may use at most 192 MiB of HBM per device.

v0:
```python
import math

import jax
import jax.numpy as jnp
from jax import lax
from jax.sharding import PartitionSpec as P

D = 512
HEADS = 8
ADAPTER = 24
TASKS = 8
LAYERS = 2
SRC = 256
TGT = 128
MICRO = 2
SEQ_MB = 1
STEP = 5


epsilon = 1e-06
clip_limit = 0.001
beta_one = 0.9
beta_two = 0.999
adam_floor = 1e-08
weight_decay = 0.01
rates = (0.5, 0.1, 0.1, 0.005)
blocked = -1000000000.0
highest = lax.Precision.HIGHEST


def merged(part, axis, combine):
    gathered = jax.tree.map(lambda a: lax.all_gather(a, axis), part)

    def take(source):
        return jax.tree.map(lambda a: lax.dynamic_index_in_dim(a, source, 0, False), gathered)

    return lax.fori_loop(
        1, lax.axis_size(axis), lambda source, state: combine(state, take(source)), take(0)
    )


def normalize(value, gain):
    scale = lax.rsqrt(jnp.mean(value * value, axis=-1, keepdims=True) + epsilon)
    return (value * scale * gain, scale)


def normalize_back(value, scale, gain, grad):
    weighted = grad * gain
    return scale * weighted - value * scale * scale * scale * jnp.mean(
        weighted * value, axis=-1, keepdims=True
    )


def gelu_back(value, grad):
    return jax.vjp(jax.nn.gelu, value)[1](grad)[0]


def split_heads(value):
    return value.reshape(value.shape[:2] + (HEADS, -1))


def project(value, weight):
    return jnp.einsum("btd,de->bte", value, weight, preferred_element_type=jnp.float32)


def project_back(grad, weight):
    return jnp.einsum("bte,de->btd", grad, weight, preferred_element_type=jnp.float32)


def probabilities(query, keys, allowed):
    width = query.shape[-1]
    scores = jnp.einsum(
        "bqhd,bkhd->bhqk", split_heads(query), split_heads(keys), preferred_element_type=jnp.float32
    ) * (width // HEADS) ** (-0.5)
    return jnp.where(allowed[:, None], scores, blocked)


def attention_forward(normed, source, weight, allowed):
    width = normed.shape[-1]
    query = project(normed, weight[:, :width]).astype(jnp.bfloat16)
    paired = project(source, weight[:, width : 3 * width]).astype(jnp.bfloat16)
    keys = paired[..., :width]
    values = paired[..., width:]
    scores = probabilities(query, keys, allowed)
    logsum = jax.nn.logsumexp(scores, axis=-1, keepdims=True)
    probs = jnp.exp(scores - logsum).astype(jnp.bfloat16)
    mixed = jnp.einsum(
        "bhqk,bkhd->bqhd", probs, split_heads(values), preferred_element_type=jnp.float32
    )
    mixed = mixed.reshape(normed.shape).astype(jnp.bfloat16)
    return (project(mixed, weight[:, 3 * width :]), (query, keys, values, logsum))


def attention_source_back(grad, source, weight, allowed, cache):
    query, keys, values, logsum = cache
    width = source.shape[-1]
    grad_mixed = project_back(grad.astype(jnp.bfloat16), weight[:, 3 * width :]).astype(
        jnp.bfloat16
    )
    probs = jnp.exp(probabilities(query, keys, allowed) - logsum)
    grad_probs = jnp.einsum(
        "bqhd,bkhd->bhqk",
        split_heads(grad_mixed),
        split_heads(values),
        preferred_element_type=jnp.float32,
    )
    grad_values = jnp.einsum(
        "bhqk,bqhd->bkhd",
        probs.astype(jnp.bfloat16),
        split_heads(grad_mixed),
        preferred_element_type=jnp.float32,
    )
    grad_scores = (
        probs * (grad_probs - jnp.sum(grad_probs * probs, axis=-1, keepdims=True))
    ).astype(jnp.bfloat16)
    grad_keys = jnp.einsum(
        "bhqk,bqhd->bkhd", grad_scores, split_heads(query), preferred_element_type=jnp.float32
    ) * (width // HEADS) ** (-0.5)
    joined = jnp.concatenate(
        [grad_keys.reshape(source.shape), grad_values.reshape(source.shape)], axis=-1
    ).astype(jnp.bfloat16)
    return project_back(joined, weight[:, width : 3 * width])


def feed_forward(state, gain, inner, outer, down, up):
    normed, scale = normalize(state, gain)
    hidden = jnp.einsum(
        "btd,df->btf", normed.astype(jnp.bfloat16), inner, preferred_element_type=jnp.float32
    )
    branch = jnp.einsum(
        "btf,fd->btd",
        jax.nn.gelu(hidden).astype(jnp.bfloat16),
        outer,
        preferred_element_type=jnp.float32,
    )
    plain = branch.astype(jnp.bfloat16)
    lowered = jnp.einsum("btd,bda->bta", plain, down, preferred_element_type=jnp.float32)
    bottleneck = jax.nn.gelu(lowered).astype(jnp.bfloat16)
    adapted = jnp.einsum(
        "bta,bad->btd", bottleneck, up, preferred_element_type=jnp.float32
    ) * math.sqrt(D / ADAPTER)
    return (state + branch + adapted, (scale, hidden, plain, lowered, bottleneck))


def feed_forward_back(grad, state, gain, inner, outer, down, up, cache):
    scale, hidden, plain, lowered, bottleneck = cache
    upscale = math.sqrt(D / ADAPTER)
    grad_low = grad.astype(jnp.bfloat16)
    grad_bottle = (
        jnp.einsum("btd,bad->bta", grad_low, up, preferred_element_type=jnp.float32) * upscale
    )
    grad_up = (
        jnp.einsum("bta,btd->bad", bottleneck, grad_low, preferred_element_type=jnp.float32)
        * upscale
    )
    grad_lowered = gelu_back(lowered, grad_bottle).astype(jnp.bfloat16)
    grad_down = jnp.einsum("btd,bta->bda", plain, grad_lowered, preferred_element_type=jnp.float32)
    grad_branch = (
        grad + jnp.einsum("bta,bda->btd", grad_lowered, down, preferred_element_type=jnp.float32)
    ).astype(jnp.bfloat16)
    grad_active = jnp.einsum("btd,fd->btf", grad_branch, outer, preferred_element_type=jnp.float32)
    grad_hidden = gelu_back(hidden, grad_active).astype(jnp.bfloat16)
    grad_normed = jnp.einsum("btf,df->btd", grad_hidden, inner, preferred_element_type=jnp.float32)
    return (grad + normalize_back(state, scale, gain, grad_normed), grad_down, grad_up)


def encoder_forward(embedded, gains, attn_w, ffn_in, ffn_out, down, up, allowed):
    normed = normalize(embedded, gains[0])[0].astype(jnp.bfloat16)
    attended, _ = attention_forward(normed, normed, attn_w[0], allowed)
    state = embedded + attended
    after, cache = feed_forward(state, gains[1], ffn_in[0], ffn_out[0], down, up)
    memory, scale = normalize(after, gains[2])
    return (memory.astype(jnp.bfloat16), (state, cache, after, scale))


def encoder_back(grad_memory, gains, ffn_in, ffn_out, down, up, saved):
    state, cache, after, scale = saved
    grad_after = normalize_back(after, scale, gains[2], grad_memory)
    _, grad_down, grad_up = feed_forward_back(
        grad_after, state, gains[1], ffn_in[0], ffn_out[0], down, up, cache
    )
    return (grad_down, grad_up)


def decoder_forward(embedded, memory, gains, attn_w, ffn_in, ffn_out, down, up, causal, allowed):
    normed = normalize(embedded, gains[3])[0].astype(jnp.bfloat16)
    attended, _ = attention_forward(normed, normed, attn_w[1], causal)
    state = embedded + attended
    crossing = normalize(state, gains[4])[0].astype(jnp.bfloat16)
    crossed, cross_cache = attention_forward(crossing, memory, attn_w[2], allowed)
    state = state + crossed
    after, cache = feed_forward(state, gains[5], ffn_in[1], ffn_out[1], down, up)
    final, scale = normalize(after, gains[6])
    return (final.astype(jnp.bfloat16), (state, cache, cross_cache, after, scale))


def decoder_back(grad_final, memory, gains, attn_w, ffn_in, ffn_out, down, up, allowed, saved):
    state, cache, cross_cache, after, scale = saved
    grad_after = normalize_back(after, scale, gains[6], grad_final)
    grad_state, grad_down, grad_up = feed_forward_back(
        grad_after, state, gains[5], ffn_in[1], ffn_out[1], down, up, cache
    )
    grad_memory = attention_source_back(grad_state, memory, attn_w[2], allowed, cross_cache)
    return (grad_memory, grad_down, grad_up)


def combine_stats(first, second):
    peak = jnp.maximum(first[0], second[0])
    total = first[1] * jnp.exp(first[0] - peak) + second[1] * jnp.exp(second[0] - peak)
    return (peak, total, first[2] + second[2])


def adamw(weight, first, second, grad, rate):
    first = beta_one * first + (1.0 - beta_one) * grad
    second = beta_two * second + (1.0 - beta_two) * grad * grad
    corrected = first / (1.0 - beta_one**STEP)
    spread = jnp.sqrt(second / (1.0 - beta_two**STEP)) + adam_floor
    return (weight - rate * (corrected / spread + weight_decay * weight), first, second)


def encode(embed_rows, first, second):
    pairs = (embed_rows[:TASKS, None, :] + embed_rows[None, TASKS:, :]).reshape(TASKS * LAYERS, -1)
    return jnp.dot(jax.nn.gelu(jnp.dot(pairs, first, precision=highest)), second, precision=highest)


def per_device(
    src_ids,
    tgt_ids,
    task_ids,
    task_len,
    tgt_count,
    table,
    attn_w,
    ffn_in,
    ffn_out,
    gains,
    embeds,
    embeds_m,
    embeds_v,
    proj_one,
    proj_one_m,
    proj_one_v,
    proj_two,
    proj_two_m,
    proj_two_v,
    hyper,
    hyper_m,
    hyper_v,
):
    groups = lax.axis_size("gen")
    member = lax.axis_index("gen")
    vocab_part = table.shape[0]
    offset = member * vocab_part
    area = D * ADAPTER
    coded, pullback = jax.vjp(encode, embeds, proj_one, proj_two)
    generated = jnp.dot(coded, hyper, precision=highest)
    slots = jnp.zeros_like(generated)
    loss_local = jnp.zeros((), jnp.float32)
    count_local = jnp.zeros((), jnp.float32)
    shape_group = (groups, MICRO, SEQ_MB)
    causal = (jnp.arange(TGT)[:, None] >= jnp.arange(TGT)[None, :])[None]
    for micro in range(MICRO):
        src_group = src_ids.reshape(shape_group + (SRC,))[:, micro]
        tgt_group = tgt_ids.reshape(shape_group + (TGT,))[:, micro]
        task_group = task_ids.reshape(shape_group)[:, micro].reshape(-1)
        count_group = tgt_count.reshape(shape_group)[:, micro].reshape(-1)
        inputs_group = jnp.concatenate(
            [src_group, jnp.zeros_like(tgt_group[..., :1]), tgt_group[..., :-1]], axis=-1
        ).reshape(-1)
        token = inputs_group - offset
        inside = (token >= 0) & (token < vocab_part)
        rows = jnp.take(table, jnp.clip(token, 0, vocab_part - 1), axis=0).astype(jnp.float32)
        embedded = (
            lax.psum_scatter(
                (rows * inside[:, None].astype(jnp.float32)).astype(jnp.bfloat16),
                "gen",
                scatter_dimension=0,
                tiled=True,
            )
            .astype(jnp.float32)
            .reshape(SEQ_MB, SRC + TGT, -1)
        )
        row_index = (task_group[:, None] * LAYERS + jnp.arange(LAYERS)[None]).reshape(-1)
        select = (row_index[:, None] == jnp.arange(TASKS * LAYERS)[None]).astype(jnp.float32)
        piece = jnp.dot(select, generated, precision=highest).astype(jnp.bfloat16)
        adapters = lax.all_to_all(piece, "gen", split_axis=0, concat_axis=1, tiled=True).reshape(
            SEQ_MB, LAYERS, -1
        )
        downs = [adapters[:, layer, :area].reshape(SEQ_MB, D, ADAPTER) for layer in range(LAYERS)]
        ups = [adapters[:, layer, area:].reshape(SEQ_MB, ADAPTER, D) for layer in range(LAYERS)]
        lengths = jnp.sum(
            jnp.where(task_group[:, None] == jnp.arange(TASKS)[None], task_len[None], 0), axis=1
        )
        own_len = lax.dynamic_slice_in_dim(lengths, member * SEQ_MB, SEQ_MB)
        allowed = jnp.arange(SRC)[None, None, :] < own_len[:, None, None]
        memory, enc_saved = encoder_forward(
            embedded[:, :SRC], gains, attn_w, ffn_in, ffn_out, downs[0], ups[0], allowed
        )
        final, dec_saved = decoder_forward(
            embedded[:, SRC:],
            memory,
            gains,
            attn_w,
            ffn_in,
            ffn_out,
            downs[1],
            ups[1],
            causal,
            allowed,
        )
        gathered = lax.all_gather(final.reshape(SEQ_MB * TGT, -1), "gen", axis=0, tiled=True)
        logits = lax.dot_general(
            gathered, table, (((1,), (1,)), ((), ())), preferred_element_type=jnp.float32
        ) * D ** (-0.5)
        targets = tgt_group.reshape(-1) - offset
        hit = (jnp.arange(vocab_part)[None] == targets[:, None]).astype(jnp.float32)
        peak = jnp.max(logits, axis=-1)
        total = jnp.sum(jnp.exp(logits - peak[:, None]), axis=-1)
        picked = jnp.sum(logits * hit, axis=-1)
        peak, total, picked = merged((peak, total, picked), "gen", combine_stats)
        logsum = peak + jnp.log(total)
        valid = (jnp.arange(TGT)[None] < count_group[:, None]).reshape(-1).astype(jnp.float32)
        losses = (logsum - picked) * valid
        loss_local = loss_local + jnp.sum(
            lax.dynamic_slice_in_dim(losses, member * SEQ_MB * TGT, SEQ_MB * TGT)
        )
        count_local = count_local + jnp.sum(
            lax.dynamic_slice_in_dim(count_group, member * SEQ_MB, SEQ_MB)
        ).astype(jnp.float32)
        grad_logits = ((jnp.exp(logits - logsum[:, None]) - hit) * valid[:, None]).astype(
            jnp.bfloat16
        )
        grad_final = lax.psum_scatter(
            jnp.dot(grad_logits, table, preferred_element_type=jnp.float32) * D ** (-0.5),
            "gen",
            scatter_dimension=0,
            tiled=True,
        ).reshape(SEQ_MB, TGT, -1)
        grad_memory, dec_down, dec_up = decoder_back(
            grad_final, memory, gains, attn_w, ffn_in, ffn_out, downs[1], ups[1], allowed, dec_saved
        )
        enc_down, enc_up = encoder_back(
            grad_memory, gains, ffn_in, ffn_out, downs[0], ups[0], enc_saved
        )
        grad_rows = jnp.stack(
            [
                jnp.concatenate(
                    [enc_down.reshape(SEQ_MB, -1), enc_up.reshape(SEQ_MB, -1)], axis=-1
                ),
                jnp.concatenate(
                    [dec_down.reshape(SEQ_MB, -1), dec_up.reshape(SEQ_MB, -1)], axis=-1
                ),
            ],
            axis=1,
        ).reshape(SEQ_MB * LAYERS, -1)
        returned = lax.all_to_all(grad_rows, "gen", split_axis=1, concat_axis=0, tiled=True)
        slots = slots + jnp.dot(select.T, returned, precision=highest)
    hyper_local = jnp.dot(coded.T, slots, precision=highest)
    coded_local = jnp.dot(slots, hyper.T, precision=highest)
    hyper_grad, coded_part, loss_dp, count_dp = lax.psum(
        (hyper_local, coded_local, loss_local, count_local), "dp"
    )
    coded_grad, hyper_square, loss_sum, token_count = lax.psum(
        (coded_part, jnp.sum(hyper_grad * hyper_grad), loss_dp, count_dp), "gen"
    )
    grad_embeds, grad_one, grad_two = pullback(coded_grad)
    count_scale = 1.0 / token_count
    grads = [grad * count_scale for grad in (grad_embeds, grad_one, grad_two, hyper_grad)]
    square = (
        hyper_square * count_scale * count_scale
        + jnp.sum(grads[0] * grads[0])
        + jnp.sum(grads[1] * grads[1])
        + jnp.sum(grads[2] * grads[2])
    )
    grad_norm = jnp.sqrt(square)
    factor = jnp.minimum(1.0, clip_limit / (grad_norm + 1e-06))
    weights = (embeds, proj_one, proj_two, hyper)
    firsts = (embeds_m, proj_one_m, proj_two_m, hyper_m)
    seconds = (embeds_v, proj_one_v, proj_two_v, hyper_v)
    updated = [
        adamw(weights[index], firsts[index], seconds[index], grads[index] * factor, rates[index])
        for index in range(4)
    ]
    return (
        loss_sum,
        token_count,
        grad_norm,
        updated[0][0],
        updated[0][1],
        updated[0][2],
        updated[1][0],
        updated[1][1],
        updated[1][2],
        updated[2][0],
        updated[2][1],
        updated[2][2],
        updated[3][0],
        updated[3][1],
        updated[3][2],
    )


def solution(mesh):
    return jax.shard_map(
        per_device,
        mesh=mesh,
        in_specs=(
            P("dp", None),
            P("dp", None),
            P("dp"),
            P(),
            P("dp"),
            P("gen", None),
            P(),
            P(),
            P(),
            P(),
            P(),
            P(),
            P(),
            P(),
            P(),
            P(),
            P(),
            P(),
            P(),
            P(None, "gen"),
            P(None, "gen"),
            P(None, "gen"),
        ),
        out_specs=(
            P(),
            P(),
            P(),
            P(),
            P(),
            P(),
            P(),
            P(),
            P(),
            P(),
            P(),
            P(),
            P(None, "gen"),
            P(None, "gen"),
            P(None, "gen"),
        ),
        check_vma=False,
    )
```

profile of v0, /device:TPU:1, one launch (start us, length us, event | category | flops | bytes accessed | tf_op | source)
XLA Modules:
  0.0 725.1 jit_solution(6497273010077203728)
XLA Ops:
  9.5 9.3 %gather_fusion = bf16[1536,512]{1,0:T(8,128)(2,1)S(1)} fusion(bf16[8032,512]{1,0:T(8,128)(2,1)} %param.33, s32[2048]{0:T(1024)S(1)} %pad_clamp_fusion.1), kind=kCustom, calls=%fused_computation.clone | custom fusion | bytes 3151872 | tf_op jit(solution)/shard_map/jit(_take)/gather | solution.py:272
  24.6 4.7 all-to-all-start
  29.4 9.3 %gather_fusion.1 = bf16[1536,512]{1,0:T(8,128)(2,1)S(1)} fusion(bf16[8032,512]{1,0:T(8,128)(2,1)} %param.33, s32[2048]{0:T(1024)S(1)} %pad_clamp_fusion), kind=kCustom, calls=%fused_computation.1.clone | custom fusion | bytes 3151872 | tf_op jit(solution)/shard_map/jit(_take)/gather | solution.py:272
  47.9 5.8 slice_bitcast_fusion.1
  149.7 7.3 %all-gather = bf16[1,512,512]{2,1,0:T(8,128)(2,1)S(1)} all-gather(bf16[1,128,512]{2,1,0:T(8,128)(2,1)S(1)} %get-tuple-element.494), channel_id=2, replica_groups=mesh['dp'=32,'gen'=4] {'gen'}, dimensions={1}, use_global_device_ids=true | all-gather | bytes 655360 | tf_op jit(solution)/shard_map/all_gather | solution.py:311
  157.0 6.9 multiply_reduce_fusion.1
  163.9 4.9 select_reduce_fusion.1
  172.2 5.2 all-gather.9
  178.0 5.1 all-gather.10
  183.8 5.1 all-gather.8
  189.5 7.5 %all-gather.4 = bf16[1,512,512]{2,1,0:T(8,128)(2,1)S(1)} all-gather(bf16[1,128,512]{2,1,0:T(8,128)(2,1)S(1)} %copy-done.53), channel_id=6, replica_groups=mesh['dp'=32,'gen'=4] {'gen'}, dimensions={1}, use_global_device_ids=true | all-gather | bytes 655360 | tf_op jit(solution)/shard_map/all_gather | solution.py:311
  197.0 5.1 multiply_reduce_fusion
  202.1 5.8 select_reduce_fusion
  207.9 5.1 all-gather.12
  213.0 5.1 all-gather.13
  218.2 5.1 all-gather.11
  228.5 14.1 %fusion.52 = f32[512,512]{1,0:T(8,128)} fusion(bf16[8032,512]{1,0:T(8,128)(2,1)} %param.33, f32[512,8032]{0,1:T(8,128)} %copy-done.1, f32[512]{0:T(512)S(1)} %copy-done.131, f32[512]{0:T(512)S(1)} %get-tuple-element.456, s32[512]{0:T(512)S(1)} %bitcast.615), kind=kOutput, calls=%fused_computation.93 | convolution fusion | flops 4240130048 | bytes 25729024 | tf_op jit(solution)/shard_map/dot_general | solution.py:334
  243.9 14.2 %fusion.51 = f32[512,512]{1,0:T(8,128)} fusion(bf16[8032,512]{1,0:T(8,128)(2,1)} %param.33, f32[512,8032]{0,1:T(8,128)} %copy-done, f32[512]{0:T(512)S(1)} %copy-done.130, f32[512]{0:T(512)S(1)} %get-tuple-element.452, s32[512]{0:T(512)S(1)} %bitcast.613), kind=kOutput, calls=%fused_computation.92 | convolution fusion | flops 4240130048 | bytes 25729024 | tf_op jit(solution)/shard_map/dot_general | solution.py:334
  258.1 6.7 reduce-scatter.9.cloned.1.call-done
  264.8 24.3 %reduce-scatter.11.cloned.1.call-done = f32[128,512]{1,0:T(8,128)} async-done(((f32[512,512]{1,0:T(8,128)}), f32[128,512]{1,0:T(8,128)}) %reduce-scatter.11.cloned.1.call-update) | async-done | bytes 262160 | tf_op jit(solution)/shard_map/reduce_scatter | solution.py:333
  346.5 86.4 %all-reduce.2 = (f32[]{:T(128)}, f32[]{:T(128)}, f32[16,64]{1,0:T(8,128)S(1)}) all-reduce(f32[]{:T(128)S(6)} %add.679, f32[]{:T(128)} %bitcast.127, f32[16,64]{1,0:T(8,128)S(1)} %fusion.449), channel_id=1, replica_groups=mesh['dp'=32,'gen'=4] {'dp'}, use_global_device_ids=true, to_apply=%region_42.44 | all-reduce | flops 1026 | bytes 8208 | tf_op jit(solution)/shard_map/psum | solution.py:360
  432.8 240.3 %all-reduce.6.cloned.1.call-done = f32[64,6144]{1,0:T(8,128)} async-done(((f32[64,6144]{1,0:T(8,128)}), f32[64,6144]{1,0:T(8,128)}) %all-reduce.6.cloned.1.call-update) | async-done | bytes 1572880 | tf_op jit(solution)/shard_map/psum | solution.py:360
  675.7 28.4 %all-reduce.3 = (f32[]{:T(128)}, f32[]{:T(128)}, f32[]{:T(128)}, f32[16,64]{1,0:T(8,128)S(1)}) all-reduce(f32[]{:T(128)} %get-tuple-element.428, f32[]{:T(128)} %get-tuple-element.429, f32[]{:T(128)} %multiply_reduce_fusion.2, f32[16,64]{1,0:T(8,128)S(1)} %get-tuple-element.430), channel_id=1, replica_groups=mesh['dp'=32,'gen'=4] {'gen'}, use_global_device_ids=true, to_apply=%region_43.45 | all-reduce | flops 1027 | bytes 8216 | tf_op jit(solution)/shard_map/psum | solution.py:363
  712.1 4.9 multiply_subtract_fusion
  (579 shorter events, 189.2 us)
Async XLA Ops:
  7.2 57.9 %reduce-scatter.5.cloned.1.call-start = ((), (), s32[]{:S(2)}) async-start(), calls=%async_computation.8 | async-start | bytes 1966080 | tf_op jit(solution)/shard_map/reduce_scatter | solution.py:274
  24.6 30.3 %all-to-all-start = ((bf16[4,2,6144]{2,1,0:T(2,128)(2,1)}), bf16[4,2,6144]{2,1,0:T(2,128)(2,1)S(1)}, u32[]{:S(2)}, u32[]{:S(2)}) async-start(bf16[4,2,6144]{2,1,0:T(2,128)(2,1)} %all_to_all.48), calls=%async_computation.1 | async-start | bytes 196608 | tf_op jit(solution)/shard_map/all_to_all | solution.py:286
  29.3 47.0 %reduce-scatter.7.cloned.1.call-start = ((), (), s32[]{:S(2)}) async-start(), calls=%async_computation.9 | async-start | bytes 1966080 | tf_op jit(solution)/shard_map/reduce_scatter | solution.py:274
  40.7 45.9 %copy-start.71 = (pred[128,128]{0,1:T(8,128)(4,1)}, pred[128,128]{0,1:T(8,128)(4,1)S(1)}, u32[]{:S(2)}) copy-start(pred[128,128]{0,1:T(8,128)(4,1)S(1)} %iota_compare_fusion.2) | copy-start | bytes 49156
  53.6 57.6 %copy-start.2 = (bf16[512,2048]{1,0:T(8,128)(2,1)}, bf16[512,2048]{1,0:T(8,128)(2,1)S(1)}, u32[]{:S(2)}) copy-start(bf16[512,2048]{1,0:T(8,128)(2,1)S(1)} %get-tuple-element.465) | copy-start | bytes 6291460
  54.9 6.7 all-to-all-start.1
  58.2 206.5 %reduce-scatter.9.cloned.1.call-start = ((), (), s32[]{:S(2)}) async-start(), calls=%async_computation.10 | async-start | bytes 1310720 | tf_op jit(solution)/shard_map/reduce_scatter | solution.py:333
  60.7 58.2 %copy-start.42 = (bf16[512,24]{1,0:T(8,128)(2,1)}, bf16[512,24]{1,0:T(8,128)(2,1)S(1)}, u32[]{:S(2)}) copy-start(bf16[512,24]{1,0:T(8,128)(2,1)S(1)} %reshape.1557) | copy-start | bytes 73732
  242.6 46.5 %reduce-scatter.11.cloned.1.call-start = ((), (), s32[]{:S(2)}) async-start(), calls=%async_computation.11 | async-start | bytes 1310720 | tf_op jit(solution)/shard_map/reduce_scatter | solution.py:333
  243.8 45.3 %copy-start.26 = (f32[1,128,512]{2,1,0:T(8,128)S(1)}, f32[1,128,512]{2,1,0:T(8,128)}, u32[]{:S(2)}) copy-start(f32[1,128,512]{2,1,0:T(8,128)} %copy-done.25) | copy-start | bytes 786436
  318.1 8.0 %all-to-all-start.3 = ((f32[2,4,6144]{2,0,1:T(2,128)}), f32[2,4,6144]{2,0,1:T(2,128)S(1)}, u32[]{:S(2)}, u32[]{:S(2)}) async-start(f32[2,4,6144]{2,0,1:T(2,128)} %copy.168), calls=%async_computation.7 | async-start | bytes 393216 | tf_op jit(solution)/shard_map/all_to_all | solution.py:356
  326.1 8.7 %all-to-all-start.2 = ((f32[2,4,6144]{2,0,1:T(2,128)}), f32[2,4,6144]{2,0,1:T(2,128)S(1)}, u32[]{:S(2)}, u32[]{:S(2)}) async-start(f32[2,4,6144]{2,0,1:T(2,128)} %copy.164), calls=%async_computation.5 | async-start | bytes 393216 | tf_op jit(solution)/shard_map/all_to_all | solution.py:356
  330.3 342.8 %all-reduce.6.cloned.1.call-start = ((), (), s32[]{:S(2)}) async-start(), calls=%async_computation.12 | async-start | bytes 3145728 | tf_op jit(solution)/shard_map/psum | solution.py:360
  338.4 365.7 %copy-start.60 = (f32[128,64]{0,1:T(8,128)S(1)}, f32[128,64]{0,1:T(8,128)}, u32[]{:S(2)}) copy-start(f32[128,64]{0,1:T(8,128)} %param.44) | copy-start | bytes 98308
  338.4 366.5 %copy-start.82 = (f32[16,128]{1,0:T(8,128)S(1)}, f32[16,128]{1,0:T(8,128)}, u32[]{:S(2)}) copy-start(f32[16,128]{1,0:T(8,128)} %copy-done.81) | copy-start | bytes 24580
  338.4 367.4 %copy-start.92 = (f32[8,2,64]{2,1,0:T(2,128)S(1)}, f32[8,2,64]{2,1,0:T(2,128)}, u32[]{:S(2)}) copy-start(f32[8,2,64]{2,1,0:T(2,128)} %copy-done.91) | copy-start | bytes 12292
  338.5 368.2 %copy-start.58 = (f32[64,128]{1,0:T(8,128)S(1)}, f32[64,128]{1,0:T(8,128)}, u32[]{:S(2)}) copy-start(f32[64,128]{1,0:T(8,128)} %param.41) | copy-start | bytes 98308
  338.5 371.7 %copy-start.93 = (f32[10,64]{1,0:T(8,128)S(1)}, f32[10,64]{1,0:T(8,128)}, u32[]{:S(2)}) copy-start(f32[10,64]{1,0:T(8,128)} %param.38) | copy-start | bytes 7684
  338.5 371.7 %copy-start.110 = (f32[10,64]{1,0:T(8,128)S(1)}, f32[10,64]{1,0:T(8,128)}, u32[]{:S(2)}) copy-start(f32[10,64]{1,0:T(8,128)} %param.39) | copy-start | bytes 7684
  338.5 371.7 %copy-start.111 = (f32[10,64]{1,0:T(8,128)S(1)}, f32[10,64]{1,0:T(8,128)}, u32[]{:S(2)}) copy-start(f32[10,64]{1,0:T(8,128)} %param.40) | copy-start | bytes 7684
  338.5 372.3 %copy-start.87 = (f32[128,64]{0,1:T(8,128)S(1)}, f32[128,64]{0,1:T(8,128)}, u32[]{:S(2)}) copy-start(f32[128,64]{0,1:T(8,128)} %param.45) | copy-start | bytes 98308
  338.5 372.3 %copy-start.88 = (f32[128,64]{0,1:T(8,128)S(1)}, f32[128,64]{0,1:T(8,128)}, u32[]{:S(2)}) copy-start(f32[128,64]{0,1:T(8,128)} %param.46) | copy-start | bytes 98308
  338.5 372.9 %copy-start.89 = (f32[64,128]{1,0:T(8,128)S(1)}, f32[64,128]{1,0:T(8,128)}, u32[]{:S(2)}) copy-start(f32[64,128]{1,0:T(8,128)} %param.42) | copy-start | bytes 98308
  338.5 372.9 %copy-start.90 = (f32[64,128]{1,0:T(8,128)S(1)}, f32[64,128]{1,0:T(8,128)}, u32[]{:S(2)}) copy-start(f32[64,128]{1,0:T(8,128)} %param.43) | copy-start | bytes 98308
  (131 other events, 1022.4 us)
Sparse Core Ops, SparseCore 0:
  21.0 27.3 reduce-scatter.4
  51.4 24.8 reduce-scatter.6
  242.8 21.9 reduce-scatter.8
  267.8 21.2 reduce-scatter.10
  338.5 334.5 all-reduce.5
where the time goes:
time: 734 us; the launch traced here: 725 us
  waiting for transfers between devices  283 us (39%)
  blocking collectives  160 us (22%)
  matrix products  124 us (17%)
  local copies, waits for them, and re-layouts  72.7 us (10%)
  other arithmetic  44 us (6%)
  between operations  23.8 us (3%)
  starting transfers between devices  16.1 us (2%)
    psum x1, waiting for transfers between devices, per_device(): lax.psum((hyper_local, coded_local, loss_local, count_local), 'dp')  240 us
    psum x1, blocking collectives, per_device(): lax.psum((hyper_local, coded_local, loss_local, count_local), 'dp')  86.4 us
    reduce_scatter x2, waiting for transfers between devices, per_device(): lax.psum_scatter(jnp.dot(grad_logits, table, preferred_element_type=jnp.f...  31 us
    all_gather x6, blocking collectives, merged(): gathered = jax.tree.map(lambda a: lax.all_gather(a, axis), part)  30.9 us
    psum x1, blocking collectives, per_device(): lax.psum((coded_part, jnp.sum(hyper_grad * hyper_grad), loss_dp, count_dp...  28.4 us
    dot_general x2, matrix products, per_device(): jnp.dot(grad_logits, table, preferred_element_type=jnp.float32)  28.3 us
    dot_general x18, matrix products, project(): jnp.einsum('btd,de->bte', value, weight, preferred_element_type=jnp.float32)  25.8 us
    gather x2, local copies, waits for them, and re-layouts, per_device(): jnp.take(table, jnp.clip(token, 0, vocab_part - 1), axis=0)  18.5 us
  transfers between devices with their start and end apart: 9, of which 7 were waited for; matrix products, arithmetic and copies ran while one was open for 8% of the time, Pallas kernels for 0%

commit v1 on v0

v1 whole, which is shorter than its diff:
```python
import math

import jax
import jax.numpy as jnp
from jax import lax
from jax.experimental import pallas as pl
from jax.experimental.pallas import tpu as pltpu
from jax.sharding import PartitionSpec as P

D = 512
HEADS = 8
ADAPTER = 24
TASKS = 8
LAYERS = 2
SRC = 256
TGT = 128
FF = 2048
SEQ_DEV = 2
GEN = 4
LOW = 128
ROWS = 392
STEP = 5


epsilon = 1e-06
clip_limit = 0.001
beta_one = 0.9
beta_two = 0.999
adam_floor = 1e-08
weight_decay = 0.01
rates = (0.5, 0.1, 0.1, 0.005)
blocked = -1000000000.0
highest = lax.Precision.HIGHEST
LOGIT_SCALE = D ** (-0.5)
EXP_SCALE = LOGIT_SCALE / math.log(2.0)
UPSCALE = math.sqrt(D / ADAPTER)
GELU_A = math.sqrt(2.0 / math.pi)
GELU_B = 0.044715
VOCAB_TILE = 2048
MESH = pl.DeviceIdType.MESH


def adamw(weight, first, second, grad, rate):
    first = beta_one * first + (1.0 - beta_one) * grad
    second = beta_two * second + (1.0 - beta_two) * grad * grad
    corrected = first / (1.0 - beta_one**STEP)
    spread = jnp.sqrt(second / (1.0 - beta_two**STEP)) + adam_floor
    return (weight - rate * (corrected / spread + weight_decay * weight), first, second)


def encode(embed_rows, first, second):
    pairs = (embed_rows[:TASKS, None, :] + embed_rows[None, TASKS:, :]).reshape(TASKS * LAYERS, -1)
    return jnp.dot(jax.nn.gelu(jnp.dot(pairs, first, precision=highest)), second, precision=highest)


def mm(left, right):
    return lax.dot_general(
        left, right, (((1,), (0,)), ((), ())), preferred_element_type=jnp.float32
    )


def mm_last(left, right):
    return lax.dot_general(
        left, right, (((1,), (1,)), ((), ())), preferred_element_type=jnp.float32
    )


def mm_first(left, right):
    return lax.dot_general(
        left, right, (((0,), (0,)), ((), ())), preferred_element_type=jnp.float32
    )


def norm_scale(value):
    return lax.rsqrt(jnp.mean(value * value, axis=-1, keepdims=True) + epsilon)


def normed(value, gain):
    return (value * norm_scale(value) * gain).astype(jnp.bfloat16)


def norm_back(value, gain, grad):
    scale = norm_scale(value)
    weighted = grad * gain
    return scale * weighted - value * (
        scale * scale * scale * jnp.mean(weighted * value, axis=-1, keepdims=True)
    )


def gelu_tanh(value):
    return jnp.tanh(value * (GELU_A + (GELU_A * GELU_B) * (value * value)))


def gelu(value):
    return (0.5 * value) * (1.0 + gelu_tanh(value))


def gelu_slope(value, tanh):
    return 0.5 * (1.0 + tanh) + (0.5 * value) * (1.0 - tanh * tanh) * (
        GELU_A + (3.0 * GELU_A * GELU_B) * (value * value)
    )


def halves():
    lane = lax.broadcasted_iota(jnp.int32, (1, 128), 1)
    return [(lane // 64 == half) for half in range(2)]


def attend(q_ref, kv_ref, k_col, v_col, q_len, k_len, allow, out_ref, probs_ref=None):
    sides = halves()
    masks = [side.astype(jnp.float32).astype(jnp.bfloat16) for side in sides]

    def pair_step(pair, carry):
        lanes = pl.multiple_of(pair * 128, 128)
        for seq in range(SEQ_DEV):
            q_rows = pl.ds(seq * q_len, q_len)
            k_rows = pl.ds(seq * k_len, k_len)
            query = q_ref[q_rows, pl.ds(lanes, 128)]
            keys = kv_ref[k_rows, pl.ds(k_col + lanes, 128)]
            values = kv_ref[k_rows, pl.ds(v_col + lanes, 128)]
            outs = []
            for half in range(2):
                scores = mm_last(query * masks[half], keys) * 0.125
                scores = jnp.where(allow(seq), scores, blocked)
                peak = jnp.max(scores, axis=-1, keepdims=True)
                weights = jnp.exp(scores - peak)
                probs = weights * (1.0 / jnp.sum(weights, axis=-1, keepdims=True))
                if probs_ref is not None:
                    probs_ref[(pair * SEQ_DEV + seq) * 2 + half] = probs
                outs.append(mm(probs.astype(jnp.bfloat16), values))
            out_ref[q_rows, pl.ds(lanes, 128)] = jnp.where(sides[0], outs[0], outs[1]).astype(
                jnp.bfloat16
            )
        return carry

    lax.fori_loop(0, HEADS // 2, pair_step, 0)


def attend_back(grad_ref, q_ref, kv_ref, probs_ref, q_len, k_len, joined_ref):
    sides = halves()
    masks = [side.astype(jnp.float32).astype(jnp.bfloat16) for side in sides]

    def pair_step(pair, carry):
        lanes = pl.multiple_of(pair * 128, 128)
        for seq in range(SEQ_DEV):
            q_rows = pl.ds(seq * q_len, q_len)
            k_rows = pl.ds(seq * k_len, k_len)
            grad = grad_ref[q_rows, pl.ds(lanes, 128)]
            query = q_ref[q_rows, pl.ds(lanes, 128)]
            values = kv_ref[k_rows, pl.ds(D + lanes, 128)]
            key_grads, value_grads = [], []
            for half in range(2):
                probs = probs_ref[(pair * SEQ_DEV + seq) * 2 + half]
                grad_probs = mm_last(grad * masks[half], values)
                value_grads.append(mm_first(probs.astype(jnp.bfloat16), grad))
                inner = jnp.sum(grad_probs * probs, axis=-1, keepdims=True)
                grad_scores = (probs * (grad_probs - inner)).astype(jnp.bfloat16)
                key_grads.append(mm_first(grad_scores, query))
            joined_ref[k_rows, pl.ds(lanes, 128)] = (
                jnp.where(sides[0], key_grads[0], key_grads[1]) * 0.125
            ).astype(jnp.bfloat16)
            joined_ref[k_rows, pl.ds(D + lanes, 128)] = jnp.where(
                sides[0], value_grads[0], value_grads[1]
            ).astype(jnp.bfloat16)
        return carry

    lax.fori_loop(0, HEADS // 2, pair_step, 0)


def feed(state_ref, gain, inner_ref, outer_ref, act_ref, slope_ref, down_ref, up_ref, length,
         plain_ref, low_ref, after_ref):
    rows = SEQ_DEV * length
    act_rows = pl.ds(0, rows)
    source = normed(state_ref[...], gain)
    for block in range(FF // D):
        columns = slice(block * D, (block + 1) * D)
        hidden = mm(source, inner_ref[:, columns])
        tanh = gelu_tanh(hidden)
        act_ref[act_rows, columns] = ((0.5 * hidden) * (1.0 + tanh)).astype(jnp.bfloat16)
        if slope_ref is not None:
            slope_ref[:, columns] = gelu_slope(hidden, tanh)
    branch = mm(act_ref[act_rows, :], outer_ref[...])
    plain_ref[...] = branch.astype(jnp.bfloat16)
    for seq in range(SEQ_DEV):
        span = slice(seq * length, (seq + 1) * length)
        lowered = mm(plain_ref[span, :], down_ref[seq])
        low_ref[span, :] = lowered
        adapted = mm(gelu(lowered).astype(jnp.bfloat16), up_ref[seq]) * UPSCALE
        after_ref[span, :] = state_ref[span, :] + branch[span, :] + adapted


def adapter_back(grad_ref, low_ref, plain_ref, down_ref, up_ref, length, grad_down_ref,
                 grad_up_ref, branch_ref=None):
    for seq in range(SEQ_DEV):
        span = slice(seq * length, (seq + 1) * length)
        grad = grad_ref[span, :]
        grad_low = grad.astype(jnp.bfloat16)
        lowered = low_ref[span, :]
        tanh = gelu_tanh(lowered)
        bottleneck = ((0.5 * lowered) * (1.0 + tanh)).astype(jnp.bfloat16)
        grad_bottle = mm_last(grad_low, up_ref[seq]) * UPSCALE
        grad_up_ref[seq] = mm_first(bottleneck, grad_low)[:ADAPTER] * UPSCALE
        grad_lowered = (grad_bottle * gelu_slope(lowered, tanh)).astype(jnp.bfloat16)
        grad_down_ref[seq] = mm_first(plain_ref[span, :], grad_lowered)
        if branch_ref is not None:
            branch_ref[span, :] = (grad + mm_last(grad_lowered, down_ref[seq])).astype(
                jnp.bfloat16
            )


def step_kernel(
    rows_ref,
    down_ref,
    up_ref,
    allow_ref,
    valid_ref,
    gains_ref,
    attn_hbm,
    inner_hbm,
    outer_hbm,
    table_hbm,
    grad_down_ref,
    grad_up_ref,
    loss_ref,
    attn,
    inner,
    outer,
    table,
    state,
    after_e,
    plain_e,
    low_e,
    qkv,
    mixed,
    act,
    memory,
    y1,
    y2,
    y3,
    q_cross,
    kv_cross,
    probs,
    slope,
    plain_d,
    low_d,
    feats,
    total,
    results,
    arrived,
    stats,
    stats_in,
    grad,
    grad_low,
    joined,
    load_sem,
    feat_send,
    feat_recv,
    result_send,
    result_recv,
    stat_send,
    stat_recv,
):
    member = lax.axis_index("gen")
    barrier = pltpu.get_barrier_semaphore()

    def peer(order):
        chip = lax.rem(member // 2 + lax.rem((order + 1) // 2, 2), 2)
        return chip * 2 + lax.rem(lax.rem(member, 2) + order // 2, 2)

    for order in range(1, GEN):
        pl.semaphore_signal(
            barrier, inc=1, device_id={"gen": peer(order)}, device_id_type=MESH
        )

    loads = []
    for source, target in (
        (attn_hbm.at[0], attn.at[0]),
        (inner_hbm.at[0], inner.at[0]),
        (outer_hbm.at[0], outer.at[0]),
        (attn_hbm.at[1], attn.at[1]),
        (attn_hbm.at[2], attn.at[2]),
        (inner_hbm.at[1], inner.at[1]),
        (outer_hbm.at[1], outer.at[1]),
        (table_hbm, table),
    ):
        loads.append(pltpu.make_async_copy(source, target, load_sem.at[len(loads)]))
        loads[-1].start()

    embedded = jnp.concatenate([rows_ref[seq, :SRC] for seq in range(SEQ_DEV)], axis=0).astype(
        jnp.float32
    )
    entry = normed(embedded, gains_ref[0:1])
    loads[0].wait()
    for block in range(3):
        columns = slice(block * D, (block + 1) * D)
        qkv[:, columns] = mm(entry, attn[0, :, columns]).astype(jnp.bfloat16)
    attend(qkv, qkv, D, 2 * D, SRC, SRC, lambda seq: allow_ref[seq : seq + 1, :] > 0.0, mixed)
    state[...] = embedded + mm(mixed[...], attn[0, :, 3 * D :])
    loads[1].wait()
    loads[2].wait()
    feed(state, gains_ref[1:2], inner.at[0], outer.at[0], act, None, down_ref.at[0], up_ref.at[0],
         SRC, plain_e, low_e, after_e)
    memory[...] = normed(after_e[...], gains_ref[2:3])

    targets = SEQ_DEV * TGT
    inputs = jnp.concatenate(
        [rows_ref[seq, SRC : SRC + TGT] for seq in range(SEQ_DEV)], axis=0
    ).astype(jnp.float32)
    entry = normed(inputs, gains_ref[3:4])
    loads[3].wait()
    own = pl.ds(0, targets)
    for block in range(3):
        columns = slice(block * D, (block + 1) * D)
        qkv[own, columns] = mm(entry, attn[1, :, columns]).astype(jnp.bfloat16)
    causal = lax.broadcasted_iota(jnp.int32, (TGT, TGT), 0) >= lax.broadcasted_iota(
        jnp.int32, (TGT, TGT), 1
    )
    attend(qkv, qkv, D, 2 * D, TGT, TGT, lambda seq: causal, mixed)
    y1[...] = inputs + mm(mixed[own, :], attn[1, :, 3 * D :])
    loads[4].wait()
    q_cross[...] = mm(normed(y1[...], gains_ref[4:5]), attn[2, :, :D]).astype(jnp.bfloat16)
    for block in range(2):
        columns = slice(block * D, (block + 1) * D)
        kv_cross[:, columns] = mm(
            memory[...], attn[2, :, (block + 1) * D : (block + 2) * D]
        ).astype(jnp.bfloat16)
    attend(q_cross, kv_cross, 0, D, TGT, SRC, lambda seq: allow_ref[seq : seq + 1, :] > 0.0,
           mixed, probs)
    y2[...] = y1[...] + mm(mixed[own, :], attn[2, :, 3 * D :])
    loads[5].wait()
    loads[6].wait()
    feed(y2, gains_ref[5:6], inner.at[1], outer.at[1], act, slope, down_ref.at[1], up_ref.at[1],
         TGT, plain_d, low_d, y3)
    feats[0] = normed(y3[...], gains_ref[6:7])

    pl.semaphore_wait(barrier, GEN - 1)

    def feature_copy(order):
        return pltpu.make_async_remote_copy(
            src_ref=feats.at[0],
            dst_ref=feats.at[order],
            send_sem=feat_send.at[order],
            recv_sem=feat_recv.at[order],
            device_id={"gen": peer(order)},
            device_id_type=MESH,
        )

    def result_copy(order):
        return pltpu.make_async_remote_copy(
            src_ref=results.at[order],
            dst_ref=arrived.at[order],
            send_sem=result_send.at[order],
            recv_sem=result_recv.at[order],
            device_id={"gen": peer(order)},
            device_id_type=MESH,
        )

    def stat_copy(order):
        return pltpu.make_async_remote_copy(
            src_ref=stats.at[order],
            dst_ref=stats_in.at[order],
            send_sem=stat_send.at[order],
            recv_sem=stat_recv.at[order],
            device_id={"gen": peer(order)},
            device_id_type=MESH,
        )

    for order in range(1, GEN):
        feature_copy(order).start()
    loads[7].wait()
    same = lax.broadcasted_iota(jnp.int32, (targets, targets), 0) == lax.broadcasted_iota(
        jnp.int32, (targets, targets), 1
    )

    def as_row(column):
        return jnp.sum(jnp.where(same, column, 0.0), axis=0, keepdims=True)

    def as_column(row):
        return jnp.sum(jnp.where(same, row, 0.0), axis=1, keepdims=True)

    def block_step(order, carry):
        @pl.when(order > 0)
        def _():
            feature_copy(order).wait_recv()

        query = feats[order]
        ends = list(range(0, table.shape[0], VOCAB_TILE)) + [table.shape[0]]
        tiles = [(ends[i], ends[i + 1]) for i in range(len(ends) - 1)]
        peak = scale = None
        scores = mm_last(query, table[tiles[0][0] : tiles[0][1], :])
        for index, (first, last) in enumerate(tiles):
            following = None
            if index + 1 < len(tiles):
                following = mm_last(query, table[tiles[index + 1][0] : tiles[index + 1][1], :])
            top = jnp.max(scores, axis=-1, keepdims=True)
            if index > 0:
                top = jnp.maximum(peak, top)
            weights = jnp.exp2((scores - top) * EXP_SCALE)
            amount = jnp.sum(weights, axis=-1, keepdims=True)
            part = mm(weights.astype(jnp.bfloat16), table[first:last, :])
            if index == 0:
                total[...] = part
                scale = amount
            else:
                shrink = jnp.exp2((peak - top) * EXP_SCALE)
                total[...] = total[...] * shrink + part
                scale = scale * shrink + amount
            peak, scores = top, following
        results[order] = total[...].astype(jnp.bfloat16)
        stats[order] = jnp.concatenate(
            [as_row(peak), as_row(scale), jnp.zeros((6, targets), jnp.float32)], axis=0
        )

        @pl.when(order > 0)
        def _():
            result_copy(order).start()
            stat_copy(order).start()

        return carry

    lax.fori_loop(0, GEN, block_step, 0)
    stats_in[0] = stats[0]
    for order in range(1, GEN):
        stat_copy(order).wait_recv()
    peaks = [as_column(stats_in[order, 0:1, :]) for order in range(GEN)]
    sums = [as_column(stats_in[order, 1:2, :]) for order in range(GEN)]
    top = jnp.maximum(jnp.maximum(peaks[0], peaks[1]), jnp.maximum(peaks[2], peaks[3]))
    shares = [jnp.exp2((peaks[order] - top) * EXP_SCALE) for order in range(GEN)]
    amount = sum(shares[order] * sums[order] for order in range(GEN))
    logsum = top * LOGIT_SCALE + jnp.log(amount)
    inverse = 1.0 / amount
    expected = total_rows = None
    total[...] = results[0].astype(jnp.float32) * (shares[0] * inverse)
    for order in range(1, GEN):
        result_copy(order).wait_recv()
        total[...] = total[...] + arrived[order].astype(jnp.float32) * (shares[order] * inverse)
    wanted = jnp.concatenate(
        [
            rows_ref[seq, SRC : SRC + TGT + 8].astype(jnp.float32)[1 : TGT + 1]
            for seq in range(SEQ_DEV)
        ],
        axis=0,
    )
    picked = jnp.sum(feats[0].astype(jnp.float32) * wanted, axis=-1, keepdims=True) * LOGIT_SCALE
    counted = valid_ref[:, 0:1]
    loss = jnp.sum((logsum - picked) * counted, axis=0, keepdims=True)
    loss_ref[...] = jnp.broadcast_to(loss, (8, 128))

    grad[own, :] = norm_back(
        y3[...], gains_ref[6:7], (total[...] - wanted) * (counted * LOGIT_SCALE)
    )
    adapter_back(grad.at[own], low_d, plain_d, down_ref.at[1], up_ref.at[1], TGT,
                 grad_down_ref.at[1], grad_up_ref.at[1], grad_low)
    for block in range(FF // D):
        columns = slice(block * D, (block + 1) * D)
        act[own, columns] = (
            mm_last(grad_low[...], outer[1, columns, :]) * slope[:, columns]
        ).astype(jnp.bfloat16)
    grad_entry = mm_last(act[own, :], inner[1])
    grad_state = grad[own, :] + norm_back(y2[...], gains_ref[5:6], grad_entry)
    mixed[own, :] = mm_last(grad_state.astype(jnp.bfloat16), attn[2, :, 3 * D :]).astype(
        jnp.bfloat16
    )
    attend_back(mixed, q_cross, kv_cross, probs, TGT, SRC, joined)
    grad_memory = mm_last(joined[...], attn[2, :, D : 3 * D])

    grad[...] = norm_back(after_e[...], gains_ref[2:3], grad_memory)
    adapter_back(grad, low_e, plain_e, down_ref.at[0], up_ref.at[0], SRC,
                 grad_down_ref.at[0], grad_up_ref.at[0])
    for order in range(1, GEN):
        feature_copy(order).wait_send()
        result_copy(order).wait_send()
        stat_copy(order).wait_send()


def step(rows, down, up, allow, valid, gains, attn_w, ffn_in, ffn_out, table):
    vmem = pl.BlockSpec(memory_space=pltpu.VMEM)
    whole = pl.BlockSpec(memory_space=pl.ANY)
    low, full = jnp.bfloat16, jnp.float32
    sources, targets = SEQ_DEV * SRC, SEQ_DEV * TGT
    return pl.pallas_call(
        step_kernel,
        out_shape=(
            jax.ShapeDtypeStruct((LAYERS, SEQ_DEV, D, LOW), full),
            jax.ShapeDtypeStruct((LAYERS, SEQ_DEV, ADAPTER, D), full),
            jax.ShapeDtypeStruct((8, 128), full),
        ),
        in_specs=[vmem] * 6 + [whole] * 4,
        out_specs=(vmem, vmem, vmem),
        scratch_shapes=[
            pltpu.VMEM(attn_w.shape, low),
            pltpu.VMEM(ffn_in.shape, low),
            pltpu.VMEM(ffn_out.shape, low),
            pltpu.VMEM(table.shape, low),
            pltpu.VMEM((sources, D), full),
            pltpu.VMEM((sources, D), full),
            pltpu.VMEM((sources, D), low),
            pltpu.VMEM((sources, LOW), full),
            pltpu.VMEM((sources, 3 * D), low),
            pltpu.VMEM((sources, D), low),
            pltpu.VMEM((sources, FF), low),
            pltpu.VMEM((sources, D), low),
            pltpu.VMEM((targets, D), full),
            pltpu.VMEM((targets, D), full),
            pltpu.VMEM((targets, D), full),
            pltpu.VMEM((targets, D), low),
            pltpu.VMEM((sources, 2 * D), low),
            pltpu.VMEM((SEQ_DEV * HEADS, TGT, SRC), full),
            pltpu.VMEM((targets, FF), full),
            pltpu.VMEM((targets, D), low),
            pltpu.VMEM((targets, LOW), full),
            pltpu.VMEM((GEN, targets, D), low),
            pltpu.VMEM((targets, D), full),
            pltpu.VMEM((GEN, targets, D), low),
            pltpu.VMEM((GEN, targets, D), low),
            pltpu.VMEM((GEN, 8, targets), full),
            pltpu.VMEM((GEN, 8, targets), full),
            pltpu.VMEM((sources, D), full),
            pltpu.VMEM((targets, D), low),
            pltpu.VMEM((sources, 2 * D), low),
            pltpu.SemaphoreType.DMA((8,)),
            pltpu.SemaphoreType.DMA((GEN,)),
            pltpu.SemaphoreType.DMA((GEN,)),
            pltpu.SemaphoreType.DMA((GEN,)),
            pltpu.SemaphoreType.DMA((GEN,)),
            pltpu.SemaphoreType.DMA((GEN,)),
            pltpu.SemaphoreType.DMA((GEN,)),
        ],
        compiler_params=pltpu.CompilerParams(
            collective_id=1, has_side_effects=True, vmem_limit_bytes=60 * 1024 * 1024
        ),
        name="forward_vocab_backward",
    )(rows, down, up, allow, valid, gains, attn_w, ffn_in, ffn_out, table)


def sum_kernel(
    slots_ref,
    totals_ref,
    coded_ref,
    hyper_ref,
    out_ref,
    small_ref,
    outgoing,
    incoming,
    shares,
    outgoing_small,
    incoming_small,
    send_sem,
    recv_sem,
    share_send_sem,
    share_recv_sem,
    small_send_sem,
    small_recv_sem,
):
    rank = lax.axis_index("dp")
    count = outgoing.shape[0]
    width = shares.shape[2]
    per_half = slots_ref.shape[1] // width
    member = lax.axis_index("gen")
    barrier = pltpu.get_barrier_semaphore()

    def greet(step, carry):
        pl.semaphore_signal(
            barrier, inc=1, device_id={"dp": lax.rem(rank + step, count)}, device_id_type=MESH
        )
        return carry

    lax.fori_loop(1, count, greet, 0)
    for step in range(1, GEN):
        pl.semaphore_signal(
            barrier, inc=1, device_id={"gen": lax.rem(member + step, GEN)}, device_id_type=MESH
        )
    for piece in range(count):
        row, column = piece // per_half * 8, piece % per_half * width
        outgoing[piece, :, :width] = slots_ref[row : row + 8, column : column + width]
        outgoing[piece, :, width:] = totals_ref[...]
    pl.semaphore_wait(barrier, count + GEN - 2)

    def scatter_to(step):
        target = lax.rem(rank + step, count)
        return pltpu.make_async_remote_copy(
            src_ref=outgoing.at[target],
            dst_ref=incoming.at[rank],
            send_sem=send_sem.at[target],
            recv_sem=recv_sem.at[rank],
            device_id={"dp": target},
            device_id_type=MESH,
        )

    def scatter_from(step):
        source = lax.rem(rank + step, count)
        return pltpu.make_async_remote_copy(
            src_ref=outgoing.at[source],
            dst_ref=incoming.at[source],
            send_sem=send_sem.at[source],
            recv_sem=recv_sem.at[source],
            device_id={"dp": source},
            device_id_type=MESH,
        )

    def share_to(step):
        target = lax.rem(rank + step, count)
        return pltpu.make_async_remote_copy(
            src_ref=shares.at[rank],
            dst_ref=shares.at[rank],
            send_sem=share_send_sem.at[target],
            recv_sem=share_recv_sem.at[rank],
            device_id={"dp": target},
            device_id_type=MESH,
        )

    def share_from(step):
        source = lax.rem(rank + step, count)
        return pltpu.make_async_remote_copy(
            src_ref=shares.at[rank],
            dst_ref=shares.at[source],
            send_sem=share_send_sem.at[source],
            recv_sem=share_recv_sem.at[source],
            device_id={"dp": source},
            device_id_type=MESH,
        )

    def each(make, act):
        def body(step, carry):
            act(make(step))
            return carry

        lax.fori_loop(1, count, body, 0)

    each(scatter_to, lambda copy: copy.start())
    incoming[rank] = outgoing[rank]
    each(scatter_from, lambda copy: copy.wait_recv())
    summed = incoming[0]
    for source in range(1, count):
        summed = summed + incoming[source]
    shares[rank] = summed[:, :width]
    each(share_to, lambda copy: copy.start())
    each(scatter_to, lambda copy: copy.wait_send())
    each(share_from, lambda copy: copy.wait_recv())
    for piece in range(count):
        row, column = piece // per_half * 8, piece % per_half * width
        out_ref[row : row + 8, column : column + width] = shares[piece]
    slots = out_ref[...]
    coded_part = lax.dot_general(
        slots, hyper_ref[...], (((1,), (1,)), ((), ())), precision=highest,
        preferred_element_type=jnp.float32,
    )
    hyper_grad = lax.dot_general(
        coded_ref[...], slots, (((0,), (0,)), ((), ())), precision=highest,
        preferred_element_type=jnp.float32,
    )
    square = jnp.sum(hyper_grad * hyper_grad, axis=0, keepdims=True)
    outgoing_small[0:16, :] = jnp.concatenate(
        [coded_part, jnp.zeros((16, 64), jnp.float32)], axis=1
    )
    outgoing_small[16:24, :] = jnp.broadcast_to(
        jnp.sum(square, axis=1, keepdims=True), (8, 128)
    )
    outgoing_small[24:32, :] = summed[:, width:]
    copies = [
        pltpu.make_async_remote_copy(
            src_ref=outgoing_small,
            dst_ref=incoming_small.at[member],
            send_sem=small_send_sem.at[step],
            recv_sem=small_recv_sem.at[step],
            device_id={"gen": lax.rem(member + step, GEN)},
            device_id_type=MESH,
        )
        for step in range(1, GEN)
    ]
    for copy in copies:
        copy.start()
    incoming_small[member] = outgoing_small[...]
    each(share_to, lambda copy: copy.wait_send())
    for copy in copies:
        copy.wait()
    small_ref[...] = (incoming_small[0] + incoming_small[1]) + (
        incoming_small[2] + incoming_small[3]
    )


def summed_over_devices(slots, totals, coded, hyper):
    vmem = pl.BlockSpec(memory_space=pltpu.VMEM)
    count = lax.axis_size("dp")
    width = slots.shape[0] * slots.shape[1] // (8 * count)
    return pl.pallas_call(
        sum_kernel,
        out_shape=(
            jax.ShapeDtypeStruct(slots.shape, jnp.float32),
            jax.ShapeDtypeStruct((32, 128), jnp.float32),
        ),
        in_specs=[vmem] * 4,
        out_specs=(vmem, vmem),
        scratch_shapes=[
            pltpu.VMEM((count, 8, width + 128), jnp.float32),
            pltpu.VMEM((count, 8, width + 128), jnp.float32),
            pltpu.VMEM((count, 8, width), jnp.float32),
            pltpu.VMEM((32, 128), jnp.float32),
            pltpu.VMEM((GEN, 32, 128), jnp.float32),
            pltpu.SemaphoreType.DMA((count,)),
            pltpu.SemaphoreType.DMA((count,)),
            pltpu.SemaphoreType.DMA((count,)),
            pltpu.SemaphoreType.DMA((count,)),
            pltpu.SemaphoreType.DMA((GEN,)),
            pltpu.SemaphoreType.DMA((GEN,)),
        ],
        compiler_params=pltpu.CompilerParams(
            collective_id=0, has_side_effects=True, vmem_limit_bytes=32 * 1024 * 1024
        ),
        name="sum_over_devices",
    )(slots, totals, coded, hyper)


def per_device(
    src_ids,
    tgt_ids,
    task_ids,
    task_len,
    tgt_count,
    table,
    attn_w,
    ffn_in,
    ffn_out,
    gains,
    embeds,
    embeds_m,
    embeds_v,
    proj_one,
    proj_one_m,
    proj_one_v,
    proj_two,
    proj_two_m,
    proj_two_v,
    hyper,
    hyper_m,
    hyper_v,
):
    groups = lax.axis_size("gen")
    member = lax.axis_index("gen")
    vocab_part = table.shape[0]
    offset = member * vocab_part
    area = D * ADAPTER
    coded, pullback = jax.vjp(encode, embeds, proj_one, proj_two)
    generated = jnp.dot(coded, hyper, precision=highest)
    sequences = groups * SEQ_DEV
    tokens = jnp.concatenate(
        [src_ids, jnp.zeros_like(tgt_ids[:, :1]), tgt_ids, jnp.zeros_like(tgt_ids[:, :7])], axis=1
    ).reshape(-1)
    token = tokens - offset
    inside = (token >= 0) & (token < vocab_part)
    rows = jnp.take(table, jnp.clip(token, 0, vocab_part - 1), axis=0)
    rows = lax.psum_scatter(
        jnp.where(inside[:, None], rows, jnp.zeros_like(rows)),
        "gen",
        scatter_dimension=0,
        tiled=True,
    ).reshape(SEQ_DEV, ROWS, -1)
    row_index = (task_ids[:, None] * LAYERS + jnp.arange(LAYERS)[None]).reshape(-1)
    select = (row_index[:, None] == jnp.arange(TASKS * LAYERS)[None]).astype(jnp.float32)
    piece = jnp.dot(select, generated, precision=highest).astype(jnp.bfloat16)
    adapters = lax.all_to_all(piece, "gen", split_axis=0, concat_axis=1, tiled=True).reshape(
        SEQ_DEV, LAYERS, -1
    )
    adapters = adapters.transpose(1, 0, 2)
    down = jnp.pad(
        adapters[..., :area].reshape(LAYERS, SEQ_DEV, D, ADAPTER),
        ((0, 0), (0, 0), (0, 0), (0, LOW - ADAPTER)),
    )
    up = jnp.pad(
        adapters[..., area:].reshape(LAYERS, SEQ_DEV, ADAPTER, D),
        ((0, 0), (0, 0), (0, LOW - ADAPTER), (0, 0)),
    )
    lengths = jnp.sum(jnp.where(task_ids[:, None] == jnp.arange(TASKS)[None], task_len[None], 0), axis=1)
    own_len = lax.dynamic_slice_in_dim(lengths, member * SEQ_DEV, SEQ_DEV)
    own_count = lax.dynamic_slice_in_dim(tgt_count, member * SEQ_DEV, SEQ_DEV)
    allow = (jnp.arange(SRC)[None, :] < own_len[:, None]).astype(jnp.float32)
    allow = jnp.pad(allow, ((0, 8 - SEQ_DEV), (0, 0)))
    valid = (jnp.arange(TGT)[None] < own_count[:, None]).reshape(-1, 1).astype(jnp.float32)
    valid = jnp.broadcast_to(valid, (SEQ_DEV * TGT, 128))
    gains = jnp.pad(gains, ((0, 1), (0, 0)))
    grad_down, grad_up, loss = step(
        rows, down, up, allow, valid, gains, attn_w, ffn_in, ffn_out, table
    )
    grad_rows = jnp.concatenate(
        [
            grad_down[..., :ADAPTER].reshape(LAYERS, SEQ_DEV, -1),
            grad_up.reshape(LAYERS, SEQ_DEV, -1),
        ],
        axis=-1,
    )
    grad_rows = grad_rows.transpose(1, 0, 2).reshape(SEQ_DEV * LAYERS, -1)
    returned = lax.all_to_all(grad_rows, "gen", split_axis=1, concat_axis=0, tiled=True)
    slots = jnp.dot(select.T, returned, precision=highest)
    count_local = jnp.sum(own_count).astype(jnp.float32)
    lane = lax.broadcasted_iota(jnp.int32, (8, 128), 1)
    totals = jnp.where(lane == 0, loss, jnp.where(lane == 1, count_local, 0.0))
    slots, small = summed_over_devices(slots, totals, coded, hyper)
    coded_grad = small[:16, :64]
    hyper_square = small[16, 0]
    loss_sum = small[24, 0]
    token_count = small[24, 1]
    hyper_grad = jnp.dot(coded.T, slots, precision=highest)
    grad_embeds, grad_one, grad_two = pullback(coded_grad)
    count_scale = 1.0 / token_count
    grads = [grad * count_scale for grad in (grad_embeds, grad_one, grad_two, hyper_grad)]
    square = (
        hyper_square * count_scale * count_scale
        + jnp.sum(grads[0] * grads[0])
        + jnp.sum(grads[1] * grads[1])
        + jnp.sum(grads[2] * grads[2])
    )
    grad_norm = jnp.sqrt(square)
    factor = jnp.minimum(1.0, clip_limit / (grad_norm + 1e-06))
    weights = (embeds, proj_one, proj_two, hyper)
    firsts = (embeds_m, proj_one_m, proj_two_m, hyper_m)
    seconds = (embeds_v, proj_one_v, proj_two_v, hyper_v)
    updated = [
        adamw(weights[index], firsts[index], seconds[index], grads[index] * factor, rates[index])
        for index in range(4)
    ]
    return (
        loss_sum,
        token_count,
        grad_norm,
        updated[0][0],
        updated[0][1],
        updated[0][2],
        updated[1][0],
        updated[1][1],
        updated[1][2],
        updated[2][0],
        updated[2][1],
        updated[2][2],
        updated[3][0],
        updated[3][1],
        updated[3][2],
    )


def solution(mesh):
    return jax.shard_map(
        per_device,
        mesh=mesh,
        in_specs=(
            P("dp", None),
            P("dp", None),
            P("dp"),
            P(),
            P("dp"),
            P("gen", None),
            P(),
            P(),
            P(),
            P(),
            P(),
            P(),
            P(),
            P(),
            P(),
            P(),
            P(),
            P(),
            P(),
            P(None, "gen"),
            P(None, "gen"),
            P(None, "gen"),
        ),
        out_specs=(
            P(),
            P(),
            P(),
            P(),
            P(),
            P(),
            P(),
            P(),
            P(),
            P(),
            P(),
            P(),
            P(None, "gen"),
            P(None, "gen"),
            P(None, "gen"),
        ),
        check_vma=False,
    )
```

time: 734 us -> 204 us (0.28); the launches traced: 725 us -> 203 us
  waiting for transfers between devices: 283 us -> 32.8 us
  blocking collectives: 160 us -> 0 us
  matrix products: 124 us -> 10.6 us
  Pallas kernels: 0 us -> 93.6 us
  local copies, waits for them, and re-layouts: 72.7 us -> 26.9 us
  other arithmetic: 44 us -> 11.5 us
  starting transfers between devices: 16.1 us -> 8.5 us
    psum x1 -> x0, waiting for transfers between devices: 240 us -> none  [per_device(): lax.psum((hyper_local, coded_local, loss_local, count_local), 'dp')]
    psum x2 -> x0, blocking collectives: 115 us -> none  [the longest x1 86.4 us: per_device(): lax.psum((hyper_local, coded_local, loss_local, count_local), 'dp')]
    dot_general x76 -> x2, matrix products: 120 us -> 7.16 us  [the longest x1 6.72 us: per_device(): hyper_grad = jnp.dot(coded.T, slots, precision=highest)]
    pallas_call x0 -> x2, Pallas kernels: none -> 93.6 us  [the longest x1 61.4 us: step(): pl.pallas_call(step_kernel, out_shape=(jax.ShapeDtypeStruct((LAYERS, SEQ_...]
    all_gather x8 -> x0, blocking collectives: 45.7 us -> none  [the longest x6 30.9 us: merged(): gathered = jax.tree.map(lambda a: lax.all_gather(a, axis), part)]
    reduce_sum x17 -> x2, other arithmetic: 19.3 us -> 0.89 us  [the longest x1 0.7 us: per_device(): count_local = jnp.sum(own_count).astype(jnp.float32)]
    unnamed x288 -> x30, local copies, waits for them, and re-layouts: 15.8 us -> 1.01 us
    slice x23 -> x3, local copies, waits for them, and re-layouts: 11.4 us -> 0.83 us  [the longest x1 0.59 us: per_device(): hyper_square = small[16, 0]]
  transfers between devices with their start and end apart: 9 -> 3, of which waited for: 7 -> 3; matrix products, arithmetic and copies ran while one was open for 8% -> 4% of each run, Pallas kernels for 0% -> 0%
where the time goes in v1:
time: 204 us; the launch traced here: 203 us
  Pallas kernels  93.6 us (46%)
  waiting for transfers between devices  32.8 us (16%)
  local copies, waits for them, and re-layouts  26.9 us (13%)
  between operations  19.5 us (10%)
  other arithmetic  11.5 us (6%)
  matrix products  10.6 us (5%)
  starting transfers between devices  8.5 us (4%)
    pallas_call x1, Pallas kernels, step(): pl.pallas_call(step_kernel, out_shape=(jax.ShapeDtypeStruct((LAYERS, SEQ_...  61.4 us
    pallas_call x1, Pallas kernels, summed_over_devices(): pl.pallas_call(sum_kernel, out_shape=(jax.ShapeDtypeStruct(slots.shape, j...  32.1 us
    reduce_scatter x1, waiting for transfers between devices, per_device(): lax.psum_scatter(jnp.where(inside[:, None], rows, jnp.zeros_like(rows)),...  25.2 us
    gather x1, local copies, waits for them, and re-layouts, per_device(): rows = jnp.take(table, jnp.clip(token, 0, vocab_part - 1), axis=0)  14.8 us
    dot_general x1, matrix products, per_device(): hyper_grad = jnp.dot(coded.T, slots, precision=highest)  6.72 us
    all_to_all x1, waiting for transfers between devices, per_device(): lax.all_to_all(grad_rows, 'gen', split_axis=1, concat_axis=0, tiled=True)  6.15 us
    select_n x1, other arithmetic, per_device(): jnp.where(inside[:, None], rows, jnp.zeros_like(rows))  5.29 us
    all_to_all x1, starting transfers between devices, per_device(): lax.all_to_all(piece, 'gen', split_axis=0, concat_axis=1, tiled=True)  4.75 us
  transfers between devices with their start and end apart: 3, of which 3 were waited for; matrix products, arithmetic and copies ran while one was open for 4% of the time, Pallas kernels for 0%

profile of v1, /device:TPU:1, one launch (start us, length us, event | category | flops | bytes accessed | tf_op | source)
XLA Modules:
  0.0 203.5 jit_solution(14327876128168431880)
XLA Ops:
  7.3 0.8 fusion.5
  8.3 0.8 compare_and_fusion.1
  9.3 14.8 %gather_fusion = bf16[3136,512]{1,0:T(8,128)(2,1)} fusion(bf16[8032,512]{1,0:T(8,128)(2,1)} %table_hbm.1, s32[4096]{0:T(1024)S(1)} %pad_clamp_fusion), kind=kCustom, calls=%fused_computation | custom fusion | bytes 6435072 | tf_op jit(solution)/shard_map/jit(_take)/gather | solution.py:751
  24.1 5.3 %select_select_fusion = bf16[3136,512]{1,0:T(8,128)(2,1)} fusion(bf16[3136,512]{1,0:T(8,128)(2,1)} %gather_fusion, pred[3136]{0:T(1024)(128)(4,1)S(1)} %compare_and_fusion, pred[3136]{0:T(1024)(128)(4,1)S(1)} %and.19), kind=kLoop, calls=%fused_computation.4 | loop fusion | flops 3211264 | bytes 6428800 | tf_op jit(solution)/shard_map/jit(_where)/select_n | solution.py:753
  30.9 0.9 fusion.41
  32.1 0.8 all_to_all.26
  32.8 4.8 %all-to-all-start = ((bf16[4,4,6144]{2,1,0:T(4,128)(2,1)}), bf16[4,4,6144]{2,1,0:T(4,128)(2,1)S(1)}, u32[]{:S(2)}, u32[]{:S(2)}) async-start(bf16[4,4,6144]{2,1,0:T(4,128)(2,1)} %all_to_all.26), calls=%async_computation.1 | async-start | bytes 393216 | tf_op jit(solution)/shard_map/all_to_all | solution.py:761
  37.9 0.7 fusion.37
  40.6 1.5 all-to-all-done
  42.7 0.7 reshape.162
  43.5 0.9 pad.24.down_ref
  44.4 0.8 pad.25.up_ref
  45.2 25.2 %reduce-scatter.2.cloned.1.call-done = bf16[784,512]{1,0:T(8,128)(2,1)} async-done(((bf16[3136,512]{1,0:T(8,128)(2,1)}), bf16[784,512]{1,0:T(8,128)(2,1)}) %reduce-scatter.2.cloned.1.call-update) | async-done | bytes 802832 | tf_op jit(solution)/shard_map/reduce_scatter | solution.py:752
  70.4 0.8 broadcast_in_dim.69.valid_ref
  71.2 61.4 %forward_vocab_backward.1 = (f32[2,2,512,128]{3,2,1,0:T(8,128)}, f32[2,2,24,512]{3,2,1,0:T(8,128)}, f32[8,128]{1,0:T(8,128)}) custom-call(bf16[2,392,512]{2,1,0:T(8,128)(2,1)} %bitcast.37, bf16[2,2,512,128]{3,2,1,0:T(8,128)(2,1)} %pad.24.down_ref, bf16[2,2,128,512]{3,2,1,0:T(8,128)(2,1)} %pad.25.up_ref, f32[8,256]{1,0:T(8,128)} %pad_convert_fusion.allow_ref, ...), custom_call_target="tpu_custom_call" | custom-call | tf_op jit(solution)/shard_map/forward_vocab_backward/pallas_call | solution.py:481
  132.6 1.9 reshape.164
  134.5 1.1 reshape.165
  136.5 1.0 copy.51
  137.5 3.7 %all-to-all-start.1 = ((f32[4,4,6144]{2,0,1:T(4,128)}), f32[4,4,6144]{2,0,1:T(4,128)S(1)}, u32[]{:S(2)}, u32[]{:S(2)}) async-start(f32[4,4,6144]{2,0,1:T(4,128)} %copy.51), calls=%async_computation.2 | async-start | bytes 786432 | tf_op jit(solution)/shard_map/all_to_all | solution.py:792
  141.3 6.1 %all-to-all-done.1 = f32[4,4,6144]{2,0,1:T(4,128)S(1)} async-done(((f32[4,4,6144]{2,0,1:T(4,128)}), f32[4,4,6144]{2,0,1:T(4,128)S(1)}, u32[]{:S(2)}, u32[]{:S(2)}) %all-to-all-start.1) | async-done | bytes 393248 | tf_op jit(solution)/shard_map/all_to_all | solution.py:792
  148.0 32.1 %sum_over_devices.1 = (f32[16,6144]{1,0:T(8,128)S(1)}, f32[32,128]{1,0:T(8,128)S(1)}) custom-call(f32[16,6144]{1,0:T(8,128)S(1)} %fusion.13.slots_ref, f32[8,128]{1,0:T(8,128)S(1)} %broadcast_select_fusion.totals_ref, f32[16,64]{1,0:T(8,128)S(1)} %fusion.22.coded_ref, f32[64,6144]{1,0:T(8,128)S(1)} %copy-done), custom_call_target="tpu_custom_call" | custom-call | tf_op jit(solution)/shard_map/sum_over_devices/pallas_call | solution.py:686
  181.6 0.8 multiply_reduce_fusion
  182.4 0.8 multiply_reduce_fusion.1
  187.4 6.7 %multiply_subtract_fusion = (f32[64,6144]{1,0:T(8,128)}, f32[64,6144]{1,0:T(8,128)}, f32[64,6144]{1,0:T(8,128)}) fusion(f32[64,6144]{1,0:T(8,128)S(1)} %copy-done, f32[64,6144]{1,0:T(8,128)} %param.42, f32[64,6144]{1,0:T(8,128)} %param.43, f32[]{:T(128)S(6)} %min.22, f32[]{:T(128)S(6)} %div.66, f32[16,64]{1,0:T(8,128)S(1)} %fusion.22.coded_ref, ...), kind=kOutput, calls=%fused_computation.7 | convolution fusion | flops 82182144 | bytes 9834504 | tf_op jit(solution)/shard_map/dot_general | solution.py:802
  (80 shorter events, 9.5 us)
Async XLA Ops:
  7.2 63.2 %reduce-scatter.2.cloned.1.call-start = ((), (), s32[]{:S(2)}) async-start(), calls=%async_computation.3 | async-start | bytes 4014080 | tf_op jit(solution)/shard_map/reduce_scatter | solution.py:752
  29.4 0.7 copy-start.13
  29.4 0.8 slice-start
  29.4 0.8 slice-start.1
  29.4 0.8 copy-start.2
  29.4 1.0 copy-start.1
  29.4 1.5 copy-start
  30.8 6.8 %copy-start.14 = (s32[8]{0:T(128)S(1)}, s32[8]{0:T(128)}, u32[]{:S(2)}) copy-start(s32[8]{0:T(128)} %param.25) | copy-start | bytes 100
  30.9 7.0 %copy-start.12 = (s32[8]{0:T(128)S(1)}, s32[8]{0:T(128)}, u32[]{:S(2)}) copy-start(s32[8]{0:T(128)} %param.26) | copy-start | bytes 100
  30.9 8.5 %copy-start.8 = (f32[7,512]{1,0:T(8,128)S(1)}, f32[7,512]{1,0:T(8,128)}, u32[]{:S(2)}) copy-start(f32[7,512]{1,0:T(8,128)} %param.31) | copy-start | bytes 43012
  32.8 9.2 %all-to-all-start = ((bf16[4,4,6144]{2,1,0:T(4,128)(2,1)}), bf16[4,4,6144]{2,1,0:T(4,128)(2,1)S(1)}, u32[]{:S(2)}, u32[]{:S(2)}) async-start(bf16[4,4,6144]{2,1,0:T(4,128)(2,1)} %all_to_all.26), calls=%async_computation.1 | async-start | bytes 393216 | tf_op jit(solution)/shard_map/all_to_all | solution.py:761
  135.8 5.5 %copy-start.11 = (f32[8,128]{1,0:T(8,128)S(1)}, f32[8,128]{1,0:T(8,128)}, u32[]{:S(2)}) copy-start(f32[8,128]{1,0:T(8,128)} %get-tuple-element.22) | copy-start | bytes 12292
  137.5 9.9 %all-to-all-start.1 = ((f32[4,4,6144]{2,0,1:T(4,128)}), f32[4,4,6144]{2,0,1:T(4,128)S(1)}, u32[]{:S(2)}, u32[]{:S(2)}) async-start(f32[4,4,6144]{2,0,1:T(4,128)} %copy.51), calls=%async_computation.2 | async-start | bytes 786432 | tf_op jit(solution)/shard_map/all_to_all | solution.py:792
  147.5 39.2 %copy-start.7 = (f32[10,64]{1,0:T(8,128)S(1)}, f32[10,64]{1,0:T(8,128)}, u32[]{:S(2)}) copy-start(f32[10,64]{1,0:T(8,128)} %param.32) | copy-start | bytes 7684
  147.6 39.2 %copy-start.9 = (f32[10,64]{1,0:T(8,128)S(1)}, f32[10,64]{1,0:T(8,128)}, u32[]{:S(2)}) copy-start(f32[10,64]{1,0:T(8,128)} %param.33) | copy-start | bytes 7684
  147.6 39.2 %copy-start.10 = (f32[10,64]{1,0:T(8,128)S(1)}, f32[10,64]{1,0:T(8,128)}, u32[]{:S(2)}) copy-start(f32[10,64]{1,0:T(8,128)} %param.34) | copy-start | bytes 7684
  187.4 6.7 %copy-start.3 = (f32[128,64]{0,1:T(8,128)S(1)}, f32[128,64]{0,1:T(8,128)}, u32[]{:S(2)}) copy-start(f32[128,64]{0,1:T(8,128)} %param.39) | copy-start | bytes 98308
  187.4 6.7 %copy-start.4 = (f32[128,64]{0,1:T(8,128)S(1)}, f32[128,64]{0,1:T(8,128)}, u32[]{:S(2)}) copy-start(f32[128,64]{0,1:T(8,128)} %param.40) | copy-start | bytes 98308
  187.4 7.4 %copy-start.5 = (f32[64,128]{1,0:T(8,128)S(1)}, f32[64,128]{1,0:T(8,128)}, u32[]{:S(2)}) copy-start(f32[64,128]{1,0:T(8,128)} %param.36) | copy-start | bytes 98308
  187.4 7.4 %copy-start.6 = (f32[64,128]{1,0:T(8,128)S(1)}, f32[64,128]{1,0:T(8,128)}, u32[]{:S(2)}) copy-start(f32[64,128]{1,0:T(8,128)} %param.37) | copy-start | bytes 98308
Sparse Core Ops, SparseCore 0:
  29.5 40.8 reduce-scatter.1

commit v2 on v1

v2 whole, which is shorter than its diff:
```python
import math

import jax
import jax.numpy as jnp
from jax import lax
from jax.experimental import pallas as pl
from jax.experimental.pallas import tpu as pltpu
from jax.sharding import PartitionSpec as P

D = 512
HEADS = 8
ADAPTER = 24
TASKS = 8
LAYERS = 2
SRC = 256
TGT = 128
FF = 2048
SEQ_DEV = 2
GEN = 4
LOW = 128
SRC_CAP = 176
TGT_CAP = 128
TGT_ROWS = TGT_CAP + 16
FLAT = 48
STEP = 5


epsilon = 1e-06
clip_limit = 0.001
beta_one = 0.9
beta_two = 0.999
adam_floor = 1e-08
weight_decay = 0.01
rates = (0.5, 0.1, 0.1, 0.005)
blocked = -1000000000.0
highest = lax.Precision.HIGHEST
LOGIT_SCALE = D ** (-0.5)
EXP_SCALE = LOGIT_SCALE / math.log(2.0)
UPSCALE = math.sqrt(D / ADAPTER)
GELU_A = math.sqrt(2.0 / math.pi)
GELU_B = 0.044715
VOCAB_TILE = 2048
UPDATE_STEPS = 6
MESH = pl.DeviceIdType.MESH


def adamw(weight, first, second, grad, rate):
    first = beta_one * first + (1.0 - beta_one) * grad
    second = beta_two * second + (1.0 - beta_two) * grad * grad
    corrected = first / (1.0 - beta_one**STEP)
    spread = jnp.sqrt(second / (1.0 - beta_two**STEP)) + adam_floor
    return (weight - rate * (corrected / spread + weight_decay * weight), first, second)


def mm(left, right):
    return lax.dot_general(
        left, right, (((1,), (0,)), ((), ())), preferred_element_type=jnp.float32
    )


def mm_last(left, right):
    return lax.dot_general(
        left, right, (((1,), (1,)), ((), ())), preferred_element_type=jnp.float32
    )


def mm_first(left, right):
    return lax.dot_general(
        left, right, (((0,), (0,)), ((), ())), preferred_element_type=jnp.float32
    )


def exact(left, right, dims):
    return lax.dot_general(
        left, right, (dims, ((), ())), precision=highest, preferred_element_type=jnp.float32
    )


def norm_scale(value):
    return lax.rsqrt(jnp.mean(value * value, axis=-1, keepdims=True) + epsilon)


def normed(value, gain):
    return (value * norm_scale(value) * gain).astype(jnp.bfloat16)


def norm_back(value, gain, grad):
    scale = norm_scale(value)
    weighted = grad * gain
    return scale * weighted - value * (
        scale * scale * scale * jnp.mean(weighted * value, axis=-1, keepdims=True)
    )


def gelu_tanh(value):
    return jnp.tanh(value * (GELU_A + (GELU_A * GELU_B) * (value * value)))


def gelu(value):
    return (0.5 * value) * (1.0 + gelu_tanh(value))


def gelu_slope(value, tanh):
    return 0.5 * (1.0 + tanh) + (0.5 * value) * (1.0 - tanh * tanh) * (
        GELU_A + (3.0 * GELU_A * GELU_B) * (value * value)
    )


def halves():
    lane = lax.broadcasted_iota(jnp.int32, (1, 128), 1)
    return [(lane // 64 == half) for half in range(2)]


def attend(q_ref, kv_ref, k_col, v_col, q_len, k_len, allow, out_ref, probs_ref=None):
    sides = halves()
    masks = [side.astype(jnp.float32).astype(jnp.bfloat16) for side in sides]

    def pair_step(pair, carry):
        lanes = pl.multiple_of(pair * 128, 128)
        for seq in range(SEQ_DEV):
            q_rows = pl.ds(seq * q_len, q_len)
            k_rows = pl.ds(seq * k_len, k_len)
            query = q_ref[q_rows, pl.ds(lanes, 128)]
            keys = kv_ref[k_rows, pl.ds(k_col + lanes, 128)]
            values = kv_ref[k_rows, pl.ds(v_col + lanes, 128)]
            outs = []
            for half in range(2):
                scores = mm_last(query * masks[half], keys) * 0.125
                scores = jnp.where(allow(seq), scores, blocked)
                peak = jnp.max(scores, axis=-1, keepdims=True)
                weights = jnp.exp(scores - peak)
                probs = weights * (1.0 / jnp.sum(weights, axis=-1, keepdims=True))
                if probs_ref is not None:
                    probs_ref[(pair * SEQ_DEV + seq) * 2 + half] = probs
                outs.append(mm(probs.astype(jnp.bfloat16), values))
            out_ref[q_rows, pl.ds(lanes, 128)] = jnp.where(sides[0], outs[0], outs[1]).astype(
                jnp.bfloat16
            )
        return carry

    lax.fori_loop(0, HEADS // 2, pair_step, 0)


def attend_back(grad_ref, q_ref, kv_ref, probs_ref, q_len, k_len, joined_ref):
    sides = halves()
    masks = [side.astype(jnp.float32).astype(jnp.bfloat16) for side in sides]

    def pair_step(pair, carry):
        lanes = pl.multiple_of(pair * 128, 128)
        for seq in range(SEQ_DEV):
            q_rows = pl.ds(seq * q_len, q_len)
            k_rows = pl.ds(seq * k_len, k_len)
            grad = grad_ref[q_rows, pl.ds(lanes, 128)]
            query = q_ref[q_rows, pl.ds(lanes, 128)]
            values = kv_ref[k_rows, pl.ds(D + lanes, 128)]
            key_grads, value_grads = [], []
            for half in range(2):
                probs = probs_ref[(pair * SEQ_DEV + seq) * 2 + half]
                grad_probs = mm_last(grad * masks[half], values)
                value_grads.append(mm_first(probs.astype(jnp.bfloat16), grad))
                inner = jnp.sum(grad_probs * probs, axis=-1, keepdims=True)
                grad_scores = (probs * (grad_probs - inner)).astype(jnp.bfloat16)
                key_grads.append(mm_first(grad_scores, query))
            joined_ref[k_rows, pl.ds(lanes, 128)] = (
                jnp.where(sides[0], key_grads[0], key_grads[1]) * 0.125
            ).astype(jnp.bfloat16)
            joined_ref[k_rows, pl.ds(D + lanes, 128)] = jnp.where(
                sides[0], value_grads[0], value_grads[1]
            ).astype(jnp.bfloat16)
        return carry

    lax.fori_loop(0, HEADS // 2, pair_step, 0)


def feed(state_ref, gain, inner_ref, outer_ref, act_ref, slope_ref, down_ref, up_ref, length,
         plain_ref, low_ref, after_ref):
    rows = SEQ_DEV * length
    act_rows = pl.ds(0, rows)
    source = normed(state_ref[...], gain)
    for block in range(FF // D):
        columns = slice(block * D, (block + 1) * D)
        hidden = mm(source, inner_ref[:, columns])
        tanh = gelu_tanh(hidden)
        act_ref[act_rows, columns] = ((0.5 * hidden) * (1.0 + tanh)).astype(jnp.bfloat16)
        if slope_ref is not None:
            slope_ref[:, columns] = gelu_slope(hidden, tanh)
    branch = mm(act_ref[act_rows, :], outer_ref[...])
    plain_ref[...] = branch.astype(jnp.bfloat16)
    for seq in range(SEQ_DEV):
        span = slice(seq * length, (seq + 1) * length)
        lowered = mm(plain_ref[span, :], down_ref[seq])
        low_ref[span, :] = lowered
        adapted = mm(gelu(lowered).astype(jnp.bfloat16), up_ref[seq]) * UPSCALE
        after_ref[span, :] = state_ref[span, :] + branch[span, :] + adapted


def adapter_back(grad_ref, low_ref, plain_ref, down_ref, up_ref, length, grad_down_ref,
                 grad_up_ref, branch_ref=None):
    for seq in range(SEQ_DEV):
        span = slice(seq * length, (seq + 1) * length)
        grad = grad_ref[span, :]
        grad_low = grad.astype(jnp.bfloat16)
        lowered = low_ref[span, :]
        tanh = gelu_tanh(lowered)
        bottleneck = ((0.5 * lowered) * (1.0 + tanh)).astype(jnp.bfloat16)
        grad_bottle = mm_last(grad_low, up_ref[seq]) * UPSCALE
        grad_up_ref[seq] = mm_first(bottleneck, grad_low)[:ADAPTER] * UPSCALE
        grad_lowered = (grad_bottle * gelu_slope(lowered, tanh)).astype(jnp.bfloat16)
        grad_down_ref[seq] = mm_first(plain_ref[span, :], grad_lowered)
        if branch_ref is not None:
            branch_ref[span, :] = (grad + mm_last(grad_lowered, down_ref[seq])).astype(
                jnp.bfloat16
            )


def pair_rows(embeds):
    return jnp.concatenate(
        [
            embeds[task : task + 1, :] + embeds[TASKS + layer : TASKS + layer + 1, :]
            for task in range(TASKS)
            for layer in range(LAYERS)
        ],
        axis=0,
    )


def prep_kernel(
    task_ref,
    len_ref,
    count_ref,
    src_ref,
    tgt_ref,
    embeds_ref,
    one_ref,
    two_ref,
    hyper_ref,
    table_hbm,
    rows_ref,
    adapters_ref,
    info_ref,
    sel_ref,
    coded_ref,
    crowded_ref,
    table,
    wide,
    generated,
    index_vmem,
    index,
    picked,
    load_sem,
    index_sem,
):
    member = lax.axis_index("gen")
    part = table.shape[0]
    offset = member * part
    cuts = [0, 2048, 4096, 6144, part]
    loads = [
        pltpu.make_async_copy(
            table_hbm.at[pl.ds(cuts[i], cuts[i + 1] - cuts[i])],
            table.at[pl.ds(cuts[i], cuts[i + 1] - cuts[i])],
            load_sem.at[i],
        )
        for i in range(4)
    ]
    for load in loads:
        load.start()

    wide_tokens = SEQ_DEV * SRC
    order = lax.broadcasted_iota(jnp.int32, (wide_tokens, wide_tokens), 0)
    upto = (
        (order <= lax.broadcasted_iota(jnp.int32, (wide_tokens, wide_tokens), 1))
        .astype(jnp.float32)
        .astype(jnp.bfloat16)
    )
    own_first = member * SEQ_DEV
    crowded = jnp.zeros((), jnp.int32)
    slots = []
    for ids_ref, length, cap, rows, start in (
        (src_ref, SRC, SRC_CAP, SRC_CAP, 0),
        (tgt_ref, TGT, TGT_CAP, TGT_ROWS, SRC_CAP),
    ):
        count = SEQ_DEV * length
        ids = jnp.concatenate(
            [
                jnp.concatenate(
                    [ids_ref[SEQ_DEV * t + s : SEQ_DEV * t + s + 1, :] for s in range(SEQ_DEV)],
                    axis=1,
                )
                for t in range(GEN)
            ],
            axis=0,
        )
        own = jnp.concatenate([ids_ref[pl.ds(own_first + s, 1), :] for s in range(SEQ_DEV)], axis=1)
        local = ids - offset
        inside = ((local >= 0) & (local < part)).astype(jnp.float32)
        held = [
            ((own >= part * o) & (own < part * (o + 1))).astype(jnp.float32) for o in range(GEN)
        ]
        marks = jnp.concatenate([inside] + held, axis=0)
        ranks = mm(marks.astype(jnp.bfloat16), upto[:count, :count]) - 1.0
        most = jnp.zeros((GEN, 1), jnp.float32)
        for o in range(GEN):
            amount = ((ids >= part * o) & (ids < part * (o + 1))).astype(jnp.float32)
            most = jnp.maximum(most, jnp.sum(amount, axis=1, keepdims=True))
        crowded = crowded + (jnp.max(most) > float(cap)).astype(jnp.int32)
        for t in range(GEN):
            place = jnp.where(inside[t : t + 1] > 0.0, ranks[t : t + 1], -1.0)
            spot = lax.broadcasted_iota(jnp.int32, (rows, count), 0).astype(jnp.float32)
            chosen = (spot == place).astype(jnp.float32).astype(jnp.bfloat16)
            token = local[t : t + 1]
            digits = jnp.concatenate(
                [
                    lax.shift_right_logical(token, 6).astype(jnp.float32) * inside[t : t + 1],
                    lax.bitwise_and(token, 63).astype(jnp.float32) * inside[t : t + 1],
                    jnp.zeros((6, count), jnp.float32),
                ],
                axis=0,
            ).astype(jnp.bfloat16)
            found = mm_last(digits, chosen)
            index_vmem[t : t + 1, start : start + rows] = (
                found[0:1] * 64.0 + found[1:2]
            ).astype(jnp.int32)
        slot = jnp.zeros((1, count), jnp.float32)
        for o in range(GEN):
            slot = slot + held[o] * (ranks[GEN + o : GEN + o + 1] + float(o * rows))
        slots.append(slot)
    index_copy = pltpu.make_async_copy(index_vmem, index, index_sem)
    index_copy.start()

    use_fast = jnp.where(crowded == 0, 1.0, 0.0)
    lane = lax.broadcasted_iota(jnp.int32, (1, SEQ_DEV * TGT), 1)
    shifted = jnp.where(
        lax.rem(lane, TGT) == 0, float(TGT_CAP), pltpu.roll(slots[1], 1, axis=1)
    )
    position = lax.broadcasted_iota(jnp.int32, (1, SRC), 1)
    allow = jnp.concatenate(
        [
            (position < len_ref[task_ref[own_first + s]]).astype(jnp.float32)
            for s in range(SEQ_DEV)
        ],
        axis=1,
    )
    place = lax.broadcasted_iota(jnp.int32, (1, TGT), 1)
    valid = jnp.concatenate(
        [(place < count_ref[own_first + s]).astype(jnp.float32) for s in range(SEQ_DEV)], axis=1
    )
    tokens = jnp.zeros((1, SEQ_DEV * TGT), jnp.float32) + sum(
        count_ref[own_first + s] for s in range(SEQ_DEV)
    ).astype(jnp.float32)

    def switch(slot):
        return jnp.where(use_fast > 0.0, slot, -1.0)

    info_ref[...] = jnp.concatenate(
        [
            switch(slots[0]),
            jnp.concatenate([switch(shifted), switch(slots[1])], axis=1),
            allow,
            jnp.concatenate([valid, tokens], axis=1),
            jnp.zeros((4, wide_tokens), jnp.float32),
        ],
        axis=0,
    )
    crowded_ref[0] = crowded

    coded = exact(
        gelu(exact(pair_rows(embeds_ref[...]), one_ref[...], ((1,), (0,)))),
        two_ref[...],
        ((1,), (0,)),
    )
    coded_ref[...] = coded
    flat = exact(coded, hyper_ref[...], ((1,), (0,)))
    pairs = TASKS * LAYERS
    for tile in range(FLAT):
        generated[pl.ds(tile, pairs, stride=FLAT), :] = flat[:, 128 * tile : 128 * (tile + 1)]
    selector = jnp.zeros((pairs, 128), jnp.float32)
    row_of = lax.broadcasted_iota(jnp.int32, (pairs, 128), 0)
    column_of = lax.broadcasted_iota(jnp.int32, (pairs, 128), 1)
    sequences = GEN * SEQ_DEV
    for seq in range(sequences):
        for layer in range(LAYERS):
            pair = task_ref[seq] * LAYERS + layer
            begin = ((seq % SEQ_DEV) * LAYERS + layer) * FLAT
            adapters_ref[seq // SEQ_DEV, begin : begin + FLAT, :] = generated[
                pl.ds(pl.multiple_of(pair * FLAT, 8), FLAT), :
            ].astype(jnp.bfloat16)
            selector = jnp.where(
                (row_of == pair) & (column_of == layer * sequences + seq), 1.0, selector
            )
    sel_ref[...] = selector

    chunk = 32
    for i in range(4):
        loads[i].wait()

        def widen(step, carry):
            begin = pl.multiple_of(cuts[i] + step * chunk, chunk)
            wide[pl.ds(begin, chunk), :] = table[pl.ds(begin, chunk), :].astype(jnp.float32)
            return carry

        lax.fori_loop(0, (cuts[i + 1] - cuts[i]) // chunk, widen, 0)
    index_copy.wait()
    for t in range(GEN):

        def fetch(step, carry):
            begin = pl.multiple_of(step * 16, 16)
            for k in range(16):
                picked[pl.ds(begin + k, 1), :] = wide[pl.ds(index[t, begin + k], 1), :]
            return carry

        lax.fori_loop(0, (SRC_CAP + TGT_ROWS) // 16, fetch, 0)
        rows_ref[t] = picked[...].astype(jnp.bfloat16)


def prep(task_ids, task_len, tgt_count, src_ids, tgt_ids, embeds, one, two, hyper, table):
    vmem = pl.BlockSpec(memory_space=pltpu.VMEM)
    smem = pl.BlockSpec(memory_space=pltpu.SMEM)
    whole = pl.BlockSpec(memory_space=pl.ANY)
    low, full = jnp.bfloat16, jnp.float32
    rows = SRC_CAP + TGT_ROWS
    pairs = TASKS * LAYERS
    return pl.pallas_call(
        prep_kernel,
        out_shape=(
            jax.ShapeDtypeStruct((GEN, rows, D), low),
            jax.ShapeDtypeStruct((GEN, SEQ_DEV * LAYERS * FLAT, 128), low),
            jax.ShapeDtypeStruct((8, SEQ_DEV * SRC), full),
            jax.ShapeDtypeStruct((pairs, 128), full),
            jax.ShapeDtypeStruct((pairs, two.shape[1]), full),
            jax.ShapeDtypeStruct((1,), jnp.int32),
        ),
        in_specs=[smem] * 3 + [vmem] * 6 + [whole],
        out_specs=(vmem, vmem, vmem, vmem, vmem, smem),
        scratch_shapes=[
            pltpu.VMEM(table.shape, low),
            pltpu.VMEM(table.shape, full),
            pltpu.VMEM((pairs * FLAT, 128), full),
            pltpu.VMEM((8, 384), jnp.int32),
            pltpu.SMEM((8, 384), jnp.int32),
            pltpu.VMEM((rows, D), full),
            pltpu.SemaphoreType.DMA((4,)),
            pltpu.SemaphoreType.DMA,
        ],
        compiler_params=pltpu.CompilerParams(vmem_limit_bytes=60 * 1024 * 1024),
        name="prepare",
    )(task_ids, task_len, tgt_count, src_ids, tgt_ids, embeds, one, two, hyper, table)


def crowded_kernel(rows_ref, out_ref, incoming, send_sem, recv_sem):
    member = lax.axis_index("gen")
    barrier = pltpu.get_barrier_semaphore()
    for step in range(1, GEN):
        pl.semaphore_signal(
            barrier, inc=1, device_id={"gen": lax.rem(member + step, GEN)}, device_id_type=MESH
        )
    pl.semaphore_wait(barrier, GEN - 1)
    copies = []
    for step in range(1, GEN):
        target = lax.rem(member + step, GEN)
        copies.append(
            pltpu.make_async_remote_copy(
                src_ref=rows_ref.at[target],
                dst_ref=incoming.at[step],
                send_sem=send_sem.at[step],
                recv_sem=recv_sem.at[step],
                device_id={"gen": target},
                device_id_type=MESH,
            )
        )
        copies[-1].start()
    total = rows_ref[member].astype(jnp.float32)
    for step in range(1, GEN):
        copies[step - 1].wait()
        total = total + incoming[step].astype(jnp.float32)
    out_ref[...] = total.astype(jnp.bfloat16)


def crowded_rows(src_ids, tgt_ids, table):
    member = lax.axis_index("gen")
    inputs = jnp.concatenate([jnp.zeros_like(tgt_ids[:, :1]), tgt_ids[:, :-1]], axis=1)
    tokens = jnp.concatenate(
        [
            ids.reshape(GEN, -1)
            for ids in (src_ids, inputs, tgt_ids)
        ],
        axis=1,
    )
    token = tokens - member * table.shape[0]
    inside = (token >= 0) & (token < table.shape[0])
    rows = jnp.take(table, jnp.clip(token, 0, table.shape[0] - 1).reshape(-1), axis=0)
    rows = jnp.where(inside.reshape(-1, 1), rows, jnp.zeros_like(rows)).reshape(
        GEN, tokens.shape[1], -1
    )
    vmem = pl.BlockSpec(memory_space=pltpu.VMEM)
    return pl.pallas_call(
        crowded_kernel,
        out_shape=jax.ShapeDtypeStruct(rows.shape[1:], jnp.bfloat16),
        in_specs=[vmem],
        out_specs=vmem,
        scratch_shapes=[
            pltpu.VMEM(rows.shape, jnp.bfloat16),
            pltpu.SemaphoreType.DMA((GEN,)),
            pltpu.SemaphoreType.DMA((GEN,)),
        ],
        compiler_params=pltpu.CompilerParams(
            collective_id=2, has_side_effects=True, vmem_limit_bytes=40 * 1024 * 1024
        ),
        name="crowded_rows",
    )(rows)


def step_kernel(
    adapters_ref,
    info_ref,
    sel_ref,
    coded_ref,
    gains_ref,
    rows_hbm,
    slow_hbm,
    hyper_hbm,
    attn_hbm,
    inner_hbm,
    outer_hbm,
    table_hbm,
    out_ref,
    small_ref,
    attn,
    inner,
    outer,
    table,
    state,
    after_e,
    plain_e,
    low_e,
    qkv,
    mixed,
    act,
    memory,
    y1,
    y2,
    y3,
    q_cross,
    kv_cross,
    probs,
    slope,
    plain_d,
    low_d,
    feats,
    total,
    results,
    arrived,
    stats,
    stats_in,
    grad,
    grad_low,
    joined,
    src_in,
    tgt_in,
    adapters_in,
    slow,
    flat_in,
    spread,
    down_ref,
    up_ref,
    grad_down_ref,
    grad_up_ref,
    wanted,
    pack,
    grads_in,
    hyper,
    outgoing,
    incoming,
    shares,
    outgoing_small,
    incoming_small,
    load_sem,
    row_send,
    src_recv,
    tgt_recv,
    adapter_recv,
    grad_send,
    grad_recv,
    scatter_sem,
    share_sem,
    small_send,
    small_recv,
    feat_send,
    feat_recv,
    result_send,
    result_recv,
    stat_send,
    stat_recv,
):
    member = lax.axis_index("gen")
    barrier = pltpu.get_barrier_semaphore()

    def peer(order):
        chip = lax.rem(member // 2 + lax.rem((order + 1) // 2, 2), 2)
        return chip * 2 + lax.rem(lax.rem(member, 2) + order // 2, 2)

    rank = lax.axis_index("dp")
    count = outgoing.shape[0]
    width = shares.shape[2]
    per_half = out_ref.shape[1] // width
    for order in range(1, GEN):
        pl.semaphore_signal(
            barrier, inc=1, device_id={"gen": peer(order)}, device_id_type=MESH
        )

    def greet(step, carry):
        pl.semaphore_signal(
            barrier, inc=1, device_id={"dp": lax.rem(rank + step, count)}, device_id_type=MESH
        )
        return carry

    lax.fori_loop(1, count, greet, 0)

    loads = []
    for source, target in (
        (attn_hbm.at[0], attn.at[0]),
        (inner_hbm.at[0], inner.at[0]),
        (outer_hbm.at[0], outer.at[0]),
        (attn_hbm.at[1], attn.at[1]),
        (attn_hbm.at[2], attn.at[2]),
        (inner_hbm.at[1], inner.at[1]),
        (outer_hbm.at[1], outer.at[1]),
        (table_hbm, table),
        (slow_hbm, slow),
        (hyper_hbm, hyper),
    ):
        loads.append(pltpu.make_async_copy(source, target, load_sem.at[len(loads)]))
        loads[-1].start()

    pl.semaphore_wait(barrier, GEN + count - 2)

    def source_copy(owner, target):
        return pltpu.make_async_remote_copy(
            src_ref=rows_hbm.at[target, pl.ds(0, SRC_CAP)],
            dst_ref=src_in.at[owner],
            send_sem=row_send.at[0, target],
            recv_sem=src_recv.at[owner],
            device_id={"gen": target},
            device_id_type=MESH,
        )

    def target_copy(owner, target):
        return pltpu.make_async_remote_copy(
            src_ref=rows_hbm.at[target, pl.ds(SRC_CAP, TGT_ROWS)],
            dst_ref=tgt_in.at[owner],
            send_sem=row_send.at[1, target],
            recv_sem=tgt_recv.at[owner],
            device_id={"gen": target},
            device_id_type=MESH,
        )

    def adapter_copy(owner, target):
        return pltpu.make_async_remote_copy(
            src_ref=adapters_ref.at[target],
            dst_ref=adapters_in.at[owner],
            send_sem=row_send.at[2, target],
            recv_sem=adapter_recv.at[owner],
            device_id={"gen": target},
            device_id_type=MESH,
        )

    for order in range(1, GEN):
        source_copy(member, peer(order)).start()
    for order in range(1, GEN):
        adapter_copy(member, peer(order)).start()
    for order in range(1, GEN):
        target_copy(member, peer(order)).start()
    own_source = pltpu.make_async_copy(
        rows_hbm.at[member, pl.ds(0, SRC_CAP)], src_in.at[member], src_recv.at[member]
    )
    own_source.start()
    own_target = pltpu.make_async_copy(
        rows_hbm.at[member, pl.ds(SRC_CAP, TGT_ROWS)], tgt_in.at[member], tgt_recv.at[member]
    )
    own_target.start()
    adapters_in[member] = adapters_ref[member]

    def spread_rows(row, lanes, incoming_rows, owner):
        height = incoming_rows.shape[1]
        spot = lax.broadcasted_iota(jnp.int32, (height, lanes.stop - lanes.start), 0)
        spot = (spot + owner * height).astype(jnp.float32)
        chosen = (spot == info_ref[row : row + 1, lanes]).astype(jnp.float32)
        return mm_first(chosen.astype(jnp.bfloat16), incoming_rows[owner])

    sources = SEQ_DEV * SRC
    targets = SEQ_DEV * TGT
    own = pl.ds(0, targets)
    loads[8].wait()
    own_source.wait()
    after_e[...] = slow[0:sources, :].astype(jnp.float32) + spread_rows(
        0, slice(0, sources), src_in, member
    )
    for order in (3, 1, 2):
        source_copy(peer(order), peer(order)).wait_recv()
        after_e[...] = after_e[...] + spread_rows(0, slice(0, sources), src_in, peer(order))
    embedded = after_e[...]

    def allowed(seq):
        return info_ref[2:3, seq * SRC : (seq + 1) * SRC] > 0.0

    entry = normed(embedded, gains_ref[0:1])
    loads[0].wait()
    for block in range(3):
        columns = slice(block * D, (block + 1) * D)
        qkv[:, columns] = mm(entry, attn[0, :, columns]).astype(jnp.bfloat16)
    attend(qkv, qkv, D, 2 * D, SRC, SRC, allowed, mixed)
    state[...] = embedded + mm(mixed[...], attn[0, :, 3 * D :])
    loads[1].wait()
    loads[2].wait()
    for order in range(1, GEN):
        adapter_copy(peer(order), peer(order)).wait_recv()
    unpack_adapters(adapters_in, flat_in, spread, down_ref, up_ref)
    feed(state, gains_ref[1:2], inner.at[0], outer.at[0], act, None, down_ref.at[0], up_ref.at[0],
         SRC, plain_e, low_e, after_e)
    memory[...] = normed(after_e[...], gains_ref[2:3])

    own_target.wait()
    for order in range(1, GEN):
        target_copy(peer(order), peer(order)).wait_recv()
    inputs = slow[sources : sources + targets, :].astype(jnp.float32)
    wanted[...] = slow[sources + targets : sources + 2 * targets, :].astype(jnp.float32)
    for owner in range(GEN):
        inputs = inputs + spread_rows(1, slice(0, targets), tgt_in, owner)
        wanted[...] = wanted[...] + spread_rows(1, slice(targets, 2 * targets), tgt_in, owner)
    entry = normed(inputs, gains_ref[3:4])
    loads[3].wait()
    for block in range(3):
        columns = slice(block * D, (block + 1) * D)
        qkv[own, columns] = mm(entry, attn[1, :, columns]).astype(jnp.bfloat16)
    causal = lax.broadcasted_iota(jnp.int32, (TGT, TGT), 0) >= lax.broadcasted_iota(
        jnp.int32, (TGT, TGT), 1
    )
    attend(qkv, qkv, D, 2 * D, TGT, TGT, lambda seq: causal, mixed)
    y1[...] = inputs + mm(mixed[own, :], attn[1, :, 3 * D :])
    loads[4].wait()
    q_cross[...] = mm(normed(y1[...], gains_ref[4:5]), attn[2, :, :D]).astype(jnp.bfloat16)
    for block in range(2):
        columns = slice(block * D, (block + 1) * D)
        kv_cross[:, columns] = mm(
            memory[...], attn[2, :, (block + 1) * D : (block + 2) * D]
        ).astype(jnp.bfloat16)
    attend(q_cross, kv_cross, 0, D, TGT, SRC, allowed,
           mixed, probs)
    y2[...] = y1[...] + mm(mixed[own, :], attn[2, :, 3 * D :])
    loads[5].wait()
    loads[6].wait()
    feed(y2, gains_ref[5:6], inner.at[1], outer.at[1], act, slope, down_ref.at[1], up_ref.at[1],
         TGT, plain_d, low_d, y3)
    feats[0] = normed(y3[...], gains_ref[6:7])


    def feature_copy(order):
        return pltpu.make_async_remote_copy(
            src_ref=feats.at[0],
            dst_ref=feats.at[order],
            send_sem=feat_send.at[order],
            recv_sem=feat_recv.at[order],
            device_id={"gen": peer(order)},
            device_id_type=MESH,
        )

    def result_copy(order):
        return pltpu.make_async_remote_copy(
            src_ref=results.at[order],
            dst_ref=arrived.at[order],
            send_sem=result_send.at[order],
            recv_sem=result_recv.at[order],
            device_id={"gen": peer(order)},
            device_id_type=MESH,
        )

    def stat_copy(order):
        return pltpu.make_async_remote_copy(
            src_ref=stats.at[order],
            dst_ref=stats_in.at[order],
            send_sem=stat_send.at[order],
            recv_sem=stat_recv.at[order],
            device_id={"gen": peer(order)},
            device_id_type=MESH,
        )

    for order in range(1, GEN):
        feature_copy(order).start()
    loads[7].wait()
    same = lax.broadcasted_iota(jnp.int32, (targets, targets), 0) == lax.broadcasted_iota(
        jnp.int32, (targets, targets), 1
    )

    def as_row(column):
        return jnp.sum(jnp.where(same, column, 0.0), axis=0, keepdims=True)

    def as_column(row):
        return jnp.sum(jnp.where(same, row, 0.0), axis=1, keepdims=True)

    def block_step(order, carry):
        @pl.when(order > 0)
        def _():
            feature_copy(order).wait_recv()

        query = feats[order]
        ends = list(range(0, table.shape[0], VOCAB_TILE)) + [table.shape[0]]
        tiles = [(ends[i], ends[i + 1]) for i in range(len(ends) - 1)]
        peak = scale = None
        scores = mm_last(query, table[tiles[0][0] : tiles[0][1], :])
        for index, (first, last) in enumerate(tiles):
            following = None
            if index + 1 < len(tiles):
                following = mm_last(query, table[tiles[index + 1][0] : tiles[index + 1][1], :])
            top = jnp.max(scores, axis=-1, keepdims=True)
            if index > 0:
                top = jnp.maximum(peak, top)
            weights = jnp.exp2((scores - top) * EXP_SCALE)
            amount = jnp.sum(weights, axis=-1, keepdims=True)
            part = mm(weights.astype(jnp.bfloat16), table[first:last, :])
            if index == 0:
                total[...] = part
                scale = amount
            else:
                shrink = jnp.exp2((peak - top) * EXP_SCALE)
                total[...] = total[...] * shrink + part
                scale = scale * shrink + amount
            peak, scores = top, following
        results[order] = total[...].astype(jnp.bfloat16)
        stats[order] = jnp.concatenate(
            [as_row(peak), as_row(scale), jnp.zeros((6, targets), jnp.float32)], axis=0
        )

        @pl.when(order > 0)
        def _():
            result_copy(order).start()
            stat_copy(order).start()

        return carry

    lax.fori_loop(0, GEN, block_step, 0)
    stats_in[0] = stats[0]
    for order in range(1, GEN):
        stat_copy(order).wait_recv()
    peaks = [as_column(stats_in[order, 0:1, :]) for order in range(GEN)]
    sums = [as_column(stats_in[order, 1:2, :]) for order in range(GEN)]
    top = jnp.maximum(jnp.maximum(peaks[0], peaks[1]), jnp.maximum(peaks[2], peaks[3]))
    parts = [jnp.exp2((peaks[order] - top) * EXP_SCALE) for order in range(GEN)]
    amount = sum(parts[order] * sums[order] for order in range(GEN))
    logsum = top * LOGIT_SCALE + jnp.log(amount)
    inverse = 1.0 / amount
    total[...] = results[0].astype(jnp.float32) * (parts[0] * inverse)
    for order in range(1, GEN):
        result_copy(order).wait_recv()
        total[...] = total[...] + arrived[order].astype(jnp.float32) * (parts[order] * inverse)
    picked = (
        jnp.sum(feats[0].astype(jnp.float32) * wanted[...], axis=-1, keepdims=True) * LOGIT_SCALE
    )
    counted = as_column(info_ref[3:4, 0:targets])
    loss = jnp.sum((logsum - picked) * counted, axis=0, keepdims=True)
    lane = lax.broadcasted_iota(jnp.int32, (8, 128), 1)
    totals = jnp.where(
        lane == 0, loss, jnp.where(lane == 1, info_ref[3:4, targets : targets + 128], 0.0)
    )

    grad[own, :] = norm_back(
        y3[...], gains_ref[6:7], (total[...] - wanted[...]) * (counted * LOGIT_SCALE)
    )
    adapter_back(grad.at[own], low_d, plain_d, down_ref.at[1], up_ref.at[1], TGT,
                 grad_down_ref.at[1], grad_up_ref.at[1], grad_low)

    def grad_copy(layer, owner, target):
        part = SEQ_DEV * FLAT
        begin = pl.multiple_of((layer * GEN + owner) * part, 8)
        return pltpu.make_async_remote_copy(
            src_ref=pack.at[layer, target],
            dst_ref=grads_in.at[pl.ds(begin, part)],
            send_sem=grad_send.at[layer, target],
            recv_sem=grad_recv.at[layer, owner],
            device_id={"gen": target},
            device_id_type=MESH,
        )

    def send_grads(layer):
        pack_grads(grad_down_ref.at[layer], grad_up_ref.at[layer], pack.at[layer])
        for order in range(1, GEN):
            grad_copy(layer, member, peer(order)).start()
        begin = pl.multiple_of((layer * GEN + member) * SEQ_DEV * FLAT, 8)
        grads_in[pl.ds(begin, SEQ_DEV * FLAT), :] = pack[layer, member]

    send_grads(1)
    for block in range(FF // D):
        columns = slice(block * D, (block + 1) * D)
        act[own, columns] = (
            mm_last(grad_low[...], outer[1, columns, :]) * slope[:, columns]
        ).astype(jnp.bfloat16)
    grad_entry = mm_last(act[own, :], inner[1])
    grad_state = grad[own, :] + norm_back(y2[...], gains_ref[5:6], grad_entry)
    mixed[own, :] = mm_last(grad_state.astype(jnp.bfloat16), attn[2, :, 3 * D :]).astype(
        jnp.bfloat16
    )
    attend_back(mixed, q_cross, kv_cross, probs, TGT, SRC, joined)
    grad_memory = mm_last(joined[...], attn[2, :, D : 3 * D])

    grad[...] = norm_back(after_e[...], gains_ref[2:3], grad_memory)
    adapter_back(grad, low_e, plain_e, down_ref.at[0], up_ref.at[0], SRC,
                 grad_down_ref.at[0], grad_up_ref.at[0])
    send_grads(0)
    for layer in range(LAYERS):
        for order in range(1, GEN):
            grad_copy(layer, peer(order), peer(order)).wait_recv()
    pairs = TASKS * LAYERS
    received = jnp.concatenate(
        [grads_in[pl.ds(tile, pairs, stride=FLAT), :] for tile in range(FLAT)], axis=1
    )
    slots = exact(sel_ref[:, 0:pairs], received, ((1,), (0,)))

    for piece in range(count):
        row, column = piece // per_half * 8, piece % per_half * width
        outgoing[piece, :, :width] = slots[row : row + 8, column : column + width]
        outgoing[piece, :, width:] = totals

    def scatter(step, carry):
        target = lax.rem(rank + step, count)
        pltpu.make_async_remote_copy(
            src_ref=outgoing.at[target],
            dst_ref=incoming.at[rank],
            send_sem=scatter_sem.at[0],
            recv_sem=scatter_sem.at[1],
            device_id={"dp": target},
            device_id_type=MESH,
        ).start()
        return carry

    def share(step, carry):
        pltpu.make_async_remote_copy(
            src_ref=shares.at[rank],
            dst_ref=shares.at[rank],
            send_sem=share_sem.at[0],
            recv_sem=share_sem.at[1],
            device_id={"dp": lax.rem(rank + step, count)},
            device_id_type=MESH,
        ).start()
        return carry

    def wait_all(ref, sem):
        others = ref.at[pl.ds(0, count - 1)]
        pltpu.make_async_copy(others, others, sem).wait()

    lax.fori_loop(1, count, scatter, 0)
    incoming[rank] = outgoing[rank]
    wait_all(incoming, scatter_sem.at[1])
    summed = incoming[0]
    for source in range(1, count):
        summed = summed + incoming[source]
    shares[rank] = summed[:, :width]
    lax.fori_loop(1, count, share, 0)
    wait_all(shares, share_sem.at[1])
    for piece in range(count):
        row, column = piece // per_half * 8, piece % per_half * width
        out_ref[row : row + 8, column : column + width] = shares[piece]

    loads[9].wait()
    slots = out_ref[...]
    coded_part = exact(slots, hyper[...], ((1,), (1,)))
    hyper_grad = exact(coded_ref[...], slots, ((0,), (0,)))
    square = jnp.sum(hyper_grad * hyper_grad, axis=0, keepdims=True)
    outgoing_small[0:16, :] = jnp.concatenate(
        [coded_part, jnp.zeros((16, 64), jnp.float32)], axis=1
    )
    outgoing_small[16:24, :] = jnp.broadcast_to(
        jnp.sum(square, axis=1, keepdims=True), (8, 128)
    )
    outgoing_small[24:32, :] = summed[:, width:]
    copies = [
        pltpu.make_async_remote_copy(
            src_ref=outgoing_small,
            dst_ref=incoming_small.at[member],
            send_sem=small_send.at[step],
            recv_sem=small_recv.at[step],
            device_id={"gen": lax.rem(member + step, GEN)},
            device_id_type=MESH,
        )
        for step in range(1, GEN)
    ]
    for copy in copies:
        copy.start()
    incoming_small[member] = outgoing_small[...]
    for order in range(1, GEN):
        source_copy(member, peer(order)).wait_send()
        adapter_copy(member, peer(order)).wait_send()
        target_copy(member, peer(order)).wait_send()
        feature_copy(order).wait_send()
        result_copy(order).wait_send()
        stat_copy(order).wait_send()
        for layer in range(LAYERS):
            grad_copy(layer, member, peer(order)).wait_send()
    wait_all(outgoing, scatter_sem.at[0])
    wait_all(shares, share_sem.at[0])
    for copy in copies:
        copy.wait()
    small_ref[...] = (incoming_small[0] + incoming_small[1]) + (
        incoming_small[2] + incoming_small[3]
    )


def unpack_adapters(entries, flat, spread, down_ref, up_ref):
    lane = lax.broadcasted_iota(jnp.int32, (1, 128), 1)
    kept = lane < ADAPTER
    run = D // 32
    for owner in range(GEN):
        flat[owner] = entries[owner].astype(jnp.float32)
    up_ref[...] = jnp.zeros(up_ref.shape, jnp.bfloat16)
    for layer in range(LAYERS):
        for seq in range(SEQ_DEV):
            base = (seq * LAYERS + layer) * FLAT
            for owner in range(GEN // 2):
                tiles = [flat[owner, pl.ds(base + j, run, stride=3), :] for j in range(3)]
                for step in range(run):
                    tile, shift = divmod(ADAPTER * step, 128)
                    piece = tiles[tile]
                    if shift:
                        piece = pltpu.roll(piece, 128 - shift, axis=1)
                    if shift + ADAPTER > 128:
                        tail = pltpu.roll(tiles[tile + 1], 128 - shift, axis=1)
                        piece = jnp.where(lane < 128 - shift, piece, tail)
                    spread[pl.ds(owner * (D // 2) + step, run, stride=run), 0:128] = jnp.where(
                        kept, piece, 0.0
                    )
            down_ref[layer, seq] = spread[:, 0:128].astype(jnp.bfloat16)
            halves_up = []
            for owner in range(GEN // 2, GEN):
                halves_up.append(
                    jnp.concatenate(
                        [
                            flat[owner, pl.ds(base + k, ADAPTER // 2, stride=4), :]
                            for k in range(4)
                        ],
                        axis=1,
                    )
                )
            joined = jnp.concatenate(halves_up + [jnp.zeros((8, D), jnp.float32)], axis=0)
            up_ref[layer, seq, 0:32, :] = joined.astype(jnp.bfloat16)


def pack_grads(grad_down, grad_up, pack):
    lane = lax.broadcasted_iota(jnp.int32, (1, 128), 1)
    run = D // 32
    for seq in range(SEQ_DEV):
        base = seq * FLAT
        for owner in range(GEN // 2):
            tiles = [jnp.zeros((run, 128), jnp.float32) for _ in range(3)]
            for step in range(run):
                tile, shift = divmod(ADAPTER * step, 128)
                piece = grad_down[seq, pl.ds(owner * (D // 2) + step, run, stride=run), :]
                if shift:
                    piece = pltpu.roll(piece, shift, axis=1)
                if shift + ADAPTER > 128:
                    tiles[tile] = tiles[tile] + jnp.where(lane >= shift, piece, 0.0)
                    tiles[tile + 1] = tiles[tile + 1] + jnp.where(lane < shift, piece, 0.0)
                else:
                    tiles[tile] = tiles[tile] + piece
            for j in range(3):
                pack[owner, pl.ds(base + j, run, stride=3), :] = tiles[j]
        for half in range(GEN // 2):
            rows = slice(half * (ADAPTER // 2), (half + 1) * (ADAPTER // 2))
            for k in range(4):
                pack[GEN // 2 + half, pl.ds(base + k, ADAPTER // 2, stride=4), :] = grad_up[
                    seq, rows, 128 * k : 128 * (k + 1)
                ]


def step(adapters, info, sel, coded, gains, rows, slow, hyper, attn_w, ffn_in, ffn_out, table):
    vmem = pl.BlockSpec(memory_space=pltpu.VMEM)
    whole = pl.BlockSpec(memory_space=pl.ANY)
    low, full = jnp.bfloat16, jnp.float32
    sources, targets = SEQ_DEV * SRC, SEQ_DEV * TGT
    pairs = TASKS * LAYERS
    count = lax.axis_size("dp")
    width = pairs * FLAT * 128 // (8 * count)
    dma = pltpu.SemaphoreType.DMA
    return pl.pallas_call(
        step_kernel,
        out_shape=(
            jax.ShapeDtypeStruct((pairs, FLAT * 128), full),
            jax.ShapeDtypeStruct((32, 128), full),
        ),
        in_specs=[vmem] * 5 + [whole] * 7,
        out_specs=(vmem, vmem),
        scratch_shapes=[
            pltpu.VMEM(attn_w.shape, low),
            pltpu.VMEM(ffn_in.shape, low),
            pltpu.VMEM(ffn_out.shape, low),
            pltpu.VMEM(table.shape, low),
            pltpu.VMEM((sources, D), full),
            pltpu.VMEM((sources, D), full),
            pltpu.VMEM((sources, D), low),
            pltpu.VMEM((sources, LOW), full),
            pltpu.VMEM((sources, 3 * D), low),
            pltpu.VMEM((sources, D), low),
            pltpu.VMEM((sources, FF), low),
            pltpu.VMEM((sources, D), low),
            pltpu.VMEM((targets, D), full),
            pltpu.VMEM((targets, D), full),
            pltpu.VMEM((targets, D), full),
            pltpu.VMEM((targets, D), low),
            pltpu.VMEM((sources, 2 * D), low),
            pltpu.VMEM((SEQ_DEV * HEADS, TGT, SRC), full),
            pltpu.VMEM((targets, FF), full),
            pltpu.VMEM((targets, D), low),
            pltpu.VMEM((targets, LOW), full),
            pltpu.VMEM((GEN, targets, D), low),
            pltpu.VMEM((targets, D), full),
            pltpu.VMEM((GEN, targets, D), low),
            pltpu.VMEM((GEN, targets, D), low),
            pltpu.VMEM((GEN, 8, targets), full),
            pltpu.VMEM((GEN, 8, targets), full),
            pltpu.VMEM((sources, D), full),
            pltpu.VMEM((targets, D), low),
            pltpu.VMEM((sources, 2 * D), low),
            pltpu.VMEM((GEN, SRC_CAP, D), low),
            pltpu.VMEM((GEN, TGT_ROWS, D), low),
            pltpu.VMEM((GEN, SEQ_DEV * LAYERS * FLAT, 128), low),
            pltpu.VMEM((sources + 2 * targets, D), low),
            pltpu.VMEM((GEN, SEQ_DEV * LAYERS * FLAT, 128), full),
            pltpu.VMEM((D, 128), full),
            pltpu.VMEM((LAYERS, SEQ_DEV, D, LOW), low),
            pltpu.VMEM((LAYERS, SEQ_DEV, LOW, D), low),
            pltpu.VMEM((LAYERS, SEQ_DEV, D, LOW), full),
            pltpu.VMEM((LAYERS, SEQ_DEV, ADAPTER, D), full),
            pltpu.VMEM((targets, D), full),
            pltpu.VMEM((LAYERS, GEN, SEQ_DEV * FLAT, 128), full),
            pltpu.VMEM((LAYERS * GEN * SEQ_DEV * FLAT, 128), full),
            pltpu.VMEM(hyper.shape, full),
            pltpu.VMEM((count, 8, width + 128), full),
            pltpu.VMEM((count, 8, width + 128), full),
            pltpu.VMEM((count, 8, width), full),
            pltpu.VMEM((32, 128), full),
            pltpu.VMEM((GEN, 32, 128), full),
            dma((10,)),
            dma((3, GEN)),
            dma((GEN,)),
            dma((GEN,)),
            dma((GEN,)),
            dma((LAYERS, GEN)),
            dma((LAYERS, GEN)),
            dma((2,)),
            dma((2,)),
            dma((GEN,)),
            dma((GEN,)),
            dma((GEN,)),
            dma((GEN,)),
            dma((GEN,)),
            dma((GEN,)),
            dma((GEN,)),
            dma((GEN,)),
        ],
        compiler_params=pltpu.CompilerParams(
            collective_id=1, has_side_effects=True, vmem_limit_bytes=62 * 1024 * 1024
        ),
        name="forward_vocab_backward_sum",
    )(adapters, info, sel, coded, gains, rows, slow, hyper, attn_w, ffn_in, ffn_out, table)


def update_kernel(
    slots_ref,
    small_ref,
    coded_ref,
    embeds,
    embeds_m,
    embeds_v,
    one,
    one_m,
    one_v,
    two,
    two_m,
    two_v,
    hyper,
    hyper_m,
    hyper_v,
    loss_ref,
    tokens_ref,
    norm_ref,
    new_embeds,
    new_embeds_m,
    new_embeds_v,
    new_one,
    new_one_m,
    new_one_v,
    new_two,
    new_two_m,
    new_two_v,
    new_hyper,
    new_hyper_m,
    new_hyper_v,
    shared,
):
    @pl.when(pl.program_id(0) == 0)
    def _():
        coded_grad = small_ref[0:16, 0:64]
        tokens = small_ref[24:25, 1:2]
        loss_ref[...] = small_ref[24:25, 0:1]
        tokens_ref[...] = tokens
        pairs = pair_rows(embeds[...])
        before = exact(pairs, one[...], ((1,), (0,)))
        tanh = gelu_tanh(before)
        active = (0.5 * before) * (1.0 + tanh)
        grad_two = exact(active, coded_grad, ((0,), (0,)))
        grad_before = exact(coded_grad, two[...], ((1,), (1,))) * gelu_slope(before, tanh)
        grad_one = exact(pairs, grad_before, ((0,), (0,)))
        grad_pairs = exact(grad_before, one[...], ((1,), (1,)))
        row = lax.broadcasted_iota(jnp.int32, (16, TASKS * LAYERS), 0)
        column = lax.broadcasted_iota(jnp.int32, (16, TASKS * LAYERS), 1)
        chosen = (row == column // LAYERS) & (row < TASKS) | (row == TASKS + column % LAYERS)
        grad_embeds = exact(chosen.astype(jnp.float32), grad_pairs, ((1,), (0,)))
        grad_embeds = grad_embeds[: TASKS + LAYERS]
        scale = 1.0 / tokens
        grads = [grad * scale for grad in (grad_embeds, grad_one, grad_two)]
        square = small_ref[16:17, 0:1] * scale * scale
        for grad in grads:
            square = square + jnp.sum(
                jnp.sum(grad * grad, axis=1, keepdims=True), axis=0, keepdims=True
            )
        norm = jnp.sqrt(square)
        norm_ref[...] = norm
        factor = jnp.minimum(1.0, clip_limit / (norm + 1e-06))
        shared[...] = jnp.broadcast_to(
            jnp.concatenate([scale, factor] + [jnp.zeros((1, 126), jnp.float32)], axis=1), (8, 128)
        )
        for index, (weight, first, second, outs) in enumerate(
            (
                (embeds, embeds_m, embeds_v, (new_embeds, new_embeds_m, new_embeds_v)),
                (one, one_m, one_v, (new_one, new_one_m, new_one_v)),
                (two, two_m, two_v, (new_two, new_two_m, new_two_v)),
            )
        ):
            for out, value in zip(
                outs,
                adamw(weight[...], first[...], second[...], grads[index] * factor, rates[index]),
            ):
                out[...] = value

    scale = shared[0:1, 0:1]
    factor = shared[0:1, 1:2]
    grad = exact(coded_ref[...], slots_ref[...], ((0,), (0,)))
    for out, value in zip(
        (new_hyper, new_hyper_m, new_hyper_v),
        adamw(hyper[...], hyper_m[...], hyper_v[...], (grad * scale) * factor, rates[3]),
    ):
        out[...] = value


def update(slots, small, coded, *weights):
    full = jnp.float32
    width = slots.shape[1]
    block = width // UPDATE_STEPS

    def kept(array):
        return pl.BlockSpec(array.shape, lambda i: (0, 0))

    def cut(array):
        return pl.BlockSpec((array.shape[0], block), lambda i: (0, i))

    one_value = jax.ShapeDtypeStruct((1, 1), full)
    arrays = list(weights)
    return pl.pallas_call(
        update_kernel,
        grid=(UPDATE_STEPS,),
        out_shape=[one_value] * 3 + [jax.ShapeDtypeStruct(w.shape, full) for w in arrays],
        in_specs=[cut(slots), kept(small), kept(coded)]
        + [kept(w) for w in arrays[:9]]
        + [cut(w) for w in arrays[9:]],
        out_specs=[kept(one_value)] * 3
        + [kept(w) for w in arrays[:9]]
        + [cut(w) for w in arrays[9:]],
        scratch_shapes=[pltpu.VMEM((8, 128), full)],
        compiler_params=pltpu.CompilerParams(vmem_limit_bytes=40 * 1024 * 1024),
        name="update",
    )(slots, small, coded, *arrays)


def per_device(
    src_ids,
    tgt_ids,
    task_ids,
    task_len,
    tgt_count,
    table,
    attn_w,
    ffn_in,
    ffn_out,
    gains,
    embeds,
    embeds_m,
    embeds_v,
    proj_one,
    proj_one_m,
    proj_one_v,
    proj_two,
    proj_two_m,
    proj_two_v,
    hyper,
    hyper_m,
    hyper_v,
):
    rows, adapters, info, sel, coded, crowded = prep(
        task_ids, task_len, tgt_count, src_ids, tgt_ids, embeds, proj_one, proj_two, hyper, table
    )
    slow = lax.cond(
        crowded[0] > 0,
        crowded_rows,
        lambda src_ids, tgt_ids, table: jnp.zeros((SEQ_DEV * (SRC + 2 * TGT), D), table.dtype),
        src_ids,
        tgt_ids,
        table,
    )
    slots, small = step(
        adapters, info, sel, coded, gains, rows, slow, hyper, attn_w, ffn_in, ffn_out, table
    )
    weights = (
        embeds, embeds_m, embeds_v,
        proj_one, proj_one_m, proj_one_v,
        proj_two, proj_two_m, proj_two_v,
        hyper, hyper_m, hyper_v,
    )
    loss_sum, token_count, grad_norm, *updated = update(slots, small, coded, *weights)
    return (loss_sum.reshape(()), token_count.reshape(()), grad_norm.reshape(()), *updated)


def solution(mesh):
    return jax.shard_map(
        per_device,
        mesh=mesh,
        in_specs=(
            P("dp", None),
            P("dp", None),
            P("dp"),
            P(),
            P("dp"),
            P("gen", None),
            P(),
            P(),
            P(),
            P(),
            P(),
            P(),
            P(),
            P(),
            P(),
            P(),
            P(),
            P(),
            P(),
            P(None, "gen"),
            P(None, "gen"),
            P(None, "gen"),
        ),
        out_specs=(
            P(),
            P(),
            P(),
            P(),
            P(),
            P(),
            P(),
            P(),
            P(),
            P(),
            P(),
            P(),
            P(None, "gen"),
            P(None, "gen"),
            P(None, "gen"),
        ),
        check_vma=False,
    )
```

time: 204 us -> 140 us (0.69)
  Pallas kernels: 93.6 us -> 129 us
  waiting for transfers between devices: 32.8 us -> 0 us
  between operations: 19.5 us -> 1.51 us
  local copies, waits for them, and re-layouts: 26.9 us -> 9.38 us
  other arithmetic: 11.5 us -> 0 us
  matrix products: 10.6 us -> 0 us
  starting transfers between devices: 8.5 us -> 0 us
    pallas_call x2 -> x3, Pallas kernels: 93.6 us -> 129 us  [the longest x1 109 us: step(): pl.pallas_call(step_kernel, out_shape=(jax.ShapeDtypeStruct((pairs, FLAT...]
    reduce_scatter x1 -> x0, waiting for transfers between devices: 25.2 us -> none  [per_device(): lax.psum_scatter(jnp.where(inside[:, None], rows, jnp.zeros_like(rows)),...]
    gather x1 -> x0, local copies, waits for them, and re-layouts: 14.8 us -> none  [per_device(): rows = jnp.take(table, jnp.clip(token, 0, vocab_part - 1), axis=0)]
    dot_general x10 -> x0, matrix products: 10.6 us -> none  [the longest x1 6.72 us: per_device(): hyper_grad = jnp.dot(coded.T, slots, precision=highest)]
    all_to_all x2 -> x0, starting transfers between devices: 8.46 us -> none  [the longest x1 4.75 us: per_device(): lax.all_to_all(piece, 'gen', split_axis=0, concat_axis=1, tiled=True)]
    unnamed x30 -> x42, local copies, waits for them, and re-layouts: 1.01 us -> 9.3 us
    all_to_all x2 -> x0, waiting for transfers between devices: 7.62 us -> none  [the longest x1 6.15 us: per_device(): lax.all_to_all(grad_rows, 'gen', split_axis=1, concat_axis=0, tiled=True)]
    select_n x4 -> x0, other arithmetic: 5.35 us -> none  [the longest x1 5.29 us: per_device(): jnp.where(inside[:, None], rows, jnp.zeros_like(rows))]
  transfers between devices with their start and end apart: 3 -> 0, of which waited for: 3 -> 0; matrix products, arithmetic and copies ran while one was open for 4% -> 0% of each run, Pallas kernels for 0% -> 0%
where the time goes in v2:
time: 140 us
  Pallas kernels  129 us (92%)
  local copies, waits for them, and re-layouts  9.38 us (7%)
  between operations  1.51 us (1%)
    pallas_call x1, Pallas kernels, step(): pl.pallas_call(step_kernel, out_shape=(jax.ShapeDtypeStruct((pairs, FLAT...  109 us
    pallas_call x1, Pallas kernels, prep(): pl.pallas_call(prep_kernel, out_shape=(jax.ShapeDtypeStruct((GEN, rows, D...  13.2 us
    unnamed x42, local copies, waits for them, and re-layouts  9.3 us
    pallas_call x1, Pallas kernels, update(): pl.pallas_call(update_kernel, grid=(UPDATE_STEPS,), out_shape=[one_value]...  6.32 us

profile of v2, /device:TPU:1, one launch (start us, length us, event | category | flops | bytes accessed | tf_op | source)
XLA Modules:
  0.0 139.6 jit_solution(3709229939924527248)
XLA Ops:
  0.6 1.5 %copy.37.two_ref.two = f32[128,64]{1,0:T(8,128)} copy(f32[128,64]{0,1:T(8,128)} %param.40) | data formatting | bytes 65536 | tf_op args[16]
  2.1 13.2 %prepare.1 = (bf16[4,320,512]{2,1,0:T(8,128)(2,1)}, bf16[4,192,128]{2,1,0:T(8,128)(2,1)}, f32[8,512]{1,0:T(8,128)}, f32[16,128]{1,0:T(8,128)}, f32[16,64]{1,0:T(8,128)}, /*index=5*/s32[1]{0:T(128)}) custom-call(s32[8]{0:T(128)} %task_ref.1, s32[8]{0:T(128)} %len_ref.1, s32[8]{0:T(128)} %count_ref.1, s32[8,256]{1,0:T(8,128)} %src_ref.1, s32[8,128]{1,0:T(8,128)} %tgt_ref.1, ...), custom_call_target="tpu_custom_call" | custom-call | tf_op jit(solution)/shard_map/prepare/pallas_call | solution.py:422
  16.0 0.3 conditional.1
  16.0 0.1 broadcast.95
  16.2 0.0 copy-start.13
  16.3 1.0 copy-done.13
  17.2 0.0 copy-start.5
  17.2 0.0 copy-start.6
  17.3 0.0 copy-start.7
  17.3 0.0 copy-start.8
  17.3 0.0 copy-start.9
  17.3 0.0 copy-start.11
  17.3 0.0 copy-start.12
  17.3 109.1 %forward_vocab_backward_sum.1 = (f32[16,6144]{1,0:T(8,128)}, f32[32,128]{1,0:T(8,128)}) custom-call(bf16[4,192,128]{2,1,0:T(8,128)(2,1)} %get-tuple-element.50.adapters_ref, f32[8,512]{1,0:T(8,128)} %get-tuple-element.51.info_ref, f32[16,128]{1,0:T(8,128)} %get-tuple-element.52.sel_ref, f32[16,64]{1,0:T(8,128)} %get-tuple-element.53.coded_ref, ...), custom_call_target="tpu_custom_call" | custom-call | tf_op jit(solution)/shard_map/forward_vocab_backward_sum/pallas_call | solution.py:1080
  126.4 0.1 copy.39.two_m
  126.5 0.1 copy.40.two_v
  126.7 1.4 %copy-done.1 = f32[64,6144]{1,0:T(8,128)S(1)} copy-done((f32[64,6144]{1,0:T(8,128)S(1)}, f32[64,6144]{1,0:T(8,128)}, u32[]{:S(2)}) %copy-start.1) | copy-done | bytes 1572888
  128.1 1.4 %copy-done.2 = f32[64,6144]{1,0:T(8,128)S(1)} copy-done((f32[64,6144]{1,0:T(8,128)S(1)}, f32[64,6144]{1,0:T(8,128)}, u32[]{:S(2)}) %copy-start.2) | copy-done | bytes 1572888
  129.5 1.0 copy-done.4
  130.5 0.7 copy-done.10
  131.2 6.3 %update.1 = (f32[1,1]{1,0:T(1,128)}, f32[1,1]{1,0:T(1,128)}, f32[1,1]{1,0:T(1,128)}, f32[10,64]{1,0:T(8,128)}, f32[10,64]{1,0:T(8,128)}, /*index=5*/f32[10,64]{1...) custom-call(f32[16,6144]{1,0:T(8,128)S(1)} %copy-done.4, ...), custom_call_target="tpu_custom_call" | custom-call | tf_op jit(solution)/shard_map/update/pallas_call | solution.py:1264
  137.5 0.7 copy.41
  138.2 0.7 copy.42
  138.9 0.7 copy.43
  (23 shorter events, 0.0 us)
Async XLA Ops:
  2.1 13.8 %copy-start.14 = (s32[8,128]{1,0:T(8,128)S(1)}, s32[8,128]{1,0:T(8,128)}, u32[]{:S(2)}) copy-start(s32[8,128]{1,0:T(8,128)} %tgt_ref.1) | copy-start | bytes 12292
  2.1 13.8 %copy-start.15 = (s32[8,256]{1,0:T(8,128)S(1)}, s32[8,256]{1,0:T(8,128)}, u32[]{:S(2)}) copy-start(s32[8,256]{1,0:T(8,128)} %src_ref.1) | copy-start | bytes 24580
  16.2 1.0 copy-start.13
  17.2 109.2 %copy-start.16 = (f32[128,64]{0,1:T(8,128)S(1)}, f32[128,64]{0,1:T(8,128)}, u32[]{:S(2)}) copy-start(f32[128,64]{0,1:T(8,128)} %param.41) | copy-start | bytes 98308
  17.2 109.3 %copy-start.17 = (f32[128,64]{0,1:T(8,128)S(1)}, f32[128,64]{0,1:T(8,128)}, u32[]{:S(2)}) copy-start(f32[128,64]{0,1:T(8,128)} %param.42) | copy-start | bytes 98308
  17.2 109.4 %copy-start = (f32[64,6144]{1,0:T(8,128)S(1)}, f32[64,6144]{1,0:T(8,128)}, u32[]{:S(2)}) copy-start(f32[64,6144]{1,0:T(8,128)} %hyper.1) | copy-start | bytes 4718596
  17.2 109.4 %copy-start.3 = (f32[128,64]{1,0:T(8,128)S(1)}, f32[128,64]{1,0:T(8,128)}, u32[]{:S(2)}) copy-start(f32[128,64]{1,0:T(8,128)} %copy.37.two_ref.two) | copy-start | bytes 98308
  17.2 109.4 %copy-start.5 = (f32[64,128]{1,0:T(8,128)S(1)}, f32[64,128]{1,0:T(8,128)}, u32[]{:S(2)}) copy-start(f32[64,128]{1,0:T(8,128)} %one.1) | copy-start | bytes 98308
  17.2 109.4 %copy-start.6 = (f32[64,128]{1,0:T(8,128)S(1)}, f32[64,128]{1,0:T(8,128)}, u32[]{:S(2)}) copy-start(f32[64,128]{1,0:T(8,128)} %one_m.1) | copy-start | bytes 98308
  17.3 109.4 %copy-start.7 = (f32[64,128]{1,0:T(8,128)S(1)}, f32[64,128]{1,0:T(8,128)}, u32[]{:S(2)}) copy-start(f32[64,128]{1,0:T(8,128)} %one_v.1) | copy-start | bytes 98308
  17.3 109.4 %copy-start.8 = (f32[10,64]{1,0:T(8,128)S(1)}, f32[10,64]{1,0:T(8,128)}, u32[]{:S(2)}) copy-start(f32[10,64]{1,0:T(8,128)} %embeds.1) | copy-start | bytes 7684
  17.3 109.4 %copy-start.9 = (f32[16,64]{1,0:T(8,128)S(1)}, f32[16,64]{1,0:T(8,128)}, u32[]{:S(2)}) copy-start(f32[16,64]{1,0:T(8,128)} %get-tuple-element.53.coded_ref) | copy-start | bytes 12292
  17.3 109.4 %copy-start.11 = (f32[10,64]{1,0:T(8,128)S(1)}, f32[10,64]{1,0:T(8,128)}, u32[]{:S(2)}) copy-start(f32[10,64]{1,0:T(8,128)} %embeds_m.1) | copy-start | bytes 7684
  17.3 109.4 %copy-start.12 = (f32[10,64]{1,0:T(8,128)S(1)}, f32[10,64]{1,0:T(8,128)}, u32[]{:S(2)}) copy-start(f32[10,64]{1,0:T(8,128)} %embeds_v.1) | copy-start | bytes 7684
  126.7 1.4 %copy-start.1 = (f32[64,6144]{1,0:T(8,128)S(1)}, f32[64,6144]{1,0:T(8,128)}, u32[]{:S(2)}) copy-start(f32[64,6144]{1,0:T(8,128)} %hyper_m.1) | copy-start | bytes 4718596
  128.1 1.4 %copy-start.2 = (f32[64,6144]{1,0:T(8,128)S(1)}, f32[64,6144]{1,0:T(8,128)}, u32[]{:S(2)}) copy-start(f32[64,6144]{1,0:T(8,128)} %hyper_v.1) | copy-start | bytes 4718596
  129.5 1.0 copy-start.4
  130.5 0.7 copy-start.10

commit v3 on v2

v3 whole, which is shorter than its diff:
```python
import math
from functools import partial

import jax
import jax.numpy as jnp
from jax import lax
from jax.experimental import pallas as pl
from jax.experimental.pallas import tpu as pltpu
from jax.sharding import PartitionSpec as P

D = 512
HEADS = 8
ADAPTER = 24
TASKS = 8
LAYERS = 2
SRC = 256
TGT = 128
FF = 2048
SEQ_DEV = 2
GEN = 4
LOW = 128
SRC_CAP = 176
TGT_CAP = 128
FLAT = 48
STEP = 5


epsilon = 1e-06
clip_limit = 0.001
beta_one = 0.9
beta_two = 0.999
adam_floor = 1e-08
weight_decay = 0.01
rates = (0.5, 0.1, 0.1, 0.005)
blocked = -1000000000.0
highest = lax.Precision.HIGHEST
LOGIT_SCALE = D ** (-0.5)
EXP_SCALE = LOGIT_SCALE / math.log(2.0)
UPSCALE = math.sqrt(D / ADAPTER)
GELU_A = math.sqrt(2.0 / math.pi)
GELU_B = 0.044715
VOCAB_TILE = 2048
UPDATE_STEPS = 4
WIDE = 5472
VMEM_LIMIT = 62 * 1024 * 1024
MESH = pl.DeviceIdType.MESH


def adamw(weight, first, second, grad, rate):
    first = beta_one * first + (1.0 - beta_one) * grad
    second = beta_two * second + (1.0 - beta_two) * grad * grad
    corrected = first * (1.0 / (1.0 - beta_one**STEP))
    spread = jnp.sqrt(second * (1.0 / (1.0 - beta_two**STEP))) + adam_floor
    return (weight - rate * (corrected / spread + weight_decay * weight), first, second)


def mm(left, right):
    return lax.dot_general(
        left, right, (((1,), (0,)), ((), ())), preferred_element_type=jnp.float32
    )


def mm_last(left, right):
    return lax.dot_general(
        left, right, (((1,), (1,)), ((), ())), preferred_element_type=jnp.float32
    )


def mm_first(left, right):
    return lax.dot_general(
        left, right, (((0,), (0,)), ((), ())), preferred_element_type=jnp.float32
    )


def exact(left, right, dims):
    return lax.dot_general(
        left, right, (dims, ((), ())), precision=highest, preferred_element_type=jnp.float32
    )


def norm_scale(value):
    return lax.rsqrt(jnp.mean(value * value, axis=-1, keepdims=True) + epsilon)


def normed(value, gain):
    return (value * norm_scale(value) * gain).astype(jnp.bfloat16)


def norm_back(value, gain, grad):
    scale = norm_scale(value)
    weighted = grad * gain
    return scale * weighted - value * (
        scale * scale * scale * jnp.mean(weighted * value, axis=-1, keepdims=True)
    )


def gelu_tanh(value):
    return jnp.tanh(value * (GELU_A + (GELU_A * GELU_B) * (value * value)))


def gelu(value):
    return (0.5 * value) * (1.0 + gelu_tanh(value))


def gelu_slope(value, tanh):
    return 0.5 * (1.0 + tanh) + (0.5 * value) * (1.0 - tanh * tanh) * (
        GELU_A + (3.0 * GELU_A * GELU_B) * (value * value)
    )


def halves():
    lane = lax.broadcasted_iota(jnp.int32, (1, 128), 1)
    return [(lane // 64 == half) for half in range(2)]


def attend(q_ref, kv_ref, k_col, v_col, q_len, k_len, allow, out_ref, probs_ref=None):
    sides = halves()
    masks = [side.astype(jnp.float32).astype(jnp.bfloat16) for side in sides]

    def pair_step(pair, carry):
        lanes = pl.multiple_of(pair * 128, 128)
        for seq in range(SEQ_DEV):
            q_rows = pl.ds(seq * q_len, q_len)
            k_rows = pl.ds(seq * k_len, k_len)
            query = q_ref[q_rows, pl.ds(lanes, 128)]
            keys = kv_ref[k_rows, pl.ds(k_col + lanes, 128)]
            values = kv_ref[k_rows, pl.ds(v_col + lanes, 128)]
            outs = []
            for half in range(2):
                scores = mm_last(query * masks[half], keys) * 0.125
                scores = jnp.where(allow(seq), scores, blocked)
                peak = jnp.max(scores, axis=-1, keepdims=True)
                weights = jnp.exp(scores - peak)
                probs = weights * (1.0 / jnp.sum(weights, axis=-1, keepdims=True))
                if probs_ref is not None:
                    begin = pl.multiple_of((pair * SEQ_DEV + seq) * q_len, 8)
                    probs_ref[pl.ds(begin, q_len), half * k_len : (half + 1) * k_len] = probs
                outs.append(mm(probs.astype(jnp.bfloat16), values))
            out_ref[q_rows, pl.ds(lanes, 128)] = jnp.where(sides[0], outs[0], outs[1]).astype(
                jnp.bfloat16
            )
        return carry

    lax.fori_loop(0, HEADS // 2, pair_step, 0)


def attend_back(grad_ref, q_ref, kv_ref, probs_ref, q_len, k_len, joined_ref):
    sides = halves()
    masks = [side.astype(jnp.float32).astype(jnp.bfloat16) for side in sides]

    def pair_step(pair, carry):
        lanes = pl.multiple_of(pair * 128, 128)
        for seq in range(SEQ_DEV):
            q_rows = pl.ds(seq * q_len, q_len)
            k_rows = pl.ds(seq * k_len, k_len)
            grad = grad_ref[q_rows, pl.ds(lanes, 128)]
            query = q_ref[q_rows, pl.ds(lanes, 128)]
            values = kv_ref[k_rows, pl.ds(D + lanes, 128)]
            key_grads, value_grads = [], []
            for half in range(2):
                begin = pl.multiple_of((pair * SEQ_DEV + seq) * q_len, 8)
                probs = probs_ref[pl.ds(begin, q_len), half * k_len : (half + 1) * k_len]
                grad_probs = mm_last(grad * masks[half], values)
                value_grads.append(mm_first(probs.astype(jnp.bfloat16), grad))
                inner = jnp.sum(grad_probs * probs, axis=-1, keepdims=True)
                grad_scores = (probs * (grad_probs - inner)).astype(jnp.bfloat16)
                key_grads.append(mm_first(grad_scores, query))
            joined_ref[k_rows, pl.ds(lanes, 128)] = (
                jnp.where(sides[0], key_grads[0], key_grads[1]) * 0.125
            ).astype(jnp.bfloat16)
            joined_ref[k_rows, pl.ds(D + lanes, 128)] = jnp.where(
                sides[0], value_grads[0], value_grads[1]
            ).astype(jnp.bfloat16)
        return carry

    lax.fori_loop(0, HEADS // 2, pair_step, 0)


def feed(state_ref, gain, inner_ref, outer_ref, act_ref, slope_ref, down_ref, up_ref, length,
         plain_ref, low_ref, after_ref):
    rows = SEQ_DEV * length
    act_rows = pl.ds(0, rows)
    source = normed(state_ref[...], gain)
    for block in range(FF // D):
        columns = slice(block * D, (block + 1) * D)
        hidden = mm(source, inner_ref[:, columns])
        tanh = gelu_tanh(hidden)
        act_ref[act_rows, columns] = ((0.5 * hidden) * (1.0 + tanh)).astype(jnp.bfloat16)
        if slope_ref is not None:
            slope_ref[pl.ds(block * rows, rows), :] = gelu_slope(hidden, tanh)
    branch = mm(act_ref[act_rows, :], outer_ref[...])
    plain_ref[...] = branch.astype(jnp.bfloat16)
    for seq in range(SEQ_DEV):
        span = slice(seq * length, (seq + 1) * length)
        lowered = mm(plain_ref[span, :], down_ref[seq])
        low_ref[span, :] = lowered
        adapted = mm(gelu(lowered).astype(jnp.bfloat16), up_ref[seq]) * UPSCALE
        after_ref[span, :] = state_ref[span, :] + branch[span, :] + adapted


def adapter_back(grad_ref, low_ref, plain_ref, down_ref, up_ref, length, grad_down_ref,
                 grad_up_ref, branch_ref=None):
    for seq in range(SEQ_DEV):
        span = slice(seq * length, (seq + 1) * length)
        grad = grad_ref[span, :]
        grad_low = grad.astype(jnp.bfloat16)
        lowered = low_ref[span, :]
        tanh = gelu_tanh(lowered)
        bottleneck = ((0.5 * lowered) * (1.0 + tanh)).astype(jnp.bfloat16)
        grad_bottle = mm_last(grad_low, up_ref[seq]) * UPSCALE
        grad_up_ref(seq)[...] = mm_first(bottleneck, grad_low)[:ADAPTER] * UPSCALE
        grad_lowered = (grad_bottle * gelu_slope(lowered, tanh)).astype(jnp.bfloat16)
        grad_down_ref(seq)[...] = mm_first(plain_ref[span, :], grad_lowered)
        if branch_ref is not None:
            branch_ref[span, :] = (grad + mm_last(grad_lowered, down_ref[seq])).astype(
                jnp.bfloat16
            )


def pair_rows(embeds):
    return jnp.concatenate(
        [
            embeds[task : task + 1, :] + embeds[TASKS + layer : TASKS + layer + 1, :]
            for task in range(TASKS)
            for layer in range(LAYERS)
        ],
        axis=0,
    )


def place_rows(src_ref, tgt_ref, member, peer, part, done):
    offset = member * part
    wide_tokens = SEQ_DEV * SRC
    order = lax.broadcasted_iota(jnp.int32, (wide_tokens, wide_tokens), 0)
    upto = (
        (order <= lax.broadcasted_iota(jnp.int32, (wide_tokens, wide_tokens), 1))
        .astype(jnp.float32)
        .astype(jnp.bfloat16)
    )
    crowded = jnp.zeros((1, 1), jnp.float32)
    slots, wanted = [], []
    for ids_ref, length, rows in ((src_ref, SRC, SRC_CAP), (tgt_ref, TGT, TGT_CAP)):
        count = SEQ_DEV * length
        ids = jnp.concatenate(
            [
                jnp.concatenate(
                    [ids_ref[pl.ds(SEQ_DEV * peer(k) + s, 1), :] for s in range(SEQ_DEV)], axis=1
                )
                for k in range(GEN)
            ],
            axis=0,
        )
        if length == TGT:
            lane = lax.broadcasted_iota(jnp.int32, (GEN, 128), 1)
            ids = jnp.concatenate([ids, jnp.where(lane == 0, 0, -1)], axis=1)
            count = count + 128
        own = ids[0:1]
        local = ids - offset
        inside = ((local >= 0) & (local < part) & (ids >= 0)).astype(jnp.float32)
        held = [
            ((own >= part * o) & (own < part * (o + 1))).astype(jnp.float32) for o in range(GEN)
        ]
        marks = jnp.concatenate([inside] + held, axis=0)
        ranks = mm(marks.astype(jnp.bfloat16), upto[:count, :count]) - 1.0
        ranks = ranks - (done * count).astype(jnp.float32)
        for o in range(GEN):
            amount = ((ids >= part * o) & (ids < part * (o + 1))).astype(jnp.float32)
            most = jnp.max(jnp.sum(amount, axis=1, keepdims=True), axis=0, keepdims=True)
            crowded = jnp.maximum(crowded, (most > float(rows)).astype(jnp.float32))
        numbers = local.astype(jnp.float32) + 1.0
        spot = lax.broadcasted_iota(jnp.int32, (rows, count), 0).astype(jnp.float32)
        columns = []
        for k in range(GEN):
            position = jnp.where(inside[k : k + 1] > 0.0, ranks[k : k + 1], -1.0)
            columns.append(
                jnp.sum(jnp.where(spot == position, numbers[k : k + 1], 0.0), axis=1, keepdims=True)
                - 1.0
            )
        wanted.append(columns)
        slot = jnp.full((1, count), -1.0, jnp.float32)
        for o in range(GEN):
            rank = ranks[GEN + o : GEN + o + 1]
            now = (held[o] > 0.0) & (rank >= 0.0) & (rank < float(rows))
            slot = jnp.where(now, rank + float(o * rows), slot)
        slots.append(slot)
    targets = SEQ_DEV * TGT
    lane = lax.broadcasted_iota(jnp.int32, (1, targets), 1)
    shifted = jnp.where(
        lax.rem(lane, TGT) == 0,
        slots[1][:, targets : targets + 1],
        pltpu.roll(slots[1][:, :targets], 1, axis=1),
    )
    return wanted, slots[0], shifted, slots[1][:, :targets], crowded


def describe(task_ref, lens_ref, count_ref, member):
    own_first = member * SEQ_DEV
    position = lax.broadcasted_iota(jnp.int32, (1, SRC), 1)
    place = lax.broadcasted_iota(jnp.int32, (1, TGT), 1)
    task = lax.broadcasted_iota(jnp.int32, (1, TASKS), 1)
    allow, valid = [], []
    tokens = jnp.zeros((1, 1), jnp.float32)
    for s in range(SEQ_DEV):
        length = jnp.sum(
            jnp.where(task == task_ref[own_first + s], lens_ref[...], 0).astype(jnp.float32),
            axis=1,
            keepdims=True,
        )
        allow.append((position.astype(jnp.float32) < length).astype(jnp.float32))
        valid.append((place < count_ref[own_first + s]).astype(jnp.float32))
        tokens = tokens + jnp.sum(valid[-1], axis=1, keepdims=True)
    return jnp.concatenate(allow, axis=1), jnp.concatenate(valid, axis=1), tokens


def generate(task_ref, embeds_ref, one_ref, two_ref, hyper_ref, coded_ref, chosen,
             adapters, sel):
    coded = exact(
        gelu(exact(pair_rows(embeds_ref[...]), one_ref[...], ((1,), (0,)))),
        two_ref[...],
        ((1,), (1,)),
    )
    coded_ref[...] = coded
    flat = exact(coded, hyper_ref[...], ((1,), (0,))).astype(jnp.bfloat16)
    pairs = TASKS * LAYERS
    sequences = GEN * SEQ_DEV
    row_of = lax.broadcasted_iota(jnp.int32, (pairs, pairs), 0)
    column_of = lax.broadcasted_iota(jnp.int32, (pairs, pairs), 1)
    picks = jnp.zeros((pairs, pairs), jnp.float32)
    selector = jnp.zeros((pairs, pairs), jnp.float32)
    for seq in range(sequences):
        for layer in range(LAYERS):
            pair = task_ref[seq] * LAYERS + layer
            picks = jnp.where(
                (row_of == seq * LAYERS + layer) & (column_of == pair), 1.0, picks
            )
            selector = jnp.where(
                (row_of == pair) & (column_of == layer * sequences + seq), 1.0, selector
            )
    sel[...] = selector
    taken = mm(picks.astype(jnp.bfloat16), flat)
    for tile in range(FLAT):
        chosen[pl.ds(tile, pairs, stride=FLAT), :] = taken[:, 128 * tile : 128 * (tile + 1)]
    share = SEQ_DEV * LAYERS * FLAT
    for target in range(GEN):
        adapters[target] = chosen[pl.ds(target * share, share), :].astype(jnp.bfloat16)


def step_kernel(
    done_ref,
    task_ref,
    count_ref,
    lens_ref,
    src_ref,
    tgt_ref,
    embeds_ref,
    one_ref,
    two_ref,
    gains_ref,
    known_hbm,
    hyper_hbm,
    attn_hbm,
    inner_hbm,
    outer_hbm,
    table_hbm,
    out_ref,
    small_ref,
    coded_ref,
    missing_ref,
    attn,
    inner,
    outer,
    table,
    wide,
    plain_e,
    qkv,
    mixed,
    act,
    memory,
    q_cross,
    plain_d,
    feats,
    stats,
    stats_in,
    grad_low,
    rows_out,
    known,
    src_in,
    tgt_in,
    generated,
    spread,
    adapters_ref,
    adapters_in,
    sel_ref,
    down_ref,
    up_ref,
    pack,
    grads_in,
    hyper,
    outgoing,
    incoming,
    shares,
    summary,
    summary_in,
    verdict_in,
    load_sem,
    row_send,
    src_recv,
    tgt_recv,
    adapter_recv,
    grad_send,
    grad_recv,
    scatter_sem,
    share_sem,
    small_send,
    small_recv,
    verdict_sem,
    feat_send,
    feat_recv,
    result_send,
    result_recv,
    stat_send,
    stat_recv,
):
    member = lax.axis_index("gen")
    barrier = pltpu.get_barrier_semaphore()
    sources = SEQ_DEV * SRC
    targets = SEQ_DEV * TGT
    own = pl.ds(0, targets)
    part = table.shape[0]

    spans = []

    def view(rows, lanes=None):
        begin = spans[-1] if spans else 0
        if lanes is None:
            spans.append(begin + rows)
            return wide.at[pl.ds(begin, rows)]
        return wide.at[pl.ds(begin, rows), lanes]

    state, after_e, grad = view(sources), view(sources), view(sources)
    y1, y2, y3, total, wanted = (view(targets) for _ in range(5))
    slope = view(targets * (FF // D))
    probs = view(SEQ_DEV * HEADS // 2 * TGT)
    low_e = view(sources, pl.ds(0, LOW))
    low_d = view(targets, pl.ds(LOW, LOW))
    view(sources)
    first_up = spans[-1]
    view(LAYERS * SEQ_DEV * ADAPTER)

    def grad_down_ref(seq):
        return spread.at[pl.ds(seq * D, D)]

    def grad_up_ref(layer, seq):
        begin = first_up + (layer * SEQ_DEV + seq) * ADAPTER
        return wide.at[pl.ds(begin, ADAPTER)]

    def flat_in(owner):
        return generated.at[pl.ds(owner * SEQ_DEV * LAYERS * FLAT, SEQ_DEV * LAYERS * FLAT)]

    kv_cross = attn.at[0, :, pl.ds(0, 2 * D)]
    joined = attn.at[0, :, pl.ds(2 * D, 2 * D)]

    def results(order):
        return outer.at[0, pl.ds(pl.multiple_of(order * targets, targets), targets)]

    def arrived(order):
        begin = pl.multiple_of((GEN + order) * targets, targets)
        return outer.at[0, pl.ds(begin, targets)]

    def peer(order):
        chip = lax.rem(member // 2 + lax.rem((order + 1) // 2, 2), 2)
        return chip * 2 + lax.rem(lax.rem(member, 2) + order // 2, 2)

    rank = lax.axis_index("dp")
    count = outgoing.shape[0]
    width = TASKS * LAYERS * FLAT * 128 // (TASKS * LAYERS * count)
    loads = []

    def load(source, target):
        loads.append(pltpu.make_async_copy(source, target, load_sem.at[len(loads)]))
        loads[-1].start()
        return loads[-1]

    cuts = [0, 2048, 4096, 6144, part]
    table_loads = [
        load(
            table_hbm.at[pl.ds(cuts[i], cuts[i + 1] - cuts[i])],
            table.at[pl.ds(cuts[i], cuts[i + 1] - cuts[i])],
        )
        for i in range(4)
    ]
    hyper_load = load(hyper_hbm, hyper)
    known_load = load(known_hbm.at[pl.ds(0, known.shape[0])], known)
    for order in range(1, GEN):
        pl.semaphore_signal(
            barrier, inc=1, device_id={"gen": peer(order)}, device_id_type=MESH
        )

    def greet(step, carry):
        pl.semaphore_signal(
            barrier, inc=1, device_id={"dp": lax.rem(rank + step, count)}, device_id_type=MESH
        )
        return carry

    lax.fori_loop(1, count, greet, 0)
    weight_loads = [
        load(source, target)
        for source, target in (
            (attn_hbm.at[0], attn.at[0]),
            (inner_hbm.at[0], inner.at[0]),
            (outer_hbm.at[0], outer.at[0]),
            (attn_hbm.at[1], attn.at[1]),
            (attn_hbm.at[2], attn.at[2]),
            (inner_hbm.at[1], inner.at[1]),
            (outer_hbm.at[1], outer.at[1]),
        )
    ]

    (source_rows, target_rows), source_slot, input_slot, target_slot, crowded = place_rows(
        src_ref, tgt_ref, member, peer, part, done_ref[0]
    )

    def gather(columns, begin, orders, first=False):
        numbers = jnp.concatenate([columns[order] for order in orders], axis=0)
        height = numbers.shape[0]
        found = None
        for i in range(len(cuts) - 1):
            if first:
                table_loads[i].wait()
            lane = lax.broadcasted_iota(jnp.int32, (height, cuts[i + 1] - cuts[i]), 1)
            hit = ((lane + cuts[i]).astype(jnp.float32) == numbers).astype(jnp.float32)
            piece = mm(hit.astype(jnp.bfloat16), table[cuts[i] : cuts[i + 1], :])
            found = piece if found is None else found + piece
        size = height // len(orders)
        for place, order in enumerate(orders):
            rows_out[peer(order), pl.ds(begin, size), :] = found[
                place * size : (place + 1) * size
            ].astype(jnp.bfloat16)

    def source_copy(owner, target):
        return pltpu.make_async_remote_copy(
            src_ref=rows_out.at[target, pl.ds(0, SRC_CAP)],
            dst_ref=src_in.at[owner],
            send_sem=row_send.at[0, target],
            recv_sem=src_recv.at[owner],
            device_id={"gen": target},
            device_id_type=MESH,
        )

    def target_copy(owner, target):
        return pltpu.make_async_remote_copy(
            src_ref=rows_out.at[target, pl.ds(SRC_CAP, TGT_CAP)],
            dst_ref=tgt_in.at[owner],
            send_sem=row_send.at[1, target],
            recv_sem=tgt_recv.at[owner],
            device_id={"gen": target},
            device_id_type=MESH,
        )

    def adapter_copy(owner, target):
        return pltpu.make_async_remote_copy(
            src_ref=adapters_ref.at[target],
            dst_ref=adapters_in.at[owner],
            send_sem=row_send.at[2, target],
            recv_sem=adapter_recv.at[owner],
            device_id={"gen": target},
            device_id_type=MESH,
        )

    pl.semaphore_wait(barrier, GEN + count - 2)
    gather(source_rows, 0, (1, 2), True)
    for order in (1, 2):
        source_copy(member, peer(order)).start()
    hyper_load.wait()
    generate(task_ref, embeds_ref, one_ref, two_ref, hyper, coded_ref, generated, adapters_ref,
             sel_ref)
    for order in range(1, GEN):
        adapter_copy(member, peer(order)).start()
    gather(target_rows, SRC_CAP, (1, 2))
    for order in (1, 2):
        target_copy(member, peer(order)).start()
    gather(source_rows, 0, (3, 0))
    source_copy(member, peer(3)).start()
    gather(target_rows, SRC_CAP, (3, 0))
    target_copy(member, peer(3)).start()
    src_in[member] = rows_out[member, 0:SRC_CAP, :]
    tgt_in[member] = rows_out[member, SRC_CAP : SRC_CAP + TGT_CAP, :]
    adapters_in[member] = adapters_ref[member]
    allow, valid, tokens = describe(task_ref, lens_ref, count_ref, member)

    def spread_rows(slot, incoming_rows, owner):
        height = incoming_rows.shape[1]
        spot = lax.broadcasted_iota(jnp.int32, (height, slot.shape[1]), 0)
        spot = (spot + owner * height).astype(jnp.float32)
        chosen = (spot == slot).astype(jnp.float32)
        return mm_first(chosen.astype(jnp.bfloat16), incoming_rows[owner])

    known_load.wait()

    def known_rows(begin, size):
        rows = known[begin : begin + size, :].astype(jnp.float32)
        return jnp.where(done_ref[0] > 0, rows, 0.0)

    after_e[...] = known_rows(0, sources) + spread_rows(
        source_slot, src_in, member
    )
    for order in (3, 1, 2):
        source_copy(peer(order), peer(order)).wait_recv()
        after_e[...] = after_e[...] + spread_rows(source_slot, src_in, peer(order))
    embedded = after_e[...]

    def allowed(seq):
        return allow[:, seq * SRC : (seq + 1) * SRC] > 0.0

    entry = normed(embedded, gains_ref[0:1])
    weight_loads[0].wait()
    for block in range(3):
        columns = slice(block * D, (block + 1) * D)
        qkv[:, columns] = mm(entry, attn[0, :, columns]).astype(jnp.bfloat16)
    attend(qkv, qkv, D, 2 * D, SRC, SRC, allowed, mixed)
    state[...] = embedded + mm(mixed[...], attn[0, :, 3 * D :])
    weight_loads[1].wait()
    weight_loads[2].wait()
    for order in range(1, GEN):
        adapter_copy(peer(order), peer(order)).wait_recv()
    unpack_adapters(adapters_in, flat_in, spread, down_ref, up_ref)
    feed(state, gains_ref[1:2], inner.at[0], outer.at[0], act, None, down_ref.at[0], up_ref.at[0],
         SRC, plain_e, low_e, after_e)
    memory[...] = normed(after_e[...], gains_ref[2:3])

    for order in range(1, GEN):
        target_copy(peer(order), peer(order)).wait_recv()
    inputs = known_rows(sources, targets)
    for owner in range(GEN):
        inputs = inputs + spread_rows(input_slot, tgt_in, owner)
    entry = normed(inputs, gains_ref[3:4])
    weight_loads[3].wait()
    for block in range(3):
        columns = slice(block * D, (block + 1) * D)
        qkv[own, columns] = mm(entry, attn[1, :, columns]).astype(jnp.bfloat16)
    causal = lax.broadcasted_iota(jnp.int32, (TGT, TGT), 0) >= lax.broadcasted_iota(
        jnp.int32, (TGT, TGT), 1
    )
    attend(qkv, qkv, D, 2 * D, TGT, TGT, lambda seq: causal, mixed)
    y1[...] = inputs + mm(mixed[own, :], attn[1, :, 3 * D :])
    weight_loads[4].wait()
    q_cross[...] = mm(normed(y1[...], gains_ref[4:5]), attn[2, :, :D]).astype(jnp.bfloat16)
    for block in range(2):
        columns = slice(block * D, (block + 1) * D)
        kv_cross[:, columns] = mm(
            memory[...], attn[2, :, (block + 1) * D : (block + 2) * D]
        ).astype(jnp.bfloat16)
    attend(q_cross, kv_cross, 0, D, TGT, SRC, allowed,
           mixed, probs)
    y2[...] = y1[...] + mm(mixed[own, :], attn[2, :, 3 * D :])
    weight_loads[5].wait()
    weight_loads[6].wait()
    feed(y2, gains_ref[5:6], inner.at[1], outer.at[1], act, slope, down_ref.at[1], up_ref.at[1],
         TGT, plain_d, low_d, y3)
    feats[0] = normed(y3[...], gains_ref[6:7])


    def feature_copy(order):
        return pltpu.make_async_remote_copy(
            src_ref=feats.at[0],
            dst_ref=feats.at[order],
            send_sem=feat_send.at[order],
            recv_sem=feat_recv.at[order],
            device_id={"gen": peer(order)},
            device_id_type=MESH,
        )

    def result_copy(order):
        return pltpu.make_async_remote_copy(
            src_ref=results(order),
            dst_ref=arrived(order),
            send_sem=result_send.at[order],
            recv_sem=result_recv.at[order],
            device_id={"gen": peer(order)},
            device_id_type=MESH,
        )

    def stat_copy(order):
        return pltpu.make_async_remote_copy(
            src_ref=stats.at[order],
            dst_ref=stats_in.at[order],
            send_sem=stat_send.at[order],
            recv_sem=stat_recv.at[order],
            device_id={"gen": peer(order)},
            device_id_type=MESH,
        )

    for order in range(1, GEN):
        feature_copy(order).start()
    wanted[...] = known_rows(sources + targets, targets)
    for owner in range(GEN):
        wanted[...] = wanted[...] + spread_rows(target_slot, tgt_in, owner)
    same = lax.broadcasted_iota(jnp.int32, (targets, targets), 0) == lax.broadcasted_iota(
        jnp.int32, (targets, targets), 1
    )

    def as_row(column):
        return jnp.sum(jnp.where(same, column, 0.0), axis=0, keepdims=True)

    def as_column(row):
        return jnp.sum(jnp.where(same, row, 0.0), axis=1, keepdims=True)

    def block_step(order, carry):
        @pl.when(order > 0)
        def _():
            feature_copy(order).wait_recv()

        query = feats[order]
        ends = list(range(0, table.shape[0], VOCAB_TILE)) + [table.shape[0]]
        tiles = [(ends[i], ends[i + 1]) for i in range(len(ends) - 1)]
        peak = scale = None
        scores = mm_last(query, table[tiles[0][0] : tiles[0][1], :])
        for index, (first, last) in enumerate(tiles):
            following = None
            if index + 1 < len(tiles):
                following = mm_last(query, table[tiles[index + 1][0] : tiles[index + 1][1], :])
            top = jnp.max(scores, axis=-1, keepdims=True)
            if index > 0:
                top = jnp.maximum(peak, top)
            weights = jnp.exp2((scores - top) * EXP_SCALE)
            amount = jnp.sum(weights, axis=-1, keepdims=True)
            part = mm(weights.astype(jnp.bfloat16), table[first:last, :])
            if index == 0:
                total[...] = part
                scale = amount
            else:
                shrink = jnp.exp2((peak - top) * EXP_SCALE)
                total[...] = total[...] * shrink + part
                scale = scale * shrink + amount
            peak, scores = top, following
        results(order)[...] = total[...].astype(jnp.bfloat16)
        stats[order] = jnp.concatenate(
            [as_row(peak), as_row(scale), jnp.zeros((6, targets), jnp.float32)], axis=0
        )

        @pl.when(order > 0)
        def _():
            result_copy(order).start()
            stat_copy(order).start()

        return carry

    lax.fori_loop(0, GEN, block_step, 0)
    stats_in[0] = stats[0]
    for order in range(1, GEN):
        stat_copy(order).wait_recv()
    peaks = [as_column(stats_in[order, 0:1, :]) for order in range(GEN)]
    sums = [as_column(stats_in[order, 1:2, :]) for order in range(GEN)]
    top = jnp.maximum(jnp.maximum(peaks[0], peaks[1]), jnp.maximum(peaks[2], peaks[3]))
    parts = [jnp.exp2((peaks[order] - top) * EXP_SCALE) for order in range(GEN)]
    amount = sum(parts[order] * sums[order] for order in range(GEN))
    logsum = top * LOGIT_SCALE + jnp.log(amount)
    inverse = 1.0 / amount
    total[...] = results(0)[...].astype(jnp.float32) * (parts[0] * inverse)
    for order in range(1, GEN):
        result_copy(order).wait_recv()
        total[...] = total[...] + arrived(order)[...].astype(jnp.float32) * (parts[order] * inverse)
    picked = (
        jnp.sum(feats[0].astype(jnp.float32) * wanted[...], axis=-1, keepdims=True) * LOGIT_SCALE
    )
    counted = as_column(valid)
    loss = jnp.sum((logsum - picked) * counted, axis=0, keepdims=True)
    lane = lax.broadcasted_iota(jnp.int32, (8, 128), 1)
    totals = jnp.where(
        lane == 0, loss, jnp.where(lane == 1, tokens, jnp.where(lane == 2, crowded, 0.0))
    )

    grad[own, :] = norm_back(
        y3[...], gains_ref[6:7], (total[...] - wanted[...]) * (counted * LOGIT_SCALE)
    )
    adapter_back(grad.at[own], low_d, plain_d, down_ref.at[1], up_ref.at[1], TGT,
                 grad_down_ref, partial(grad_up_ref, 1), grad_low)

    def grad_copy(layer, owner, target):
        part = SEQ_DEV * FLAT
        begin = pl.multiple_of((layer * GEN + owner) * part, 8)
        return pltpu.make_async_remote_copy(
            src_ref=pack.at[layer, target],
            dst_ref=grads_in.at[pl.ds(begin, part)],
            send_sem=grad_send.at[layer, target],
            recv_sem=grad_recv.at[layer, owner],
            device_id={"gen": target},
            device_id_type=MESH,
        )

    def send_grads(layer):
        pack_grads(grad_down_ref, partial(grad_up_ref, layer), pack.at[layer])
        for order in range(1, GEN):
            grad_copy(layer, member, peer(order)).start()
        begin = pl.multiple_of((layer * GEN + member) * SEQ_DEV * FLAT, 8)
        grads_in[pl.ds(begin, SEQ_DEV * FLAT), :] = pack[layer, member]

    send_grads(1)
    for block in range(FF // D):
        columns = slice(block * D, (block + 1) * D)
        act[own, columns] = (
            mm_last(grad_low[...], outer[1, columns, :])
            * slope[pl.ds(block * targets, targets), :]
        ).astype(jnp.bfloat16)
    grad_entry = mm_last(act[own, :], inner[1])
    grad_state = grad[own, :] + norm_back(y2[...], gains_ref[5:6], grad_entry)
    mixed[own, :] = mm_last(grad_state.astype(jnp.bfloat16), attn[2, :, 3 * D :]).astype(
        jnp.bfloat16
    )
    attend_back(mixed, q_cross, kv_cross, probs, TGT, SRC, joined)
    grad_memory = mm_last(joined[...], attn[2, :, D : 3 * D])

    grad[...] = norm_back(after_e[...], gains_ref[2:3], grad_memory)
    adapter_back(grad, low_e, plain_e, down_ref.at[0], up_ref.at[0], SRC,
                 grad_down_ref, partial(grad_up_ref, 0))
    send_grads(0)
    for layer in range(LAYERS):
        for order in range(1, GEN):
            grad_copy(layer, peer(order), peer(order)).wait_recv()
    pairs = TASKS * LAYERS
    received = jnp.concatenate(
        [grads_in[pl.ds(tile, pairs, stride=FLAT), :] for tile in range(FLAT)], axis=1
    )
    slots = exact(sel_ref[...], received, ((1,), (0,)))

    padded = outgoing.shape[2]
    for piece in range(count):
        low_edge = piece * width // 128 * 128
        shift = piece * width - low_edge
        window = slots[:, low_edge : low_edge + padded]
        if shift:
            window = pltpu.roll(window, padded - shift, axis=1)
        outgoing[piece] = window

    def scatter(step, carry):
        target = lax.rem(rank + step, count)
        pltpu.make_async_remote_copy(
            src_ref=outgoing.at[target],
            dst_ref=incoming.at[rank],
            send_sem=scatter_sem.at[0],
            recv_sem=scatter_sem.at[1],
            device_id={"dp": target},
            device_id_type=MESH,
        ).start()
        return carry

    def share(step, carry):
        pltpu.make_async_remote_copy(
            src_ref=shares.at[rank],
            dst_ref=shares.at[rank],
            send_sem=share_sem.at[0],
            recv_sem=share_sem.at[1],
            device_id={"dp": lax.rem(rank + step, count)},
            device_id_type=MESH,
        ).start()
        return carry

    def announce(step, carry):
        pltpu.make_async_remote_copy(
            src_ref=verdict_in.at[rank],
            dst_ref=verdict_in.at[rank],
            send_sem=verdict_sem.at[0],
            recv_sem=verdict_sem.at[1],
            device_id={"dp": lax.rem(rank + step, count)},
            device_id_type=MESH,
        ).start()
        return carry

    def wait_all(ref, sem):
        others = ref.at[pl.ds(0, count - 1)]
        pltpu.make_async_copy(others, others, sem).wait()

    lax.fori_loop(1, count, scatter, 0)
    incoming[rank] = outgoing[rank]
    wait_all(incoming, scatter_sem.at[1])
    summed = incoming[0]
    for source in range(1, count):
        summed = summed + incoming[source]
    shares[rank] = summed

    window_lane = lax.broadcasted_iota(jnp.int32, (1, padded), 1)
    piece_rows = jnp.where(window_lane < width, summed, 0.0)
    shift = lax.rem(rank * width, 128)
    if width % 128:
        piece_rows = jnp.where(
            shift > 0, pltpu.roll(piece_rows, width % 128, axis=1), piece_rows
        )
    low_edge = pl.multiple_of(rank * width // 128 * 128, 128)
    piece_hyper = hyper[:, pl.ds(low_edge, padded)]
    coded_part = exact(piece_rows, piece_hyper, ((1,), (1,)))
    hyper_grad = exact(coded_ref[...], piece_rows, ((0,), (0,)))
    square = jnp.sum(
        jnp.sum(hyper_grad * hyper_grad, axis=0, keepdims=True), axis=1, keepdims=True
    )
    summary[0:16, :] = jnp.concatenate(
        [coded_part, jnp.broadcast_to(square, (16, 64))], axis=1
    )
    summary[16:24, :] = totals
    copies = [
        pltpu.make_async_remote_copy(
            src_ref=summary,
            dst_ref=summary_in.at[member],
            send_sem=small_send.at[step],
            recv_sem=small_recv.at[step],
            device_id={"gen": lax.rem(member + step, GEN)},
            device_id_type=MESH,
        )
        for step in range(1, GEN)
    ]
    for copy in copies:
        copy.start()
    summary_in[member] = summary[...]
    lax.fori_loop(1, count, share, 0)
    for copy in copies:
        copy.wait_recv()
    verdict_in[rank] = (summary_in[0] + summary_in[1]) + (summary_in[2] + summary_in[3])
    lax.fori_loop(1, count, announce, 0)
    for order in range(1, GEN):
        source_copy(member, peer(order)).wait_send()
        adapter_copy(member, peer(order)).wait_send()
        target_copy(member, peer(order)).wait_send()
        feature_copy(order).wait_send()
        result_copy(order).wait_send()
        stat_copy(order).wait_send()
        for layer in range(LAYERS):
            grad_copy(layer, member, peer(order)).wait_send()
    for copy in copies:
        copy.wait_send()
    wait_all(outgoing, scatter_sem.at[0])
    wait_all(shares, share_sem.at[1])
    for piece in range(0, count, 2 if width % 128 else 1):
        first = shares[piece]
        if width % 128:
            second = pltpu.roll(shares[piece + 1], width % 128, axis=1)
            middle = width // 128 * 128
            begin = piece * width
            lane128 = lax.broadcasted_iota(jnp.int32, (1, 128), 1)
            out_ref[:, begin : begin + middle] = first[:, :middle]
            out_ref[:, begin + middle : begin + middle + 128] = jnp.where(
                lane128 < width % 128, first[:, middle : middle + 128], second[:, :128]
            )
            out_ref[:, begin + middle + 128 : begin + 2 * width] = second[
                :, 128 : 2 * width - middle
            ]
        else:
            out_ref[:, piece * width : (piece + 1) * width] = first[:, :width]
    wait_all(verdict_in, verdict_sem.at[1])
    result = verdict_in[0]
    for source in range(1, count):
        result = result + verdict_in[source]
    small_ref[...] = result
    missing_ref[0] = jnp.max(result[16:17, 2:3]).astype(jnp.int32)
    wait_all(shares, share_sem.at[0])
    wait_all(verdict_in, verdict_sem.at[0])


def unpack_adapters(entries, flat, spread, down_ref, up_ref):
    lane = lax.broadcasted_iota(jnp.int32, (1, 128), 1)
    kept = lane < ADAPTER
    run = D // 32
    for owner in range(GEN):
        flat(owner)[...] = entries[owner].astype(jnp.float32)
    up_ref[...] = jnp.zeros(up_ref.shape, jnp.bfloat16)
    for layer in range(LAYERS):
        for seq in range(SEQ_DEV):
            base = (seq * LAYERS + layer) * FLAT
            for owner in range(GEN // 2):
                tiles = [flat(owner)[pl.ds(base + j, run, stride=3), :] for j in range(3)]
                for step in range(run):
                    tile, shift = divmod(ADAPTER * step, 128)
                    piece = tiles[tile]
                    if shift:
                        piece = pltpu.roll(piece, 128 - shift, axis=1)
                    if shift + ADAPTER > 128:
                        tail = pltpu.roll(tiles[tile + 1], 128 - shift, axis=1)
                        piece = jnp.where(lane < 128 - shift, piece, tail)
                    spread[pl.ds(owner * (D // 2) + step, run, stride=run), :] = jnp.where(
                        kept, piece, 0.0
                    )
            down_ref[layer, seq] = spread[pl.ds(0, D), :].astype(jnp.bfloat16)
            halves_up = []
            for owner in range(GEN // 2, GEN):
                halves_up.append(
                    jnp.concatenate(
                        [
                            flat(owner)[pl.ds(base + k, ADAPTER // 2, stride=4), :]
                            for k in range(4)
                        ],
                        axis=1,
                    )
                )
            joined = jnp.concatenate(halves_up + [jnp.zeros((8, D), jnp.float32)], axis=0)
            up_ref[layer, seq, 0:32, :] = joined.astype(jnp.bfloat16)


def pack_grads(grad_down, grad_up, pack):
    lane = lax.broadcasted_iota(jnp.int32, (1, 128), 1)
    run = D // 32
    for seq in range(SEQ_DEV):
        base = seq * FLAT
        for owner in range(GEN // 2):
            tiles = [jnp.zeros((run, 128), jnp.float32) for _ in range(3)]
            for step in range(run):
                tile, shift = divmod(ADAPTER * step, 128)
                piece = grad_down(seq)[pl.ds(owner * (D // 2) + step, run, stride=run), :]
                if shift:
                    piece = pltpu.roll(piece, shift, axis=1)
                if shift + ADAPTER > 128:
                    tiles[tile] = tiles[tile] + jnp.where(lane >= shift, piece, 0.0)
                    tiles[tile + 1] = tiles[tile + 1] + jnp.where(lane < shift, piece, 0.0)
                else:
                    tiles[tile] = tiles[tile] + piece
            for j in range(3):
                pack[owner, pl.ds(base + j, run, stride=3), :] = tiles[j]
        for half in range(GEN // 2):
            rows = slice(half * (ADAPTER // 2), (half + 1) * (ADAPTER // 2))
            for k in range(4):
                pack[GEN // 2 + half, pl.ds(base + k, ADAPTER // 2, stride=4), :] = grad_up(seq)[
                    rows, 128 * k : 128 * (k + 1)
                ]


def step(done, known, task_ids, task_len, tgt_count, src_ids, tgt_ids, embeds, one, two, gains,
         hyper, attn_w, ffn_in, ffn_out, table):
    vmem = pl.BlockSpec(memory_space=pltpu.VMEM)
    smem = pl.BlockSpec(memory_space=pltpu.SMEM)
    whole = pl.BlockSpec(memory_space=pl.ANY)
    low, full = jnp.bfloat16, jnp.float32
    sources, targets = SEQ_DEV * SRC, SEQ_DEV * TGT
    pairs = TASKS * LAYERS
    count = lax.axis_size("dp")
    width = FLAT * 128 // count
    padded = (width + 127) // 128 * 128
    dma = pltpu.SemaphoreType.DMA
    return pl.pallas_call(
        step_kernel,
        out_shape=(
            jax.ShapeDtypeStruct((pairs, FLAT * 128), full),
            jax.ShapeDtypeStruct((24, 128), full),
            jax.ShapeDtypeStruct((pairs, two.shape[0]), full),
            jax.ShapeDtypeStruct((1,), jnp.int32),
        ),
        in_specs=[smem] * 3 + [vmem] * 7 + [whole] * 6,
        out_specs=(vmem, vmem, vmem, smem),
        scratch_shapes=[
            pltpu.VMEM(attn_w.shape, low),
            pltpu.VMEM(ffn_in.shape, low),
            pltpu.VMEM(ffn_out.shape, low),
            pltpu.VMEM(table.shape, low),
            pltpu.VMEM((WIDE, D), full),
            pltpu.VMEM((sources, D), low),
            pltpu.VMEM((sources, 3 * D), low),
            pltpu.VMEM((sources, D), low),
            pltpu.VMEM((sources, FF), low),
            pltpu.VMEM((sources, D), low),
            pltpu.VMEM((targets, D), low),
            pltpu.VMEM((targets, D), low),
            pltpu.VMEM((GEN, targets, D), low),
            pltpu.VMEM((GEN, 8, targets), full),
            pltpu.VMEM((GEN, 8, targets), full),
            pltpu.VMEM((targets, D), low),
            pltpu.VMEM((GEN, SRC_CAP + TGT_CAP, D), low),
            pltpu.VMEM((sources + 2 * targets, D), low),
            pltpu.VMEM((GEN, SRC_CAP, D), low),
            pltpu.VMEM((GEN, TGT_CAP, D), low),
            pltpu.VMEM((pairs * FLAT, 128), full),
            pltpu.VMEM((SEQ_DEV * D, LOW), full),
            pltpu.VMEM((GEN, SEQ_DEV * LAYERS * FLAT, 128), low),
            pltpu.VMEM((GEN, SEQ_DEV * LAYERS * FLAT, 128), low),
            pltpu.VMEM((pairs, pairs), full),
            pltpu.VMEM((LAYERS, SEQ_DEV, D, LOW), low),
            pltpu.VMEM((LAYERS, SEQ_DEV, LOW, D), low),
            pltpu.VMEM((LAYERS, GEN, SEQ_DEV * FLAT, 128), full),
            pltpu.VMEM((LAYERS * GEN * SEQ_DEV * FLAT, 128), full),
            pltpu.VMEM(hyper.shape, full),
            pltpu.VMEM((count, pairs, padded), full),
            pltpu.VMEM((count, pairs, padded), full),
            pltpu.VMEM((count, pairs, padded), full),
            pltpu.VMEM((24, 128), full),
            pltpu.VMEM((GEN, 24, 128), full),
            pltpu.VMEM((count, 24, 128), full),
            dma((14,)),
            dma((3, GEN)),
            dma((GEN,)),
            dma((GEN,)),
            dma((GEN,)),
            dma((LAYERS, GEN)),
            dma((LAYERS, GEN)),
            dma((2,)),
            dma((2,)),
            dma((GEN,)),
            dma((GEN,)),
            dma((2,)),
            dma((GEN,)),
            dma((GEN,)),
            dma((GEN,)),
            dma((GEN,)),
            dma((GEN,)),
            dma((GEN,)),
        ],
        compiler_params=pltpu.CompilerParams(
            collective_id=1, has_side_effects=True, vmem_limit_bytes=VMEM_LIMIT
        ),
        name="rows_forward_vocab_backward_sum",
    )(done, task_ids, tgt_count, task_len.reshape(1, -1), src_ids, tgt_ids, embeds, one, two, gains,
      known, hyper, attn_w, ffn_in, ffn_out, table)


def update_kernel(
    slots_ref,
    small_ref,
    coded_ref,
    embeds,
    embeds_m,
    embeds_v,
    one,
    one_m,
    one_v,
    two,
    two_m,
    two_v,
    hyper,
    hyper_m,
    hyper_v,
    loss_ref,
    tokens_ref,
    norm_ref,
    new_embeds,
    new_embeds_m,
    new_embeds_v,
    new_one,
    new_one_m,
    new_one_v,
    new_two,
    new_two_m,
    new_two_v,
    new_hyper,
    new_hyper_m,
    new_hyper_v,
    held,
    fresh,
    load_sem,
    store_sem,
):
    block = held.shape[3]

    def span(step):
        return pl.ds(step * block, block)

    loads = [
        [
            pltpu.make_async_copy(
                array.at[:, span(step)], held.at[step, index], load_sem.at[step, index]
            )
            for index, array in enumerate((hyper, hyper_m, hyper_v))
        ]
        for step in range(UPDATE_STEPS)
    ]
    for group in loads:
        for load in group:
            load.start()
    coded_grad = small_ref[0:16, 0:64]
    tokens = small_ref[16:17, 1:2]
    loss_ref[...] = small_ref[16:17, 0:1]
    tokens_ref[...] = tokens
    pairs = pair_rows(embeds[...])
    before = exact(pairs, one[...], ((1,), (0,)))
    tanh = gelu_tanh(before)
    active = (0.5 * before) * (1.0 + tanh)
    grad_two = exact(coded_grad, active, ((0,), (0,)))
    grad_before = exact(coded_grad, two[...], ((1,), (0,))) * gelu_slope(before, tanh)
    grad_one = exact(pairs, grad_before, ((0,), (0,)))
    grad_pairs = exact(grad_before, one[...], ((1,), (1,)))
    row = lax.broadcasted_iota(jnp.int32, (16, TASKS * LAYERS), 0)
    column = lax.broadcasted_iota(jnp.int32, (16, TASKS * LAYERS), 1)
    chosen = (row == column // LAYERS) & (row < TASKS) | (row == TASKS + column % LAYERS)
    grad_embeds = exact(chosen.astype(jnp.float32), grad_pairs, ((1,), (0,)))
    grad_embeds = grad_embeds[: TASKS + LAYERS]
    scale = 1.0 / tokens
    grads = [grad * scale for grad in (grad_embeds, grad_one, grad_two)]
    square = small_ref[0:1, 64:65] * scale * scale
    for grad in grads:
        square = square + jnp.sum(
            jnp.sum(grad * grad, axis=1, keepdims=True), axis=0, keepdims=True
        )
    norm = jnp.sqrt(square)
    norm_ref[...] = norm
    factor = jnp.minimum(1.0, clip_limit / (norm + 1e-06))
    for index, (weight, first, second, outs) in enumerate(
        (
            (embeds, embeds_m, embeds_v, (new_embeds, new_embeds_m, new_embeds_v)),
            (one, one_m, one_v, (new_one, new_one_m, new_one_v)),
            (two, two_m, two_v, (new_two, new_two_m, new_two_v)),
        )
    ):
        for out, value in zip(
            outs,
            adamw(weight[...], first[...], second[...], grads[index] * factor, rates[index]),
        ):
            out[...] = value

    stores = []
    clip = scale * factor
    spread = stacked_left(coded_ref[...])
    for step in range(UPDATE_STEPS):
        for load in loads[step]:
            load.wait()
        columns = slice(step * block, (step + 1) * block)
        grad = mm_first(spread, stacked_right(slots_ref[:, columns])) * clip
        values = adamw(held[step, 0], held[step, 1], held[step, 2], grad, rates[3])
        for index, (array, value) in enumerate(zip((new_hyper, new_hyper_m, new_hyper_v), values)):
            fresh[step, index] = value
            stores.append(
                pltpu.make_async_copy(
                    fresh.at[step, index], array.at[:, span(step)], store_sem.at[step, index]
                )
            )
            stores[-1].start()
    for store in stores:
        store.wait()


def split(value):
    high = value.astype(jnp.bfloat16)
    rest = value - high.astype(jnp.float32)
    middle = rest.astype(jnp.bfloat16)
    return high, middle, (rest - middle.astype(jnp.float32)).astype(jnp.bfloat16)


def stacked_left(value):
    high, middle, low = split(value)
    return jnp.concatenate([high, high, middle, high, middle, low], axis=0)


def stacked_right(value):
    high, middle, low = split(value)
    return jnp.concatenate([high, middle, high, low, middle, high], axis=0)


def update(slots, small, coded, *weights):
    full = jnp.float32
    vmem = pl.BlockSpec(memory_space=pltpu.VMEM)
    whole = pl.BlockSpec(memory_space=pl.ANY)
    block = slots.shape[1] // UPDATE_STEPS
    one_value = jax.ShapeDtypeStruct((1, 1), full)
    buffer = pltpu.VMEM((UPDATE_STEPS, 3, weights[9].shape[0], block), full)
    return pl.pallas_call(
        update_kernel,
        out_shape=[one_value] * 3 + [jax.ShapeDtypeStruct(w.shape, full) for w in weights],
        in_specs=[vmem] * 12 + [whole] * 3,
        out_specs=[vmem] * 12 + [whole] * 3,
        scratch_shapes=[
            buffer,
            buffer,
            pltpu.SemaphoreType.DMA((UPDATE_STEPS, 3)),
            pltpu.SemaphoreType.DMA((UPDATE_STEPS, 3)),
        ],
        compiler_params=pltpu.CompilerParams(vmem_limit_bytes=VMEM_LIMIT),
        name="update",
    )(slots, small, coded, *weights)


def ring_rows(src_ids, tgt_ids, table):
    member = lax.axis_index("gen")
    inputs = jnp.concatenate([jnp.zeros_like(tgt_ids[:, :1]), tgt_ids[:, :-1]], axis=1)
    tokens = jnp.concatenate(
        [ids.reshape(GEN, -1) for ids in (src_ids, inputs, tgt_ids)], axis=1
    )
    ring = [(source, (source + 1) % GEN) for source in range(GEN)]

    def held(target):
        token = lax.dynamic_index_in_dim(tokens, target, 0, False) - member * table.shape[0]
        inside = (token >= 0) & (token < table.shape[0])
        rows = jnp.take(table, jnp.clip(token, 0, table.shape[0] - 1), axis=0)
        return jnp.where(inside[:, None], rows, jnp.zeros_like(rows))

    def pass_on(hop, rows):
        rows = lax.ppermute(rows, "gen", ring)
        return rows + held(lax.rem(member - 1 - hop + 2 * GEN, GEN))

    rows = lax.fori_loop(1, GEN, pass_on, held(lax.rem(member - 1 + GEN, GEN)))
    return jnp.pad(rows, ((0, table.shape[0] - rows.shape[0]), (0, 0)))


def per_device(
    src_ids,
    tgt_ids,
    task_ids,
    task_len,
    tgt_count,
    table,
    attn_w,
    ffn_in,
    ffn_out,
    gains,
    embeds,
    embeds_m,
    embeds_v,
    proj_one,
    proj_one_m,
    proj_one_v,
    proj_two,
    proj_two_m,
    proj_two_v,
    hyper,
    hyper_m,
    hyper_v,
):
    weights = (
        embeds, embeds_m, embeds_v,
        proj_one, proj_one_m, proj_one_v,
        proj_two.T, proj_two_m.T, proj_two_v.T,
        hyper, hyper_m, hyper_v,
    )
    inputs = (
        task_ids, task_len, tgt_count, src_ids, tgt_ids, embeds, proj_one, proj_two.T, gains,
        hyper, attn_w, ffn_in, ffn_out, table,
    )
    slots, small, coded, crowded = step(jnp.zeros((1,), jnp.int32), table, *inputs)

    def again(state):
        rows = ring_rows(src_ids, tgt_ids, table)
        slots, small, coded, _ = step(jnp.ones((1,), jnp.int32), rows, *inputs)
        return jnp.zeros((1,), jnp.int32), slots, small, coded

    _, slots, small, coded = lax.while_loop(
        lambda state: state[0][0] > 0, again, (crowded, slots, small, coded)
    )
    loss_sum, token_count, grad_norm, *updated = update(slots, small, coded, *weights)
    updated[6:9] = [value.T for value in updated[6:9]]
    return (loss_sum.reshape(()), token_count.reshape(()), grad_norm.reshape(()), *updated)


def solution(mesh):
    return jax.shard_map(
        per_device,
        mesh=mesh,
        in_specs=(
            P("dp", None),
            P("dp", None),
            P("dp"),
            P(),
            P("dp"),
            P("gen", None),
            P(),
            P(),
            P(),
            P(),
            P(),
            P(),
            P(),
            P(),
            P(),
            P(),
            P(),
            P(),
            P(),
            P(None, "gen"),
            P(None, "gen"),
            P(None, "gen"),
        ),
        out_specs=(
            P(),
            P(),
            P(),
            P(),
            P(),
            P(),
            P(),
            P(),
            P(),
            P(),
            P(),
            P(),
            P(None, "gen"),
            P(None, "gen"),
            P(None, "gen"),
        ),
        check_vma=False,
    )
```

time: 140 us -> 124 us (0.89); the launches traced: 140 us -> 121 us
  Pallas kernels: 129 us -> 119 us
  local copies, waits for them, and re-layouts: 9.38 us -> 0.04 us
    pallas_call x2 -> x1, Pallas kernels: 19.5 us -> 6.75 us  [update(): pl.pallas_call(update_kernel, out_shape=[one_value] * 3 + [jax.ShapeDtype...]
    unnamed x42 -> x18, local copies, waits for them, and re-layouts: 9.3 us -> 0.04 us
    pallas_call x1, Pallas kernels: 109 us -> 113 us  [step(): pl.pallas_call(step_kernel, out_shape=(jax.ShapeDtypeStruct((pairs, FLAT...]
where the time goes in v3:
time: 124 us; the launch traced here: 121 us
  Pallas kernels  119 us (96%)
    pallas_call x1, Pallas kernels, step(): pl.pallas_call(step_kernel, out_shape=(jax.ShapeDtypeStruct((pairs, FLAT...  113 us
    pallas_call x1, Pallas kernels, update(): pl.pallas_call(update_kernel, out_shape=[one_value] * 3 + [jax.ShapeDtype...  6.75 us

profile of v3, /device:TPU:1, one launch (start us, length us, event | category | flops | bytes accessed | tf_op | source)
XLA Modules:
  0.0 121.3 jit_solution(5486156173801001706)
XLA Ops:
  0.6 0.0 copy-start
  0.7 0.0 copy-start.1
  0.7 0.0 copy-start.2
  0.7 0.0 copy-start.3
  0.7 0.0 copy-start.4
  0.7 0.0 copy-start.5
  0.7 0.0 copy-start.6
  0.7 0.0 copy-start.7
  0.7 0.0 copy-start.8
  0.7 112.7 %rows_forward_vocab_backward_sum.3 = (f32[16,6144]{1,0:T(8,128)}, f32[24,128]{1,0:T(8,128)}, f32[16,64]{1,0:T(8,128)}, s32[1]{0:T(128)}) custom-call(s32[1]{0:T(128)} %constant.127.clone.1.done_ref, s32[8]{0:T(128)} %task_ref.1, s32[8]{0:T(128)} %count_ref.1, s32[1,8]{1,0:T(1,128)} %bitcast.26, s32[8,256]{1,0:T(8,128)} %src_ref.1, s32[8,128]{1,0:T(8,128)} %tgt_ref.1, ...), custom_call_target="tpu_custom_call" | custom-call | tf_op jit(solution)/shard_map/rows_forward_vocab_backward_sum/pallas_call | solution.py:1035
  113.5 0.0 copy-done
  113.5 0.0 copy-done.1
  113.5 0.0 copy-done.2
  113.5 0.0 copy-done.3
  113.5 0.0 copy-done.4
  113.5 0.0 copy-done.5
  113.5 0.0 copy-done.6
  113.5 0.0 copy-done.7
  113.5 0.0 copy-done.8
  113.5 0.8 while.27
  114.3 6.7 %update.1 = (f32[1,1]{1,0:T(1,128)}, f32[1,1]{1,0:T(1,128)}, f32[1,1]{1,0:T(1,128)}, f32[10,64]{1,0:T(8,128)}, f32[10,64]{1,0:T(8,128)}, /*index=5*/f32[10,64]{1...) custom-call(f32[16,6144]{1,0:T(8,128)} %get-tuple-element.266.slots_, ...), custom_call_target="tpu_custom_call" | custom-call | tf_op jit(solution)/shard_map/update/pallas_call | solution.py:1247
Async XLA Ops:
  0.6 112.8 %copy-start = (f32[64,128]{1,0:T(8,128)S(1)}, f32[64,128]{1,0:T(8,128)}, u32[]{:S(2)}) copy-start(f32[64,128]{1,0:T(8,128)} %one.1) | copy-start | bytes 98308
  0.7 112.8 %copy-start.1 = (f32[128,64]{0,1:T(8,128)S(1)}, f32[128,64]{0,1:T(8,128)}, u32[]{:S(2)}) copy-start(f32[128,64]{0,1:T(8,128)} %param.44) | copy-start | bytes 98308
  0.7 112.8 %copy-start.2 = (s32[8,128]{1,0:T(8,128)S(1)}, s32[8,128]{1,0:T(8,128)}, u32[]{:S(2)}) copy-start(s32[8,128]{1,0:T(8,128)} %tgt_ref.1) | copy-start | bytes 12292
  0.7 112.8 %copy-start.3 = (s32[8,256]{1,0:T(8,128)S(1)}, s32[8,256]{1,0:T(8,128)}, u32[]{:S(2)}) copy-start(s32[8,256]{1,0:T(8,128)} %src_ref.1) | copy-start | bytes 24580
  0.7 112.8 %copy-start.4 = (f32[7,512]{1,0:T(8,128)S(1)}, f32[7,512]{1,0:T(8,128)}, u32[]{:S(2)}) copy-start(f32[7,512]{1,0:T(8,128)} %gains_ref.1) | copy-start | bytes 43012
  0.7 112.8 %copy-start.5 = (f32[10,64]{1,0:T(8,128)S(1)}, f32[10,64]{1,0:T(8,128)}, u32[]{:S(2)}) copy-start(f32[10,64]{1,0:T(8,128)} %embeds.1) | copy-start | bytes 7684
  0.7 112.8 %copy-start.6 = (s32[8]{0:T(128)S(1)}, s32[8]{0:T(128)}, u32[]{:S(2)}) copy-start(s32[8]{0:T(128)} %task_ref.1) | copy-start | bytes 100
  0.7 112.8 %copy-start.7 = (s32[8]{0:T(128)S(1)}, s32[8]{0:T(128)}, u32[]{:S(2)}) copy-start(s32[8]{0:T(128)} %count_ref.1) | copy-start | bytes 100
  0.7 112.8 %copy-start.8 = (s32[8]{0:T(128)S(1)}, s32[8]{0:T(128)}, u32[]{:S(2)}) copy-start(s32[8]{0:T(128)} %param.31) | copy-start | bytes 100

commit v4 on v3

--- a/solution.py
+++ b/solution.py
@@ -21,6 +21,7 @@
 LOW = 128
 SRC_CAP = 176
 TGT_CAP = 128
+SRC_SPAN = 256
 FLAT = 48
 STEP = 5
 
@@ -41,7 +42,6 @@
 GELU_B = 0.044715
 VOCAB_TILE = 2048
 UPDATE_STEPS = 4
-WIDE = 5472
 VMEM_LIMIT = 62 * 1024 * 1024
 MESH = pl.DeviceIdType.MESH
 
@@ -118,7 +118,7 @@
     masks = [side.astype(jnp.float32).astype(jnp.bfloat16) for side in sides]
 
     def pair_step(pair, carry):
-        lanes = pl.multiple_of(pair * 128, 128)
+        lanes = pair * 128
         for seq in range(SEQ_DEV):
             q_rows = pl.ds(seq * q_len, q_len)
             k_rows = pl.ds(seq * k_len, k_len)
@@ -133,7 +133,7 @@
                 weights = jnp.exp(scores - peak)
                 probs = weights * (1.0 / jnp.sum(weights, axis=-1, keepdims=True))
                 if probs_ref is not None:
-                    begin = pl.multiple_of((pair * SEQ_DEV + seq) * q_len, 8)
+                    begin = (pair * SEQ_DEV + seq) * q_len
                     probs_ref[pl.ds(begin, q_len), half * k_len : (half + 1) * k_len] = probs
                 outs.append(mm(probs.astype(jnp.bfloat16), values))
             out_ref[q_rows, pl.ds(lanes, 128)] = jnp.where(sides[0], outs[0], outs[1]).astype(
@@ -141,7 +141,8 @@
             )
         return carry
 
-    lax.fori_loop(0, HEADS // 2, pair_step, 0)
+    for pair in range(HEADS // 2):
+        pair_step(pair, 0)
 
 
 def attend_back(grad_ref, q_ref, kv_ref, probs_ref, q_len, k_len, joined_ref):
@@ -149,7 +150,7 @@
     masks = [side.astype(jnp.float32).astype(jnp.bfloat16) for side in sides]
 
     def pair_step(pair, carry):
-        lanes = pl.multiple_of(pair * 128, 128)
+        lanes = pair * 128
         for seq in range(SEQ_DEV):
             q_rows = pl.ds(seq * q_len, q_len)
             k_rows = pl.ds(seq * k_len, k_len)
@@ -158,7 +159,7 @@
             values = kv_ref[k_rows, pl.ds(D + lanes, 128)]
             key_grads, value_grads = [], []
             for half in range(2):
-                begin = pl.multiple_of((pair * SEQ_DEV + seq) * q_len, 8)
+                begin = (pair * SEQ_DEV + seq) * q_len
                 probs = probs_ref[pl.ds(begin, q_len), half * k_len : (half + 1) * k_len]
                 grad_probs = mm_last(grad * masks[half], values)
                 value_grads.append(mm_first(probs.astype(jnp.bfloat16), grad))
@@ -173,7 +174,8 @@
             ).astype(jnp.bfloat16)
         return carry
 
-    lax.fori_loop(0, HEADS // 2, pair_step, 0)
+    for pair in range(HEADS // 2):
+        pair_step(pair, 0)
 
 
 def feed(state_ref, gain, inner_ref, outer_ref, act_ref, slope_ref, down_ref, up_ref, length,
@@ -228,18 +230,14 @@
     )
 
 
-def place_rows(src_ref, tgt_ref, member, peer, part, done):
+def place_rows(src_ref, tgt_ref, member, peer, part, done, index_vmem):
     offset = member * part
-    wide_tokens = SEQ_DEV * SRC
-    order = lax.broadcasted_iota(jnp.int32, (wide_tokens, wide_tokens), 0)
-    upto = (
-        (order <= lax.broadcasted_iota(jnp.int32, (wide_tokens, wide_tokens), 1))
-        .astype(jnp.float32)
-        .astype(jnp.bfloat16)
-    )
     crowded = jnp.zeros((1, 1), jnp.float32)
-    slots, wanted = [], []
-    for ids_ref, length, rows in ((src_ref, SRC, SRC_CAP), (tgt_ref, TGT, TGT_CAP)):
+    slots = []
+    for ids_ref, length, rows, begin in (
+        (src_ref, SRC, SRC_CAP, 0),
+        (tgt_ref, TGT, TGT_CAP, SRC_SPAN),
+    ):
         count = SEQ_DEV * length
         ids = jnp.concatenate(
             [
@@ -256,32 +254,37 @@
             count = count + 128
         own = ids[0:1]
         local = ids - offset
-        inside = ((local >= 0) & (local < part) & (ids >= 0)).astype(jnp.float32)
-        held = [
-            ((own >= part * o) & (own < part * (o + 1))).astype(jnp.float32) for o in range(GEN)
-        ]
-        marks = jnp.concatenate([inside] + held, axis=0)
-        ranks = mm(marks.astype(jnp.bfloat16), upto[:count, :count]) - 1.0
-        ranks = ranks - (done * count).astype(jnp.float32)
+        inside = ((local >= 0) & (local < part) & (ids >= 0)).astype(jnp.int32)
+        held = [((own >= part * o) & (own < part * (o + 1))).astype(jnp.int32) for o in range(GEN)]
+        ranks = jnp.concatenate([inside] + held, axis=0)
+        lane = lax.broadcasted_iota(jnp.int32, ranks.shape, 1)
+        reach = 1
+        while reach < count:
+            ranks = ranks + jnp.where(lane >= reach, pltpu.roll(ranks, reach, axis=1), 0)
+            reach = 2 * reach
+        ranks = ranks - 1 - done * count
         for o in range(GEN):
             amount = ((ids >= part * o) & (ids < part * (o + 1))).astype(jnp.float32)
             most = jnp.max(jnp.sum(amount, axis=1, keepdims=True), axis=0, keepdims=True)
             crowded = jnp.maximum(crowded, (most > float(rows)).astype(jnp.float32))
-        numbers = local.astype(jnp.float32) + 1.0
-        spot = lax.broadcasted_iota(jnp.int32, (rows, count), 0).astype(jnp.float32)
-        columns = []
+        spot = lax.broadcasted_iota(jnp.int32, (rows, count), 0)
+        span = (rows + 127) // 128 * 128
+        same = lax.broadcasted_iota(jnp.int32, (rows, span), 0) == lax.broadcasted_iota(
+            jnp.int32, (rows, span), 1
+        )
         for k in range(GEN):
-            position = jnp.where(inside[k : k + 1] > 0.0, ranks[k : k + 1], -1.0)
-            columns.append(
-                jnp.sum(jnp.where(spot == position, numbers[k : k + 1], 0.0), axis=1, keepdims=True)
-                - 1.0
+            position = jnp.where(inside[k : k + 1] > 0, ranks[k : k + 1], -1)
+            numbers = jnp.sum(
+                jnp.where(spot == position, local[k : k + 1], 0), axis=1, keepdims=True
             )
-        wanted.append(columns)
+            index_vmem[k : k + 1, begin : begin + span] = jnp.sum(
+                jnp.where(same, numbers, 0), axis=0, keepdims=True
+            )
         slot = jnp.full((1, count), -1.0, jnp.float32)
         for o in range(GEN):
             rank = ranks[GEN + o : GEN + o + 1]
-            now = (held[o] > 0.0) & (rank >= 0.0) & (rank < float(rows))
-            slot = jnp.where(now, rank + float(o * rows), slot)
+            now = (held[o] > 0) & (rank >= 0) & (rank < rows)
+            slot = jnp.where(now, (rank + o * rows).astype(jnp.float32), slot)
         slots.append(slot)
     targets = SEQ_DEV * TGT
     lane = lax.broadcasted_iota(jnp.int32, (1, targets), 1)
@@ -290,7 +293,7 @@
         slots[1][:, targets : targets + 1],
         pltpu.roll(slots[1][:, :targets], 1, axis=1),
     )
-    return wanted, slots[0], shifted, slots[1][:, :targets], crowded
+    return slots[0], shifted, slots[1][:, :targets], crowded
 
 
 def describe(task_ref, lens_ref, count_ref, member):
@@ -320,7 +323,7 @@
         ((1,), (1,)),
     )
     coded_ref[...] = coded
-    flat = exact(coded, hyper_ref[...], ((1,), (0,))).astype(jnp.bfloat16)
+    flat = mm(stacked_left(coded, 1), stacked_right(hyper_ref[...])).astype(jnp.bfloat16)
     pairs = TASKS * LAYERS
     sequences = GEN * SEQ_DEV
     row_of = lax.broadcasted_iota(jnp.int32, (pairs, pairs), 0)
@@ -375,14 +378,13 @@
     qkv,
     mixed,
     act,
-    memory,
-    q_cross,
-    plain_d,
     feats,
     stats,
     stats_in,
-    grad_low,
     rows_out,
+    picked_rows,
+    index_vmem,
+    index,
     known,
     src_in,
     tgt_in,
@@ -414,6 +416,7 @@
     small_send,
     small_recv,
     verdict_sem,
+    index_sem,
     feat_send,
     feat_recv,
     result_send,
@@ -457,6 +460,10 @@
     def flat_in(owner):
         return generated.at[pl.ds(owner * SEQ_DEV * LAYERS * FLAT, SEQ_DEV * LAYERS * FLAT)]
 
+    memory = inner.at[0, :, pl.ds(0, D)]
+    q_cross = attn.at[1, pl.ds(0, targets), pl.ds(0, D)]
+    plain_d = attn.at[1, pl.ds(targets, targets), pl.ds(0, D)]
+    grad_low = attn.at[1, pl.ds(0, targets), pl.ds(D, D)]
     kv_cross = attn.at[0, :, pl.ds(0, 2 * D)]
     joined = attn.at[0, :, pl.ds(2 * D, 2 * D)]
 
@@ -516,26 +523,36 @@
         )
     ]
 
-    (source_rows, target_rows), source_slot, input_slot, target_slot, crowded = place_rows(
-        src_ref, tgt_ref, member, peer, part, done_ref[0]
-    )
-
-    def gather(columns, begin, orders, first=False):
-        numbers = jnp.concatenate([columns[order] for order in orders], axis=0)
-        height = numbers.shape[0]
-        found = None
-        for i in range(len(cuts) - 1):
-            if first:
-                table_loads[i].wait()
-            lane = lax.broadcasted_iota(jnp.int32, (height, cuts[i + 1] - cuts[i]), 1)
-            hit = ((lane + cuts[i]).astype(jnp.float32) == numbers).astype(jnp.float32)
-            piece = mm(hit.astype(jnp.bfloat16), table[cuts[i] : cuts[i + 1], :])
-            found = piece if found is None else found + piece
-        size = height // len(orders)
-        for place, order in enumerate(orders):
-            rows_out[peer(order), pl.ds(begin, size), :] = found[
-                place * size : (place + 1) * size
-            ].astype(jnp.bfloat16)
+    source_slot, input_slot, target_slot, crowded = place_rows(
+        src_ref, tgt_ref, member, peer, part, done_ref[0], index_vmem
+    )
+    index_copy = pltpu.make_async_copy(index_vmem, index, index_sem)
+    index_copy.start()
+    chunk = 32
+    for i in range(len(cuts) - 1):
+        table_loads[i].wait()
+
+        def widen(step, carry):
+            begin = pl.multiple_of(cuts[i] + step * chunk, chunk)
+            wide[pl.ds(begin, chunk), :] = table[pl.ds(begin, chunk), :].astype(jnp.float32)
+            return carry
+
+        lax.fori_loop(0, (cuts[i + 1] - cuts[i]) // chunk, widen, 0)
+    index_copy.wait()
+
+    def gather(order, begin, first, size):
+        def fetch(step, carry):
+            place = pl.multiple_of(step * 16, 16)
+            for k in range(16):
+                picked_rows[pl.ds(place + k, 1), :] = wide[
+                    pl.ds(index[order, first + place + k], 1), :
+                ]
+            return carry
+
+        lax.fori_loop(0, size // 16, fetch, 0)
+        rows_out[peer(order), pl.ds(begin, size), :] = picked_rows[pl.ds(0, size), :].astype(
+            jnp.bfloat16
+        )
 
     def source_copy(owner, target):
         return pltpu.make_async_remote_copy(
@@ -568,21 +585,23 @@
         )
 
     pl.semaphore_wait(barrier, GEN + count - 2)
-    gather(source_rows, 0, (1, 2), True)
     for order in (1, 2):
+        gather(order, 0, 0, SRC_CAP)
         source_copy(member, peer(order)).start()
     hyper_load.wait()
     generate(task_ref, embeds_ref, one_ref, two_ref, hyper, coded_ref, generated, adapters_ref,
              sel_ref)
     for order in range(1, GEN):
         adapter_copy(member, peer(order)).start()
-    gather(target_rows, SRC_CAP, (1, 2))
     for order in (1, 2):
+        gather(order, SRC_CAP, SRC_SPAN, TGT_CAP)
         target_copy(member, peer(order)).start()
-    gather(source_rows, 0, (3, 0))
+    gather(3, 0, 0, SRC_CAP)
     source_copy(member, peer(3)).start()
-    gather(target_rows, SRC_CAP, (3, 0))
+    gather(3, SRC_CAP, SRC_SPAN, TGT_CAP)
     target_copy(member, peer(3)).start()
+    gather(0, 0, 0, SRC_CAP)
+    gather(0, SRC_CAP, SRC_SPAN, TGT_CAP)
     src_in[member] = rows_out[member, 0:SRC_CAP, :]
     tgt_in[member] = rows_out[member, SRC_CAP : SRC_CAP + TGT_CAP, :]
     adapters_in[member] = adapters_ref[member]
@@ -821,16 +840,19 @@
     received = jnp.concatenate(
         [grads_in[pl.ds(tile, pairs, stride=FLAT), :] for tile in range(FLAT)], axis=1
     )
-    slots = exact(sel_ref[...], received, ((1,), (0,)))
-
-    padded = outgoing.shape[2]
+    chosen = sel_ref[...].astype(jnp.bfloat16)
+    slots = mm(
+        jnp.concatenate([chosen] * 3, axis=1), jnp.concatenate(split(received), axis=0)
+    )
+
+    padded = (width + 127) // 128 * 128
     for piece in range(count):
         low_edge = piece * width // 128 * 128
         shift = piece * width - low_edge
         window = slots[:, low_edge : low_edge + padded]
         if shift:
             window = pltpu.roll(window, padded - shift, axis=1)
-        outgoing[piece] = window
+        outgoing[piece] = packed(window, width)
 
     def scatter(step, carry):
         target = lax.rem(rank + step, count)
@@ -878,8 +900,7 @@
         summed = summed + incoming[source]
     shares[rank] = summed
 
-    window_lane = lax.broadcasted_iota(jnp.int32, (1, padded), 1)
-    piece_rows = jnp.where(window_lane < width, summed, 0.0)
+    piece_rows = unpacked(summed, width)
     shift = lax.rem(rank * width, 128)
     if width % 128:
         piece_rows = jnp.where(
@@ -929,9 +950,9 @@
     wait_all(outgoing, scatter_sem.at[0])
     wait_all(shares, share_sem.at[1])
     for piece in range(0, count, 2 if width % 128 else 1):
-        first = shares[piece]
+        first = unpacked(shares[piece], width)
         if width % 128:
-            second = pltpu.roll(shares[piece + 1], width % 128, axis=1)
+            second = pltpu.roll(unpacked(shares[piece + 1], width), width % 128, axis=1)
             middle = width // 128 * 128
             begin = piece * width
             lane128 = lax.broadcasted_iota(jnp.int32, (1, 128), 1)
@@ -952,6 +973,27 @@
     missing_ref[0] = jnp.max(result[16:17, 2:3]).astype(jnp.int32)
     wait_all(shares, share_sem.at[0])
     wait_all(verdict_in, verdict_sem.at[0])
+
+
+def packed(window, width):
+    tiles = [window[:, 128 * i : 128 * (i + 1)] for i in range(width // 128)]
+    if width % 128:
+        rest = window[:, width // 128 * 128 :]
+        rows = rest.shape[0] // 2
+        lane = lax.broadcasted_iota(jnp.int32, (1, 128), 1)
+        tiles.append(jnp.where(lane < 64, rest[:rows], pltpu.roll(rest[rows:], 64, axis=1)))
+    return jnp.concatenate(tiles, axis=0)
+
+
+def unpacked(rows, width):
+    pairs = TASKS * LAYERS
+    tiles = [rows[pairs * i : pairs * (i + 1)] for i in range(width // 128)]
+    if width % 128:
+        rest = rows[width // 128 * pairs :]
+        lane = lax.broadcasted_iota(jnp.int32, (1, 128), 1)
+        both = jnp.concatenate([rest, pltpu.roll(rest, 64, axis=1)], axis=0)
+        tiles.append(jnp.where(lane < 64, both, 0.0))
+    return jnp.concatenate(tiles, axis=1)
 
 
 def unpack_adapters(entries, flat, spread, down_ref, up_ref):
@@ -1030,7 +1072,6 @@
     pairs = TASKS * LAYERS
     count = lax.axis_size("dp")
     width = FLAT * 128 // count
-    padded = (width + 127) // 128 * 128
     dma = pltpu.SemaphoreType.DMA
     return pl.pallas_call(
         step_kernel,
@@ -1047,19 +1088,18 @@
             pltpu.VMEM(ffn_in.shape, low),
             pltpu.VMEM(ffn_out.shape, low),
             pltpu.VMEM(table.shape, low),
-            pltpu.VMEM((WIDE, D), full),
+            pltpu.VMEM(table.shape, full),
             pltpu.VMEM((sources, D), low),
             pltpu.VMEM((sources, 3 * D), low),
             pltpu.VMEM((sources, D), low),
             pltpu.VMEM((sources, FF), low),
-            pltpu.VMEM((sources, D), low),
-            pltpu.VMEM((targets, D), low),
-            pltpu.VMEM((targets, D), low),
             pltpu.VMEM((GEN, targets, D), low),
             pltpu.VMEM((GEN, 8, targets), full),
             pltpu.VMEM((GEN, 8, targets), full),
-            pltpu.VMEM((targets, D), low),
             pltpu.VMEM((GEN, SRC_CAP + TGT_CAP, D), low),
+            pltpu.VMEM((SRC_CAP, D), full),
+            pltpu.VMEM((8, 384), jnp.int32),
+            pltpu.SMEM((8, 384), jnp.int32),
             pltpu.VMEM((sources + 2 * targets, D), low),
             pltpu.VMEM((GEN, SRC_CAP, D), low),
             pltpu.VMEM((GEN, TGT_CAP, D), low),
@@ -1073,9 +1113,9 @@
             pltpu.VMEM((LAYERS, GEN, SEQ_DEV * FLAT, 128), full),
             pltpu.VMEM((LAYERS * GEN * SEQ_DEV * FLAT, 128), full),
             pltpu.VMEM(hyper.shape, full),
-            pltpu.VMEM((count, pairs, padded), full),
-            pltpu.VMEM((count, pairs, padded), full),
-            pltpu.VMEM((count, pairs, padded), full),
+            pltpu.VMEM((count, pairs * width // 128, 128), full),
+            pltpu.VMEM((count, pairs * width // 128, 128), full),
+            pltpu.VMEM((count, pairs * width // 128, 128), full),
             pltpu.VMEM((24, 128), full),
             pltpu.VMEM((GEN, 24, 128), full),
             pltpu.VMEM((count, 24, 128), full),
@@ -1091,6 +1131,7 @@
             dma((GEN,)),
             dma((GEN,)),
             dma((2,)),
+            dma,
             dma((GEN,)),
             dma((GEN,)),
             dma((GEN,)),
@@ -1163,6 +1204,10 @@
     tokens = small_ref[16:17, 1:2]
     loss_ref[...] = small_ref[16:17, 0:1]
     tokens_ref[...] = tokens
+    spread = stacked_left(coded_ref[...])
+    for step in range(UPDATE_STEPS):
+        columns = slice(step * block, (step + 1) * block)
+        fresh[step, 0] = mm_first(spread, stacked_right(slots_ref[:, columns]))
     pairs = pair_rows(embeds[...])
     before = exact(pairs, one[...], ((1,), (0,)))
     tanh = gelu_tanh(before)
@@ -1201,12 +1246,10 @@
 
     stores = []
     clip = scale * factor
-    spread = stacked_left(coded_ref[...])
     for step in range(UPDATE_STEPS):
         for load in loads[step]:
             load.wait()
-        columns = slice(step * block, (step + 1) * block)
-        grad = mm_first(spread, stacked_right(slots_ref[:, columns])) * clip
+        grad = fresh[step, 0] * clip
         values = adamw(held[step, 0], held[step, 1], held[step, 2], grad, rates[3])
         for index, (array, value) in enumerate(zip((new_hyper, new_hyper_m, new_hyper_v), values)):
             fresh[step, index] = value
@@ -1227,9 +1270,9 @@
     return high, middle, (rest - middle.astype(jnp.float32)).astype(jnp.bfloat16)
 
 
-def stacked_left(value):
+def stacked_left(value, axis=0):
     high, middle, low = split(value)
-    return jnp.concatenate([high, high, middle, high, middle, low], axis=0)
+    return jnp.concatenate([high, high, middle, high, middle, low], axis=axis)
 
 
 def stacked_right(value):

time: 124 us -> 108 us (0.87); the launches traced: 121 us -> 108 us
  Pallas kernels: 119 us -> 106 us
    pallas_call x1, Pallas kernels: 113 us -> 99.4 us  [step(): pl.pallas_call(step_kernel, out_shape=(jax.ShapeDtypeStruct((pairs, FLAT...]
where the time goes in v4:
time: 108 us
  Pallas kernels  106 us (98%)
    pallas_call x1, Pallas kernels, step(): pl.pallas_call(step_kernel, out_shape=(jax.ShapeDtypeStruct((pairs, FLAT...  99.4 us
    pallas_call x1, Pallas kernels, update(): pl.pallas_call(update_kernel, out_shape=[one_value] * 3 + [jax.ShapeDtype...  6.44 us

profile of v4, /device:TPU:1, one launch (start us, length us, event | category | flops | bytes accessed | tf_op | source)
XLA Modules:
  0.0 107.6 jit_solution(2814514313460270680)
XLA Ops:
  0.6 0.0 copy-start
  0.7 0.0 copy-start.1
  0.7 0.0 copy-start.2
  0.7 0.0 copy-start.3
  0.7 0.0 copy-start.4
  0.7 0.0 copy-start.5
  0.7 0.0 copy-start.6
  0.7 0.0 copy-start.7
  0.7 0.0 copy-start.8
  0.7 99.4 %rows_forward_vocab_backward_sum.3 = (f32[16,6144]{1,0:T(8,128)}, f32[24,128]{1,0:T(8,128)}, f32[16,64]{1,0:T(8,128)}, s32[1]{0:T(128)}) custom-call(s32[1]{0:T(128)} %constant.127.clone.1.done_ref, s32[8]{0:T(128)} %task_ref.1, s32[8]{0:T(128)} %count_ref.1, s32[1,8]{1,0:T(1,128)} %bitcast.26, s32[8,256]{1,0:T(8,128)} %src_ref.1, s32[8,128]{1,0:T(8,128)} %tgt_ref.1, ...), custom_call_target="tpu_custom_call" | custom-call | tf_op jit(solution)/shard_map/rows_forward_vocab_backward_sum/pallas_call | solution.py:1076
  100.1 0.0 copy-done
  100.1 0.0 copy-done.1
  100.1 0.0 copy-done.2
  100.2 0.0 copy-done.3
  100.2 0.0 copy-done.4
  100.2 0.0 copy-done.5
  100.2 0.0 copy-done.6
  100.2 0.0 copy-done.7
  100.2 0.0 copy-done.8
  100.2 0.8 while.27
  101.0 6.4 %update.1 = (f32[1,1]{1,0:T(1,128)}, f32[1,1]{1,0:T(1,128)}, f32[1,1]{1,0:T(1,128)}, f32[10,64]{1,0:T(8,128)}, f32[10,64]{1,0:T(8,128)}, /*index=5*/f32[10,64]{1...) custom-call(f32[16,6144]{1,0:T(8,128)} %get-tuple-element.266.slots_, ...), custom_call_target="tpu_custom_call" | custom-call | tf_op jit(solution)/shard_map/update/pallas_call | solution.py:1290
Async XLA Ops:
  0.6 99.5 %copy-start = (f32[64,128]{1,0:T(8,128)S(1)}, f32[64,128]{1,0:T(8,128)}, u32[]{:S(2)}) copy-start(f32[64,128]{1,0:T(8,128)} %one.1) | copy-start | bytes 98308
  0.7 99.5 %copy-start.1 = (f32[128,64]{0,1:T(8,128)S(1)}, f32[128,64]{0,1:T(8,128)}, u32[]{:S(2)}) copy-start(f32[128,64]{0,1:T(8,128)} %param.44) | copy-start | bytes 98308
  0.7 99.5 %copy-start.2 = (s32[8,128]{1,0:T(8,128)S(1)}, s32[8,128]{1,0:T(8,128)}, u32[]{:S(2)}) copy-start(s32[8,128]{1,0:T(8,128)} %tgt_ref.1) | copy-start | bytes 12292
  0.7 99.5 %copy-start.3 = (s32[8,256]{1,0:T(8,128)S(1)}, s32[8,256]{1,0:T(8,128)}, u32[]{:S(2)}) copy-start(s32[8,256]{1,0:T(8,128)} %src_ref.1) | copy-start | bytes 24580
  0.7 99.5 %copy-start.4 = (f32[7,512]{1,0:T(8,128)S(1)}, f32[7,512]{1,0:T(8,128)}, u32[]{:S(2)}) copy-start(f32[7,512]{1,0:T(8,128)} %gains_ref.1) | copy-start | bytes 43012
  0.7 99.5 %copy-start.5 = (f32[10,64]{1,0:T(8,128)S(1)}, f32[10,64]{1,0:T(8,128)}, u32[]{:S(2)}) copy-start(f32[10,64]{1,0:T(8,128)} %embeds.1) | copy-start | bytes 7684
  0.7 99.5 %copy-start.6 = (s32[8]{0:T(128)S(1)}, s32[8]{0:T(128)}, u32[]{:S(2)}) copy-start(s32[8]{0:T(128)} %task_ref.1) | copy-start | bytes 100
  0.7 99.5 %copy-start.7 = (s32[8]{0:T(128)S(1)}, s32[8]{0:T(128)}, u32[]{:S(2)}) copy-start(s32[8]{0:T(128)} %count_ref.1) | copy-start | bytes 100
  0.7 99.5 %copy-start.8 = (s32[8]{0:T(128)S(1)}, s32[8]{0:T(128)}, u32[]{:S(2)}) copy-start(s32[8]{0:T(128)} %param.31) | copy-start | bytes 100

commit v5 on v4

--- a/solution.py
+++ b/solution.py
@@ -20,7 +20,7 @@
 GEN = 4
 LOW = 128
 SRC_CAP = 176
-TGT_CAP = 128
+TGT_CAP = 64
 SRC_SPAN = 256
 FLAT = 48
 STEP = 5
@@ -42,7 +42,7 @@
 GELU_B = 0.044715
 VOCAB_TILE = 2048
 UPDATE_STEPS = 4
-VMEM_LIMIT = 62 * 1024 * 1024
+VMEM_LIMIT = 63 * 1024 * 1024
 MESH = pl.DeviceIdType.MESH
 
 
@@ -230,70 +230,78 @@
     )
 
 
-def place_rows(src_ref, tgt_ref, member, peer, part, done, index_vmem):
-    offset = member * part
+def rank_tokens(ids_ref, peer, member, part, done):
+    length = ids_ref.shape[1]
+    ids = jnp.concatenate(
+        [
+            jnp.concatenate(
+                [ids_ref[pl.ds(SEQ_DEV * peer(k) + s, 1), :] for s in range(SEQ_DEV)], axis=1
+            )
+            for k in range(GEN)
+        ],
+        axis=0,
+    )
+    if length == TGT:
+        lane = lax.broadcasted_iota(jnp.int32, (GEN, 128), 1)
+        ids = jnp.concatenate([ids, jnp.where(lane == 0, 0, -1)], axis=1)
+    count = ids.shape[1]
+    own = ids[0:1]
+    local = ids - member * part
+    inside = ((local >= 0) & (local < part) & (ids >= 0)).astype(jnp.int32)
+    held = [((own >= part * o) & (own < part * (o + 1))).astype(jnp.int32) for o in range(GEN)]
+    lane = lax.broadcasted_iota(jnp.int32, ids.shape, 1)
+    fresh = ((lax.rem(lane, length) == 0) | (ids != pltpu.roll(ids, 1, axis=1))).astype(jnp.int32)
+    inside = inside * fresh
+    ranks = jnp.concatenate([inside] + [mark * fresh[0:1] for mark in held], axis=0)
+    lane = lax.broadcasted_iota(jnp.int32, ranks.shape, 1)
+    reach = 1
+    while reach < count:
+        ranks = ranks + jnp.where(lane >= reach, pltpu.roll(ranks, reach, axis=1), 0)
+        reach = 2 * reach
+    return ids, local, inside, held, ranks - 1 - done * count, fresh
+
+
+def row_numbers(ranked, peer_order, rows):
+    _, local, inside, _, ranks, _ = ranked
+    k = peer_order
+    spot = lax.broadcasted_iota(jnp.int32, (rows, local.shape[1]), 0)
+    position = jnp.where(inside[k : k + 1] > 0, ranks[k : k + 1], -1)
+    return jnp.sum(jnp.where(spot == position, local[k : k + 1], 0), axis=1, keepdims=True)
+
+
+def list_rows(ranked, rows, begin, index_vmem):
+    span = (rows + 127) // 128 * 128
+    same = lax.broadcasted_iota(jnp.int32, (rows, span), 0) == lax.broadcasted_iota(
+        jnp.int32, (rows, span), 1
+    )
+    for k in range(GEN):
+        index_vmem[k : k + 1, begin : begin + span] = jnp.sum(
+            jnp.where(same, row_numbers(ranked, k, rows), 0), axis=0, keepdims=True
+        )
+
+
+def token_places(ranked, rows, part):
+    ids, _, _, held, ranks, fresh = ranked
+    slot = jnp.full((1, ids.shape[1]), -1.0, jnp.float32)
     crowded = jnp.zeros((1, 1), jnp.float32)
-    slots = []
-    for ids_ref, length, rows, begin in (
-        (src_ref, SRC, SRC_CAP, 0),
-        (tgt_ref, TGT, TGT_CAP, SRC_SPAN),
-    ):
-        count = SEQ_DEV * length
-        ids = jnp.concatenate(
-            [
-                jnp.concatenate(
-                    [ids_ref[pl.ds(SEQ_DEV * peer(k) + s, 1), :] for s in range(SEQ_DEV)], axis=1
-                )
-                for k in range(GEN)
-            ],
-            axis=0,
-        )
-        if length == TGT:
-            lane = lax.broadcasted_iota(jnp.int32, (GEN, 128), 1)
-            ids = jnp.concatenate([ids, jnp.where(lane == 0, 0, -1)], axis=1)
-            count = count + 128
-        own = ids[0:1]
-        local = ids - offset
-        inside = ((local >= 0) & (local < part) & (ids >= 0)).astype(jnp.int32)
-        held = [((own >= part * o) & (own < part * (o + 1))).astype(jnp.int32) for o in range(GEN)]
-        ranks = jnp.concatenate([inside] + held, axis=0)
-        lane = lax.broadcasted_iota(jnp.int32, ranks.shape, 1)
-        reach = 1
-        while reach < count:
-            ranks = ranks + jnp.where(lane >= reach, pltpu.roll(ranks, reach, axis=1), 0)
-            reach = 2 * reach
-        ranks = ranks - 1 - done * count
-        for o in range(GEN):
-            amount = ((ids >= part * o) & (ids < part * (o + 1))).astype(jnp.float32)
-            most = jnp.max(jnp.sum(amount, axis=1, keepdims=True), axis=0, keepdims=True)
-            crowded = jnp.maximum(crowded, (most > float(rows)).astype(jnp.float32))
-        spot = lax.broadcasted_iota(jnp.int32, (rows, count), 0)
-        span = (rows + 127) // 128 * 128
-        same = lax.broadcasted_iota(jnp.int32, (rows, span), 0) == lax.broadcasted_iota(
-            jnp.int32, (rows, span), 1
-        )
-        for k in range(GEN):
-            position = jnp.where(inside[k : k + 1] > 0, ranks[k : k + 1], -1)
-            numbers = jnp.sum(
-                jnp.where(spot == position, local[k : k + 1], 0), axis=1, keepdims=True
-            )
-            index_vmem[k : k + 1, begin : begin + span] = jnp.sum(
-                jnp.where(same, numbers, 0), axis=0, keepdims=True
-            )
-        slot = jnp.full((1, count), -1.0, jnp.float32)
-        for o in range(GEN):
-            rank = ranks[GEN + o : GEN + o + 1]
-            now = (held[o] > 0) & (rank >= 0) & (rank < rows)
-            slot = jnp.where(now, (rank + o * rows).astype(jnp.float32), slot)
-        slots.append(slot)
+    for o in range(GEN):
+        amount = ((ids >= part * o) & (ids < part * (o + 1)) & (fresh > 0)).astype(jnp.float32)
+        most = jnp.max(jnp.sum(amount, axis=1, keepdims=True), axis=0, keepdims=True)
+        crowded = jnp.maximum(crowded, (most > float(rows)).astype(jnp.float32))
+        rank = ranks[GEN + o : GEN + o + 1]
+        now = (held[o] > 0) & (rank >= 0) & (rank < rows)
+        slot = jnp.where(now, (rank + o * rows).astype(jnp.float32), slot)
+    return slot, crowded
+
+
+def after_zero(slot):
     targets = SEQ_DEV * TGT
     lane = lax.broadcasted_iota(jnp.int32, (1, targets), 1)
-    shifted = jnp.where(
+    return jnp.where(
         lax.rem(lane, TGT) == 0,
-        slots[1][:, targets : targets + 1],
-        pltpu.roll(slots[1][:, :targets], 1, axis=1),
-    )
-    return slots[0], shifted, slots[1][:, :targets], crowded
+        slot[:, targets : targets + 1],
+        pltpu.roll(slot[:, :targets], 1, axis=1),
+    )
 
 
 def describe(task_ref, lens_ref, count_ref, member):
@@ -396,6 +404,8 @@
     down_ref,
     up_ref,
     pack,
+    pack_low,
+    grads_low_in,
     grads_in,
     hyper,
     outgoing,
@@ -503,13 +513,10 @@
             barrier, inc=1, device_id={"gen": peer(order)}, device_id_type=MESH
         )
 
-    def greet(step, carry):
+    for step in range(1, count):
         pl.semaphore_signal(
             barrier, inc=1, device_id={"dp": lax.rem(rank + step, count)}, device_id_type=MESH
         )
-        return carry
-
-    lax.fori_loop(1, count, greet, 0)
     weight_loads = [
         load(source, target)
         for source, target in (
@@ -523,14 +530,56 @@
         )
     ]
 
-    source_slot, input_slot, target_slot, crowded = place_rows(
-        src_ref, tgt_ref, member, peer, part, done_ref[0], index_vmem
-    )
+    def source_copy(owner, target):
+        return pltpu.make_async_remote_copy(
+            src_ref=rows_out.at[target, pl.ds(0, SRC_CAP)],
+            dst_ref=src_in.at[owner],
+            send_sem=row_send.at[0, target],
+            recv_sem=src_recv.at[owner],
+            device_id={"gen": target},
+            device_id_type=MESH,
+        )
+
+    def target_copy(owner, target):
+        return pltpu.make_async_remote_copy(
+            src_ref=rows_out.at[target, pl.ds(SRC_CAP, TGT_CAP)],
+            dst_ref=tgt_in.at[owner],
+            send_sem=row_send.at[1, target],
+            recv_sem=tgt_recv.at[owner],
+            device_id={"gen": target},
+            device_id_type=MESH,
+        )
+
+    def adapter_copy(owner, target):
+        return pltpu.make_async_remote_copy(
+            src_ref=adapters_ref.at[target],
+            dst_ref=adapters_in.at[owner],
+            send_sem=row_send.at[2, target],
+            recv_sem=adapter_recv.at[owner],
+            device_id={"gen": target},
+            device_id_type=MESH,
+        )
+
+    sources_ranked = rank_tokens(src_ref, peer, member, part, done_ref[0])
+    numbers = row_numbers(sources_ranked, 1, SRC_CAP)
+    found = None
+    for i in range(len(cuts) - 1):
+        lane = lax.broadcasted_iota(jnp.int32, (SRC_CAP, cuts[i + 1] - cuts[i]), 1)
+        hit = (lane + cuts[i] == numbers).astype(jnp.float32).astype(jnp.bfloat16)
+        table_loads[i].wait()
+        piece = mm(hit, table[cuts[i] : cuts[i + 1], :])
+        found = piece if found is None else found + piece
+    rows_out[peer(1), pl.ds(0, SRC_CAP), :] = found.astype(jnp.bfloat16)
+    pl.semaphore_wait(barrier, GEN + count - 2)
+    source_copy(member, peer(1)).start()
+
+    targets_ranked = rank_tokens(tgt_ref, peer, member, part, done_ref[0])
+    list_rows(sources_ranked, SRC_CAP, 0, index_vmem)
+    list_rows(targets_ranked, TGT_CAP, SRC_SPAN, index_vmem)
     index_copy = pltpu.make_async_copy(index_vmem, index, index_sem)
     index_copy.start()
     chunk = 32
     for i in range(len(cuts) - 1):
-        table_loads[i].wait()
 
         def widen(step, carry):
             begin = pl.multiple_of(cuts[i] + step * chunk, chunk)
@@ -554,40 +603,8 @@
             jnp.bfloat16
         )
 
-    def source_copy(owner, target):
-        return pltpu.make_async_remote_copy(
-            src_ref=rows_out.at[target, pl.ds(0, SRC_CAP)],
-            dst_ref=src_in.at[owner],
-            send_sem=row_send.at[0, target],
-            recv_sem=src_recv.at[owner],
-            device_id={"gen": target},
-            device_id_type=MESH,
-        )
-
-    def target_copy(owner, target):
-        return pltpu.make_async_remote_copy(
-            src_ref=rows_out.at[target, pl.ds(SRC_CAP, TGT_CAP)],
-            dst_ref=tgt_in.at[owner],
-            send_sem=row_send.at[1, target],
-            recv_sem=tgt_recv.at[owner],
-            device_id={"gen": target},
-            device_id_type=MESH,
-        )
-
-    def adapter_copy(owner, target):
-        return pltpu.make_async_remote_copy(
-            src_ref=adapters_ref.at[target],
-            dst_ref=adapters_in.at[owner],
-            send_sem=row_send.at[2, target],
-            recv_sem=adapter_recv.at[owner],
-            device_id={"gen": target},
-            device_id_type=MESH,
-        )
-
-    pl.semaphore_wait(barrier, GEN + count - 2)
-    for order in (1, 2):
-        gather(order, 0, 0, SRC_CAP)
-        source_copy(member, peer(order)).start()
+    gather(2, 0, 0, SRC_CAP)
+    source_copy(member, peer(2)).start()
     hyper_load.wait()
     generate(task_ref, embeds_ref, one_ref, two_ref, hyper, coded_ref, generated, adapters_ref,
              sel_ref)
@@ -605,14 +622,19 @@
     src_in[member] = rows_out[member, 0:SRC_CAP, :]
     tgt_in[member] = rows_out[member, SRC_CAP : SRC_CAP + TGT_CAP, :]
     adapters_in[member] = adapters_ref[member]
+    source_slot, crowded_sources = token_places(sources_ranked, SRC_CAP, part)
+    target_slot, crowded_targets = token_places(targets_ranked, TGT_CAP, part)
+    input_slot, target_slot = after_zero(target_slot), target_slot[:, :targets]
+    crowded = jnp.maximum(crowded_sources, crowded_targets)
     allow, valid, tokens = describe(task_ref, lens_ref, count_ref, member)
 
-    def spread_rows(slot, incoming_rows, owner):
+    def spread_rows(slot, incoming_rows, first, owners):
         height = incoming_rows.shape[1]
-        spot = lax.broadcasted_iota(jnp.int32, (height, slot.shape[1]), 0)
-        spot = (spot + owner * height).astype(jnp.float32)
-        chosen = (spot == slot).astype(jnp.float32)
-        return mm_first(chosen.astype(jnp.bfloat16), incoming_rows[owner])
+        spot = lax.broadcasted_iota(jnp.int32, (owners * height, slot.shape[1]), 0)
+        spot = (spot + first * height).astype(jnp.float32)
+        chosen = (spot == slot).astype(jnp.float32).astype(jnp.bfloat16)
+        rows = jnp.concatenate([incoming_rows[first + k] for k in range(owners)], axis=0)
+        return mm_first(chosen, rows)
 
     known_load.wait()
 
@@ -620,12 +642,12 @@
         rows = known[begin : begin + size, :].astype(jnp.float32)
         return jnp.where(done_ref[0] > 0, rows, 0.0)
 
-    after_e[...] = known_rows(0, sources) + spread_rows(
-        source_slot, src_in, member
-    )
-    for order in (3, 1, 2):
+    near = member // 2 * 2
+    source_copy(peer(3), peer(3)).wait_recv()
+    after_e[...] = known_rows(0, sources) + spread_rows(source_slot, src_in, near, 2)
+    for order in (1, 2):
         source_copy(peer(order), peer(order)).wait_recv()
-        after_e[...] = after_e[...] + spread_rows(source_slot, src_in, peer(order))
+    after_e[...] = after_e[...] + spread_rows(source_slot, src_in, 2 - near, 2)
     embedded = after_e[...]
 
     def allowed(seq):
@@ -649,9 +671,7 @@
 
     for order in range(1, GEN):
         target_copy(peer(order), peer(order)).wait_recv()
-    inputs = known_rows(sources, targets)
-    for owner in range(GEN):
-        inputs = inputs + spread_rows(input_slot, tgt_in, owner)
+    inputs = known_rows(sources, targets) + spread_rows(input_slot, tgt_in, 0, GEN)
     entry = normed(inputs, gains_ref[3:4])
     weight_loads[3].wait()
     for block in range(3):
@@ -711,9 +731,9 @@
 
     for order in range(1, GEN):
         feature_copy(order).start()
-    wanted[...] = known_rows(sources + targets, targets)
-    for owner in range(GEN):
-        wanted[...] = wanted[...] + spread_rows(target_slot, tgt_in, owner)
+    wanted[...] = known_rows(sources + targets, targets) + spread_rows(
+        target_slot, tgt_in, 0, GEN
+    )
     same = lax.broadcasted_iota(jnp.int32, (targets, targets), 0) == lax.broadcasted_iota(
         jnp.int32, (targets, targets), 1
     )
@@ -799,8 +819,8 @@
         part = SEQ_DEV * FLAT
         begin = pl.multiple_of((layer * GEN + owner) * part, 8)
         return pltpu.make_async_remote_copy(
-            src_ref=pack.at[layer, target],
-            dst_ref=grads_in.at[pl.ds(begin, part)],
+            src_ref=pack.at[layer, target] if layer else pack_low.at[target],
+            dst_ref=grads_in.at[pl.ds(begin, part)] if layer else grads_low_in.at[owner],
             send_sem=grad_send.at[layer, target],
             recv_sem=grad_recv.at[layer, owner],
             device_id={"gen": target},
@@ -809,10 +829,15 @@
 
     def send_grads(layer):
         pack_grads(grad_down_ref, partial(grad_up_ref, layer), pack.at[layer])
+        if layer == 0:
+            pack_low[...] = pack[0].astype(jnp.bfloat16)
         for order in range(1, GEN):
             grad_copy(layer, member, peer(order)).start()
-        begin = pl.multiple_of((layer * GEN + member) * SEQ_DEV * FLAT, 8)
-        grads_in[pl.ds(begin, SEQ_DEV * FLAT), :] = pack[layer, member]
+        if layer == 0:
+            grads_low_in[member] = pack_low[member]
+        else:
+            begin = pl.multiple_of((layer * GEN + member) * SEQ_DEV * FLAT, 8)
+            grads_in[pl.ds(begin, SEQ_DEV * FLAT), :] = pack[layer, member]
 
     send_grads(1)
     for block in range(FF // D):
@@ -836,6 +861,10 @@
     for layer in range(LAYERS):
         for order in range(1, GEN):
             grad_copy(layer, peer(order), peer(order)).wait_recv()
+    for owner in range(GEN):
+        grads_in[pl.ds(owner * SEQ_DEV * FLAT, SEQ_DEV * FLAT), :] = grads_low_in[owner].astype(
+            jnp.float32
+        )
     pairs = TASKS * LAYERS
     received = jnp.concatenate(
         [grads_in[pl.ds(tile, pairs, stride=FLAT), :] for tile in range(FLAT)], axis=1
@@ -1111,6 +1140,8 @@
             pltpu.VMEM((LAYERS, SEQ_DEV, D, LOW), low),
             pltpu.VMEM((LAYERS, SEQ_DEV, LOW, D), low),
             pltpu.VMEM((LAYERS, GEN, SEQ_DEV * FLAT, 128), full),
+            pltpu.VMEM((GEN, SEQ_DEV * FLAT, 128), low),
+            pltpu.VMEM((GEN, SEQ_DEV * FLAT, 128), low),
             pltpu.VMEM((LAYERS * GEN * SEQ_DEV * FLAT, 128), full),
             pltpu.VMEM(hyper.shape, full),
             pltpu.VMEM((count, pairs * width // 128, 128), full),

time: 108 us -> 106 us (0.981)
  Pallas kernels: 106 us -> 104 us
    pallas_call x1, Pallas kernels: 99.4 us -> 97.9 us  [step(): pl.pallas_call(step_kernel, out_shape=(jax.ShapeDtypeStruct((pairs, FLAT...]
where the time goes in v5:
time: 106 us
  Pallas kernels  104 us (98%)
    pallas_call x1, Pallas kernels, step(): pl.pallas_call(step_kernel, out_shape=(jax.ShapeDtypeStruct((pairs, FLAT...  97.9 us
    pallas_call x1, Pallas kernels, update(): pl.pallas_call(update_kernel, out_shape=[one_value] * 3 + [jax.ShapeDtype...  6.44 us

profile of v5, /device:TPU:1, one launch (start us, length us, event | category | flops | bytes accessed | tf_op | source)
XLA Modules:
  0.0 106.2 jit_solution(3954651280709351295)
XLA Ops:
  0.6 0.0 copy-start
  0.7 0.0 copy-start.1
  0.7 0.0 copy-start.2
  0.7 0.0 copy-start.3
  0.7 0.0 copy-start.4
  0.7 0.0 copy-start.5
  0.7 0.0 copy-start.6
  0.7 0.0 copy-start.7
  0.7 0.0 copy-start.8
  0.7 97.9 %rows_forward_vocab_backward_sum.3 = (f32[16,6144]{1,0:T(8,128)}, f32[24,128]{1,0:T(8,128)}, f32[16,64]{1,0:T(8,128)}, s32[1]{0:T(128)}) custom-call(s32[1]{0:T(128)} %constant.127.clone.1.done_ref, s32[8]{0:T(128)} %task_ref.1, s32[8]{0:T(128)} %count_ref.1, s32[1,8]{1,0:T(1,128)} %bitcast.26, s32[8,256]{1,0:T(8,128)} %src_ref.1, s32[8,128]{1,0:T(8,128)} %tgt_ref.1, ...), custom_call_target="tpu_custom_call" | custom-call | tf_op jit(solution)/shard_map/rows_forward_vocab_backward_sum/pallas_call | solution.py:1105
  98.7 0.0 copy-done
  98.7 0.0 copy-done.1
  98.7 0.0 copy-done.2
  98.7 0.0 copy-done.3
  98.7 0.0 copy-done.4
  98.7 0.0 copy-done.5
  98.7 0.0 copy-done.6
  98.7 0.0 copy-done.7
  98.8 0.0 copy-done.8
  98.8 0.8 while.27
  99.5 6.4 %update.1 = (f32[1,1]{1,0:T(1,128)}, f32[1,1]{1,0:T(1,128)}, f32[1,1]{1,0:T(1,128)}, f32[10,64]{1,0:T(8,128)}, f32[10,64]{1,0:T(8,128)}, /*index=5*/f32[10,64]{1...) custom-call(f32[16,6144]{1,0:T(8,128)} %get-tuple-element.266.slots_, ...), custom_call_target="tpu_custom_call" | custom-call | tf_op jit(solution)/shard_map/update/pallas_call | solution.py:1321
Async XLA Ops:
  0.6 98.0 %copy-start = (f32[64,128]{1,0:T(8,128)S(1)}, f32[64,128]{1,0:T(8,128)}, u32[]{:S(2)}) copy-start(f32[64,128]{1,0:T(8,128)} %one.1) | copy-start | bytes 98308
  0.7 98.0 %copy-start.1 = (f32[128,64]{0,1:T(8,128)S(1)}, f32[128,64]{0,1:T(8,128)}, u32[]{:S(2)}) copy-start(f32[128,64]{0,1:T(8,128)} %param.44) | copy-start | bytes 98308
  0.7 98.0 %copy-start.2 = (s32[8,128]{1,0:T(8,128)S(1)}, s32[8,128]{1,0:T(8,128)}, u32[]{:S(2)}) copy-start(s32[8,128]{1,0:T(8,128)} %tgt_ref.1) | copy-start | bytes 12292
  0.7 98.0 %copy-start.3 = (s32[8,256]{1,0:T(8,128)S(1)}, s32[8,256]{1,0:T(8,128)}, u32[]{:S(2)}) copy-start(s32[8,256]{1,0:T(8,128)} %src_ref.1) | copy-start | bytes 24580
  0.7 98.0 %copy-start.4 = (f32[7,512]{1,0:T(8,128)S(1)}, f32[7,512]{1,0:T(8,128)}, u32[]{:S(2)}) copy-start(f32[7,512]{1,0:T(8,128)} %gains_ref.1) | copy-start | bytes 43012
  0.7 98.0 %copy-start.5 = (f32[10,64]{1,0:T(8,128)S(1)}, f32[10,64]{1,0:T(8,128)}, u32[]{:S(2)}) copy-start(f32[10,64]{1,0:T(8,128)} %embeds.1) | copy-start | bytes 7684
  0.7 98.0 %copy-start.6 = (s32[8]{0:T(128)S(1)}, s32[8]{0:T(128)}, u32[]{:S(2)}) copy-start(s32[8]{0:T(128)} %task_ref.1) | copy-start | bytes 100
  0.7 98.0 %copy-start.7 = (s32[8]{0:T(128)S(1)}, s32[8]{0:T(128)}, u32[]{:S(2)}) copy-start(s32[8]{0:T(128)} %count_ref.1) | copy-start | bytes 100
  0.7 98.0 %copy-start.8 = (s32[8]{0:T(128)S(1)}, s32[8]{0:T(128)}, u32[]{:S(2)}) copy-start(s32[8]{0:T(128)} %param.31) | copy-start | bytes 100

commit v6 on v5

--- a/solution.py
+++ b/solution.py
@@ -41,7 +41,7 @@
 GELU_A = math.sqrt(2.0 / math.pi)
 GELU_B = 0.044715
 VOCAB_TILE = 2048
-UPDATE_STEPS = 4
+UPDATE_STEPS = 8
 VMEM_LIMIT = 63 * 1024 * 1024
 MESH = pl.DeviceIdType.MESH
 

time: 106 us -> 107 us (level)
  no operation moved by 1% of the time
where the time goes in v6:
time: 107 us
  Pallas kernels  105 us (98%)
    pallas_call x1, Pallas kernels, step(): pl.pallas_call(step_kernel, out_shape=(jax.ShapeDtypeStruct((pairs, FLAT...  97.9 us
    pallas_call x1, Pallas kernels, update(): pl.pallas_call(update_kernel, out_shape=[one_value] * 3 + [jax.ShapeDtype...  7.04 us

profile of v6, /device:TPU:1, one launch (start us, length us, event | category | flops | bytes accessed | tf_op | source)
XLA Modules:
  0.0 106.8 jit_solution(4414604591134604714)
XLA Ops:
  0.6 0.0 copy-start
  0.7 0.0 copy-start.1
  0.7 0.0 copy-start.2
  0.7 0.0 copy-start.3
  0.7 0.0 copy-start.4
  0.7 0.0 copy-start.5
  0.7 0.0 copy-start.6
  0.7 0.0 copy-start.7
  0.7 0.0 copy-start.8
  0.7 97.9 %rows_forward_vocab_backward_sum.3 = (f32[16,6144]{1,0:T(8,128)}, f32[24,128]{1,0:T(8,128)}, f32[16,64]{1,0:T(8,128)}, s32[1]{0:T(128)}) custom-call(s32[1]{0:T(128)} %constant.127.clone.1.done_ref, s32[8]{0:T(128)} %task_ref.1, s32[8]{0:T(128)} %count_ref.1, s32[1,8]{1,0:T(1,128)} %bitcast.26, s32[8,256]{1,0:T(8,128)} %src_ref.1, s32[8,128]{1,0:T(8,128)} %tgt_ref.1, ...), custom_call_target="tpu_custom_call" | custom-call | tf_op jit(solution)/shard_map/rows_forward_vocab_backward_sum/pallas_call | solution.py:1105
  98.7 0.0 copy-done
  98.7 0.0 copy-done.1
  98.7 0.0 copy-done.2
  98.7 0.0 copy-done.3
  98.7 0.0 copy-done.4
  98.7 0.0 copy-done.5
  98.7 0.0 copy-done.6
  98.7 0.0 copy-done.7
  98.8 0.0 copy-done.8
  98.8 0.8 while.27
  99.5 7.0 %update.1 = (f32[1,1]{1,0:T(1,128)}, f32[1,1]{1,0:T(1,128)}, f32[1,1]{1,0:T(1,128)}, f32[10,64]{1,0:T(8,128)}, f32[10,64]{1,0:T(8,128)}, /*index=5*/f32[10,64]{1...) custom-call(f32[16,6144]{1,0:T(8,128)} %get-tuple-element.266.slots_, ...), custom_call_target="tpu_custom_call" | custom-call | tf_op jit(solution)/shard_map/update/pallas_call | solution.py:1321
Async XLA Ops:
  0.6 98.0 %copy-start = (f32[64,128]{1,0:T(8,128)S(1)}, f32[64,128]{1,0:T(8,128)}, u32[]{:S(2)}) copy-start(f32[64,128]{1,0:T(8,128)} %one.1) | copy-start | bytes 98308
  0.7 98.0 %copy-start.1 = (f32[128,64]{0,1:T(8,128)S(1)}, f32[128,64]{0,1:T(8,128)}, u32[]{:S(2)}) copy-start(f32[128,64]{0,1:T(8,128)} %param.44) | copy-start | bytes 98308
  0.7 98.0 %copy-start.2 = (s32[8,128]{1,0:T(8,128)S(1)}, s32[8,128]{1,0:T(8,128)}, u32[]{:S(2)}) copy-start(s32[8,128]{1,0:T(8,128)} %tgt_ref.1) | copy-start | bytes 12292
  0.7 98.0 %copy-start.3 = (s32[8,256]{1,0:T(8,128)S(1)}, s32[8,256]{1,0:T(8,128)}, u32[]{:S(2)}) copy-start(s32[8,256]{1,0:T(8,128)} %src_ref.1) | copy-start | bytes 24580
  0.7 98.0 %copy-start.4 = (f32[7,512]{1,0:T(8,128)S(1)}, f32[7,512]{1,0:T(8,128)}, u32[]{:S(2)}) copy-start(f32[7,512]{1,0:T(8,128)} %gains_ref.1) | copy-start | bytes 43012
  0.7 98.0 %copy-start.5 = (f32[10,64]{1,0:T(8,128)S(1)}, f32[10,64]{1,0:T(8,128)}, u32[]{:S(2)}) copy-start(f32[10,64]{1,0:T(8,128)} %embeds.1) | copy-start | bytes 7684
  0.7 98.0 %copy-start.6 = (s32[8]{0:T(128)S(1)}, s32[8]{0:T(128)}, u32[]{:S(2)}) copy-start(s32[8]{0:T(128)} %task_ref.1) | copy-start | bytes 100
  0.7 98.0 %copy-start.7 = (s32[8]{0:T(128)S(1)}, s32[8]{0:T(128)}, u32[]{:S(2)}) copy-start(s32[8]{0:T(128)} %count_ref.1) | copy-start | bytes 100
  0.7 98.0 %copy-start.8 = (s32[8]{0:T(128)S(1)}, s32[8]{0:T(128)}, u32[]{:S(2)}) copy-start(s32[8]{0:T(128)} %param.31) | copy-start | bytes 100
